TPU v7x, 32 devices: a whole 2x2x4 slice. The times are simulated.
32 devices in a mesh: groups: 2 (over y), leaf: 4 (over z), sample: 4 (over x, core).
Axes of the slice: x: 2, y: 2, z: 4, core: 2. Of those that a mesh axis runs over, the one named last changes fastest.
Arguments:
- points: bfloat16 [16384, 256], P(('groups', 'leaf', 'sample')), parts along dimension 0, may hold values from -40 to 40
- cotangent: bfloat16 [16384, 256], P(('groups', 'leaf', 'sample')), parts along dimension 0, may hold values from -6 to 6
- dest_pos: int32 [16384], P(('groups', 'leaf', 'sample')), parts along dimension 0, may hold values from 0 to 8191, as said below
- w_qkv: bfloat16 [256, 768], replicated, may hold values from -8 to 8
- w_out: bfloat16 [256, 256], replicated, may hold values from -0.375 to 0.375
- w_up: bfloat16 [256, 1024], replicated, may hold values from -0.375 to 0.375
- w_down: bfloat16 [1024, 256], replicated, may hold values from -0.1875 to 0.1875
- gain_attn: float32 [256], replicated, may hold values from 0.1 to 1.9
- gain_mlp: float32 [256], replicated, may hold values from 0.1 to 1.9
Outputs:
- grad_points: bfloat16 [16384, 256], P(('groups', 'leaf', 'sample')), parts along dimension 0
- grad_w_qkv: float32 [512, 768], P(('groups', 'leaf')), parts along dimension 0
- grad_w_out: float32 [512, 256], P(('groups', 'leaf')), parts along dimension 0
- grad_w_up: float32 [512, 1024], P(('groups', 'leaf')), parts along dimension 0
- grad_w_down: float32 [2048, 256], P(('groups', 'leaf')), parts along dimension 0
- grad_gain_attn: float32 [512], P(('groups', 'leaf')), parts along dimension 0
- grad_gain_mlp: float32 [512], P(('groups', 'leaf')), parts along dimension 0
There are 2 independent parts, one for each index of `groups`. A program takes and returns all parts, laid end to end along the dimension named above; an argument that names none is the same for every part. Nothing has to cross between parts.
Inputs may be any that keep to these rules, and one draw needn't show every extreme that they name: `dest_pos`: a permutation of the 8192 positions; of the 512 points of one device, at most 64 have positions in any one aligned block of 512 positions, and in every draw some device reaches exactly 64 for some block.
All inputs are finite; a program needn't handle non-finite values.
Results may differ from a plain program's by a relative error of at most 0.0059.
The roundings to bfloat16 on the way count: a program that leaves them out, or rounds other values in their place, can miss the bound.
Values may be sent and summed in bfloat16 or wider, within the bound.
No kernel may reach another device: no remote copies, remote signals or barrier semaphores. Data moves between devices by JAX's collectives and lax.ppermute only.
A program may use at most 64 MiB of HBM per device.

v0:
```python
import math

import jax
import jax.numpy as jnp
from jax import lax
from jax.sharding import PartitionSpec as P

HEADS = 8
BALL = 256
HEAD_DIM = 32


EPSILON = 1e-06
GELU_COEF = math.sqrt(2.0 / math.pi)


def rms_scale(matrix):
    return lax.rsqrt(jnp.mean(matrix * matrix, axis=1, keepdims=True) + EPSILON)


def gelu_parts(pre_act):
    tanh_val = jnp.tanh(GELU_COEF * (pre_act + 0.044715 * pre_act * pre_act * pre_act))
    value = 0.5 * pre_act * (1.0 + tanh_val)
    slope = 0.5 * (1.0 + tanh_val) + 0.5 * pre_act * (1.0 - tanh_val * tanh_val) * GELU_COEF * (
        1.0 + 3.0 * 0.044715 * pre_act * pre_act
    )
    return (value, slope)


def ball_split(ball_block):
    ball_groups = ball_block.shape[0] // BALL
    split_parts = ball_block.reshape(ball_groups, BALL, 3, HEADS, HEAD_DIM)
    return (split_parts[:, :, 0], split_parts[:, :, 1], split_parts[:, :, 2])


def softmax_probs(queries, key_rows):
    scores = jnp.einsum(
        "gqhd,gkhd->ghqk", queries, key_rows, preferred_element_type=jnp.float32
    ) * HEAD_DIM ** (-0.5)
    return jax.nn.softmax(scores, axis=-1)


def ball_forward(operands):
    queries, key_rows, values = ball_split(operands[0])
    probs_low = softmax_probs(queries, key_rows).astype(jnp.bfloat16)
    mixed = jnp.einsum("ghqk,gkhd->gqhd", probs_low, values, preferred_element_type=jnp.float32)
    return mixed.reshape(-1, HEADS * HEAD_DIM).astype(jnp.bfloat16)


def ball_backward(operands):
    ball_block, grad_block = operands
    queries, key_rows, values = ball_split(ball_block)
    attn_probs = softmax_probs(queries, key_rows)
    probs_low = attn_probs.astype(jnp.bfloat16)
    upstream = grad_block.reshape(queries.shape)
    grad_values = jnp.einsum(
        "ghqk,gqhd->gkhd", probs_low, upstream, preferred_element_type=jnp.float32
    )
    grad_probs = jnp.einsum("gqhd,gkhd->ghqk", upstream, values, preferred_element_type=jnp.float32)
    row_delta = jnp.sum(grad_probs * attn_probs, axis=-1, keepdims=True)
    grad_scores = (attn_probs * (grad_probs - row_delta)).astype(jnp.bfloat16)
    grad_queries = jnp.einsum(
        "ghqk,gkhd->gqhd", grad_scores, key_rows, preferred_element_type=jnp.float32
    ) * HEAD_DIM ** (-0.5)
    grad_keys = jnp.einsum(
        "ghqk,gqhd->gkhd", grad_scores, queries, preferred_element_type=jnp.float32
    ) * HEAD_DIM ** (-0.5)
    stacked = jnp.stack([grad_queries, grad_keys, grad_values], axis=2)
    return stacked.reshape(-1, 3 * HEADS * HEAD_DIM).astype(jnp.bfloat16)


def over_balls(function, operands):
    row_count = operands[0].shape[0]
    ball_count = row_count // BALL
    per_group = math.gcd(ball_count, max(1, 512 // BALL))
    shaped = tuple(
        (
            operand.reshape(ball_count // per_group, per_group * BALL, operand.shape[1])
            for operand in operands
        )
    )
    result = lax.map(function, shaped)
    return result.reshape(row_count, result.shape[2])


def layer_grads(rotated, rot_cot, w_qkv, w_out, w_up, w_down, gain_attn, gain_mlp):
    rotated_f = rotated.astype(jnp.float32)
    scale_one = rms_scale(rotated_f)
    norm_one = rotated_f * scale_one
    normed_one = (norm_one * gain_attn).astype(jnp.bfloat16)
    qkv_rows = jnp.dot(normed_one, w_qkv, preferred_element_type=jnp.float32).astype(jnp.bfloat16)
    attended = over_balls(ball_forward, (qkv_rows,))
    middle = rotated_f + jnp.dot(attended, w_out, preferred_element_type=jnp.float32)
    scale_two = rms_scale(middle)
    norm_two = middle * scale_two
    normed_two = (norm_two * gain_mlp).astype(jnp.bfloat16)
    pre_act = jnp.dot(normed_two, w_up, preferred_element_type=jnp.float32)
    act_value, act_slope = gelu_parts(pre_act)
    hidden = act_value.astype(jnp.bfloat16)
    grad_down = jnp.dot(hidden.T, rot_cot, preferred_element_type=jnp.float32)
    grad_pre = (jnp.dot(rot_cot, w_down.T, preferred_element_type=jnp.float32) * act_slope).astype(
        jnp.bfloat16
    )
    grad_up = jnp.dot(normed_two.T, grad_pre, preferred_element_type=jnp.float32)
    grad_normed_two = jnp.dot(grad_pre, w_up.T, preferred_element_type=jnp.float32)
    grad_gain_two = jnp.sum(grad_normed_two * norm_two, axis=0)
    inner_two = grad_normed_two * gain_mlp
    grad_middle = rot_cot.astype(jnp.float32) + scale_two * (
        inner_two - norm_two * jnp.mean(inner_two * norm_two, axis=1, keepdims=True)
    )
    grad_middle_low = grad_middle.astype(jnp.bfloat16)
    grad_out = jnp.dot(attended.T, grad_middle_low, preferred_element_type=jnp.float32)
    grad_attended = jnp.dot(grad_middle_low, w_out.T, preferred_element_type=jnp.float32).astype(
        jnp.bfloat16
    )
    grad_qkv_rows = over_balls(ball_backward, (qkv_rows, grad_attended))
    grad_qkv = jnp.dot(normed_one.T, grad_qkv_rows, preferred_element_type=jnp.float32)
    grad_normed_one = jnp.dot(grad_qkv_rows, w_qkv.T, preferred_element_type=jnp.float32)
    grad_gain_one = jnp.sum(grad_normed_one * norm_one, axis=0)
    inner_one = grad_normed_one * gain_attn
    grad_rot = grad_middle + scale_one * (
        inner_one - norm_one * jnp.mean(inner_one * norm_one, axis=1, keepdims=True)
    )
    return (grad_rot, grad_qkv, grad_out, grad_up, grad_down, grad_gain_one, grad_gain_two)


def local(points, cotangent, dest_pos, w_qkv, w_out, w_up, w_down, gain_attn, gain_mlp):
    row_count, feat_width = points.shape
    peer_count = lax.axis_size(("leaf", "sample"))
    capacity = 2 * row_count // peer_count
    owner_dev = dest_pos // row_count
    target_row = dest_pos % row_count
    one_hot = (owner_dev[:, None] == jnp.arange(peer_count, dtype=jnp.int32)[None, :]).astype(
        jnp.int32
    )
    rank_within = jnp.sum(jnp.cumsum(one_hot, axis=0) * one_hot, axis=1) - 1
    slot_index = owner_dev * capacity + rank_within
    send_points = (
        jnp.zeros((peer_count * capacity, feat_width), jnp.bfloat16).at[slot_index].set(points)
    )
    send_cot = (
        jnp.zeros((peer_count * capacity, feat_width), jnp.bfloat16).at[slot_index].set(cotangent)
    )
    send_target = (
        jnp.full((peer_count * capacity,), row_count, jnp.int32).at[slot_index].set(target_row)
    )
    recv_points, recv_cot, recv_target = (
        lax.all_to_all(
            send_points.reshape(peer_count, capacity, feat_width),
            ("leaf", "sample"),
            split_axis=0,
            concat_axis=0,
            tiled=True,
        ),
        lax.all_to_all(
            send_cot.reshape(peer_count, capacity, feat_width),
            ("leaf", "sample"),
            split_axis=0,
            concat_axis=0,
            tiled=True,
        ),
        lax.all_to_all(
            send_target.reshape(peer_count, capacity),
            ("leaf", "sample"),
            split_axis=0,
            concat_axis=0,
            tiled=True,
        ),
    )
    flat_target = recv_target.reshape(-1)
    rotated = (
        jnp.zeros((row_count, feat_width), jnp.bfloat16)
        .at[flat_target]
        .set(recv_points.reshape(-1, feat_width), mode="drop")
    )
    rot_cot = (
        jnp.zeros((row_count, feat_width), jnp.bfloat16)
        .at[flat_target]
        .set(recv_cot.reshape(-1, feat_width), mode="drop")
    )
    grad_rot, grad_qkv, grad_out, grad_up, grad_down, grad_gain_one, grad_gain_two = layer_grads(
        rotated, rot_cot, w_qkv, w_out, w_up, w_down, gain_attn, gain_mlp
    )
    back_rows = grad_rot.astype(jnp.bfloat16)[jnp.minimum(flat_target, row_count - 1)]
    returned = lax.all_to_all(
        back_rows.reshape(peer_count, capacity, feat_width),
        ("leaf", "sample"),
        split_axis=0,
        concat_axis=0,
        tiled=True,
    )
    grad_points = returned.reshape(-1, feat_width)[slot_index]
    inv_root = 1.0 / math.sqrt(row_count * peer_count)
    shares = (
        lax.psum_scatter(grad_qkv, "leaf", scatter_dimension=0, tiled=True),
        lax.psum_scatter(grad_out, "leaf", scatter_dimension=0, tiled=True),
        lax.psum_scatter(grad_up, "leaf", scatter_dimension=0, tiled=True),
        lax.psum_scatter(grad_down, "leaf", scatter_dimension=0, tiled=True),
        lax.psum_scatter(grad_gain_one, "leaf", scatter_dimension=0, tiled=True),
        lax.psum_scatter(grad_gain_two, "leaf", scatter_dimension=0, tiled=True),
    )
    totals = lax.psum((shares[0], shares[1], shares[2], shares[3], shares[4], shares[5]), "sample")
    return (
        grad_points,
        totals[0] * inv_root,
        totals[1] * inv_root,
        totals[2] * inv_root,
        totals[3] * inv_root,
        totals[4] * inv_root,
        totals[5] * inv_root,
    )


def solution(mesh):
    in_specs = (
        P(("groups", "leaf", "sample"), None),
        P(("groups", "leaf", "sample"), None),
        P(("groups", "leaf", "sample")),
        P(),
        P(),
        P(),
        P(),
        P(),
        P(),
    )
    out_specs = (
        P(("groups", "leaf", "sample"), None),
        P(("groups", "leaf"), None),
        P(("groups", "leaf"), None),
        P(("groups", "leaf"), None),
        P(("groups", "leaf"), None),
        P(("groups", "leaf")),
        P(("groups", "leaf")),
    )
    return jax.shard_map(local, mesh=mesh, in_specs=in_specs, out_specs=out_specs, check_vma=False)
```

profile of v0, /device:TPU:0, one launch (start us, length us, event | category | flops | bytes accessed | tf_op | source)
XLA Modules:
  0.0 249.3 jit_solution(2096667558495499400)
XLA Ops:
  12.6 7.4 %all-to-all-start = ((s32[16,1,64]{2,1,0:T(1,128)}), s32[16,1,64]{2,1,0:T(1,128)S(1)}, u32[]{:S(2)}, u32[]{:S(2)}) async-start(s32[16,1,64]{2,1,0:T(1,128)} %all_to_all.15), calls=%async_computation | async-start | bytes 16384 | tf_op jit(solution)/shard_map/all_to_all | solution.py:162
  20.0 3.5 %scatter_custom_fusion.3 = bf16[1024,256]{1,0:T(8,128)(2,1)} fusion(s32[512]{0:T(512)S(1)} %compare_select_fusion.2, bf16[512,256]{1,0:T(8,128)(2,1)} %param.9, bf16[]{:T(256)} %constant.52.clone.1), kind=kCustom, calls=%fused_computation.65 | custom fusion | bytes 524800 | tf_op jit(solution)/shard_map/scatter | solution.py:139
  23.5 2.8 %all-to-all-done = s32[16,1,64]{2,1,0:T(1,128)S(1)} async-done(((s32[16,1,64]{2,1,0:T(1,128)}), s32[16,1,64]{2,1,0:T(1,128)S(1)}, u32[]{:S(2)}, u32[]{:S(2)}) %all-to-all-start) | async-done | bytes 4128 | tf_op jit(solution)/shard_map/all_to_all | solution.py:162
  26.3 3.7 %all-to-all-start.2 = ((bf16[16,64,256]{2,1,0:T(8,128)(2,1)}), bf16[16,64,256]{2,1,0:T(8,128)(2,1)S(1)}, u32[]{:S(2)}, u32[]{:S(2)}) async-start(bf16[16,64,256]{2,1,0:T(8,128)(2,1)} %bitcast.5), calls=%async_computation.2 | async-start | bytes 1048576 | tf_op jit(solution)/shard_map/all_to_all | solution.py:148
  30.0 3.5 %scatter_custom_fusion.1 = bf16[1024,256]{1,0:T(8,128)(2,1)} fusion(s32[512]{0:T(512)S(1)} %compare_select_fusion.2, bf16[512,256]{1,0:T(8,128)(2,1)} %param.10, bf16[]{:T(256)} %constant.52.clone.1), kind=kCustom, calls=%fused_computation.67 | custom fusion | bytes 524800 | tf_op jit(solution)/shard_map/scatter | solution.py:142
  33.5 10.9 %all-to-all-done.2 = bf16[16,64,256]{2,1,0:T(8,128)(2,1)S(1)} async-done(((bf16[16,64,256]{2,1,0:T(8,128)(2,1)}), bf16[16,64,256]{2,1,0:T(8,128)(2,1)S(1)}, u32[]{:S(2)}, u32[]{:S(2)}) %all-to-all-start.2) | async-done | bytes 524320 | tf_op jit(solution)/shard_map/all_to_all | solution.py:148
  44.4 4.0 %all-to-all-start.1 = ((bf16[16,64,256]{2,1,0:T(8,128)(2,1)}), bf16[16,64,256]{2,1,0:T(8,128)(2,1)S(1)}, u32[]{:S(2)}, u32[]{:S(2)}) async-start(bf16[16,64,256]{2,1,0:T(8,128)(2,1)} %bitcast.3), calls=%async_computation.1 | async-start | bytes 1048576 | tf_op jit(solution)/shard_map/all_to_all | solution.py:155
  49.8 5.0 %scatter_custom_fusion.4 = bf16[512,256]{1,0:T(8,128)(2,1)S(1)} fusion(s32[1024]{0:T(1024)S(1)} %bitcast.116, bf16[1024,256]{1,0:T(8,128)(2,1)S(1)} %bitcast.113, bf16[]{:T(256)} %constant.52.clone.1), kind=kCustom, calls=%fused_computation.78 | custom fusion | bytes 262146 | tf_op jit(solution)/shard_map/scatter | solution.py:174
  55.0 7.9 %all-to-all-done.1 = bf16[16,64,256]{2,1,0:T(8,128)(2,1)S(1)} async-done(((bf16[16,64,256]{2,1,0:T(8,128)(2,1)}), bf16[16,64,256]{2,1,0:T(8,128)(2,1)S(1)}, u32[]{:S(2)}, u32[]{:S(2)}) %all-to-all-start.1) | async-done | bytes 524320 | tf_op jit(solution)/shard_map/all_to_all | solution.py:155
  62.9 5.1 %scatter_custom_fusion.2 = bf16[512,256]{1,0:T(8,128)(2,1)S(1)} fusion(s32[1024]{0:T(1024)S(1)} %bitcast.117, bf16[1024,256]{1,0:T(8,128)(2,1)S(1)} %bitcast.112, bf16[]{:T(256)} %constant.52.clone.1), kind=kCustom, calls=%fused_computation.80 | custom fusion | bytes 262146 | tf_op jit(solution)/shard_map/scatter | solution.py:179
  70.1 3.5 %fusion.67 = (f32[2,8,256]{2,1,0:T(8,128)S(1)}, f32[2,8,256,256]{2,3,1,0:T(8,128)}) fusion(bf16[2,256,1,8,32]{1,0,4,3,2:T(2,128)(2,1)S(1)} %get-tuple-element.41, bf16[2,256,1,8,32]{1,0,4,3,2:T(2,128)(2,1)S(1)} %get-tuple-element.40), kind=kOutput, calls=%fused_computation.122 | convolution fusion | flops 70254848 | bytes 4734976 | tf_op jit(solution)/shard_map/while/body/eval_jaxpr/sub | solution.py:40
  74.2 2.6 %fusion.16 = bf16[2,256,8,32]{1,3,2,0:T(8,128)(2,1)S(1)} fusion(bf16[2,256,1,8,32]{1,0,4,3,2:T(2,128)(2,1)S(1)} %get-tuple-element.42, f32[2,8,256,256]{2,3,1,0:T(8,128)} %get-tuple-element.48, f32[2,8,256]{2,1,0:T(8,128)S(1)} %get-tuple-element.47), kind=kOutput, calls=%fused_computation.36 | convolution fusion | flops 69337088 | bytes 4734976 | tf_op jit(solution)/shard_map/while/body/eval_jaxpr/ghqk,gkhd->gqhd/dot_general | solution.py:46
  84.1 3.8 %fusion.17 = bf16[2,256,1,8,32]{1,4,3,0,2:T(8,128)(2,1)} fusion(bf16[2,256,8,32]{1,0,3,2:T(2,128)(2,1)S(1)} %reshape.169, f32[2,8,256,256]{2,3,1,0:T(8,128)} %get-tuple-element.48, f32[2,8,256]{2,1,0:T(8,128)} %copy-done.15), kind=kOutput, calls=%fused_computation.37 | convolution fusion | flops 69337088 | bytes 4734976 | tf_op jit(solution)/shard_map/while/body/eval_jaxpr/ghqk,gqhd->gkhd/dot_general | solution.py:56
  87.9 2.8 %multiply_reduce_fusion = (f32[2,8,256]{2,1,0:T(8,128)S(1)}, f32[2,8,256,256]{2,3,1,0:T(8,128)}) fusion(f32[2,8,256,256]{2,3,1,0:T(8,128)S(1)} %copy-done.1, f32[2,8,256]{2,1,0:T(8,128)S(1)} %copy-done.16, bf16[2,256,1,8,32]{1,0,4,3,2:T(2,128)(2,1)S(1)} %copy-done.12, bf16[2,256,8,32]{1,0,3,2:T(2,128)(2,1)S(1)} %reshape.169), kind=kOutput, calls=%fused_computation.9 | convolution fusion | flops 70250496 | bytes 8945664 | tf_op jit(solution)/shard_map/while/body/eval_jaxpr/gqhd,gkhd->ghqk/dot_general | solution.py:59
  90.8 4.3 %multiply_convert_fusion = bf16[2,8,256,256]{2,3,1,0:T(8,128)(2,1)S(1)} fusion(f32[2,8,256,256]{2,3,1,0:T(8,128)} %get-tuple-element.53, f32[2,8,256]{2,1,0:T(8,128)S(1)} %get-tuple-element.52, f32[2,8,256,256]{2,3,1,0:T(8,128)} %get-tuple-element.48, f32[2,8,256]{2,1,0:T(8,128)S(1)} %copy-done.16), kind=kLoop, calls=%fused_computation.8 | loop fusion | flops 4194304 | bytes 10518528 | tf_op jit(solution)/shard_map/while/body/eval_jaxpr/convert_element_type | solution.py:61
  100.1 3.4 %fusion.20 = f32[1024,256]{1,0:T(8,128)} fusion(bf16[512,256]{1,0:T(8,128)(2,1)S(1)} %scatter_custom_fusion.2, f32[512,1024]{1,0:T(8,128)} %copy-done.3), kind=kOutput, calls=%fused_computation.40 | convolution fusion | flops 273154048 | bytes 3407872 | tf_op jit(solution)/shard_map/dot_general | solution.py:100
  107.2 4.9 %gather_fusion = bf16[1024,256]{1,0:T(8,128)(2,1)} fusion(bf16[512,256]{1,0:T(8,128)(2,1)S(1)} %copy.69, s32[1024]{0:T(1024)S(1)} %broadcast_clamp_fusion), kind=kCustom, calls=%fused_computation | custom fusion | bytes 1052672 | tf_op jit(solution)/shard_map/gather | solution.py:184
  112.1 4.1 %all-to-all-start.3 = ((bf16[16,64,256]{2,1,0:T(8,128)(2,1)}), bf16[16,64,256]{2,1,0:T(8,128)(2,1)S(1)}, u32[]{:S(2)}, u32[]{:S(2)}) async-start(bf16[16,64,256]{2,1,0:T(8,128)(2,1)} %bitcast.18), calls=%async_computation.3 | async-start | bytes 1048576 | tf_op jit(solution)/shard_map/all_to_all | solution.py:185
  116.3 25.9 %reduce-scatter.5.cloned.1.call-done = f32[64,768]{1,0:T(8,128)} async-done(((f32[256,768]{1,0:T(8,128)}), f32[64,768]{1,0:T(8,128)}) %reduce-scatter.5.cloned.1.call-update) | async-done | bytes 196624 | tf_op jit(solution)/shard_map/reduce_scatter | solution.py:195
  142.2 29.9 %reduce-scatter.11.cloned.1.call-done = f32[256,256]{1,0:T(8,128)} async-done(((f32[1024,256]{1,0:T(8,128)}), f32[256,256]{1,0:T(8,128)}) %reduce-scatter.11.cloned.1.call-update) | async-done | bytes 262160 | tf_op jit(solution)/shard_map/reduce_scatter | solution.py:198
  172.1 28.0 %reduce-scatter.9.cloned.1.call-done = f32[64,1024]{1,0:T(8,128)} async-done(((f32[256,1024]{1,0:T(8,128)}), f32[64,1024]{1,0:T(8,128)}) %reduce-scatter.9.cloned.1.call-update) | async-done | bytes 262160 | tf_op jit(solution)/shard_map/reduce_scatter | solution.py:197
  201.3 9.4 %all-reduce.4 = (f32[256]{0:T(256)S(1)}, f32[256]{0:T(256)S(1)}) all-reduce(f32[256]{0:T(256)S(1)} %get-tuple-element.30, f32[256]{0:T(256)S(1)} %copy-done.21), channel_id=6, replica_groups=mesh['groups'=2,'leaf'=4,'sample'=4] {'leaf'}, use_global_device_ids=true, to_apply=%region_24.25.clone | all-reduce | flops 512 | bytes 4096
  210.9 6.0 %all-reduce.2 = (f32[64]{0:T(128)S(1)}, f32[64]{0:T(128)S(1)}) all-reduce(f32[64]{0:T(128)S(1)} %dynamic-slice.3, f32[64]{0:T(128)S(1)} %dynamic-slice.5), channel_id=1, replica_groups=mesh['groups'=2,'leaf'=4,'sample'=4] {'sample'}, use_global_device_ids=true, to_apply=%region_25.26 | all-reduce | flops 128 | bytes 1024 | tf_op jit(solution)/shard_map/psum | solution.py:202
  220.0 16.4 %all-reduce.7.cloned.1.call-done = (f32[64,768]{1,0:T(8,128)}, f32[64,256]{1,0:T(8,128)}, f32[64,1024]{1,0:T(8,128)}, f32[256,256]{1,0:T(8,128)}) async-done(((f32[64,768]{1,0:T(8,128)}, f32[64,256]{1,0:T(8,128)}, f32[64,1024]{1,0:T(8,128)}, f32[256,256]{1,0:T(8,128)}), (f32[64,768]{1,0:T(8,128)}, f32[64,256]{1,0:T(8,128)}, f32[64,1024]{1,0:T(8,128)}, f32[256,256]{1,0:T(8,128)})) %all-reduce.7.cloned.1.call-update) | async-done | bytes 786448 | tf_op jit(solution)/shard_map/psum | solution.py:202
  (117 shorter events, 35.5 us)
Async XLA Ops:
  7.2 70.3 %copy-start = (bf16[256,1024]{1,0:T(8,128)(2,1)S(1)}, bf16[256,1024]{1,0:T(8,128)(2,1)}, u32[]{:S(2)}) copy-start(bf16[256,1024]{1,0:T(8,128)(2,1)} %param.14) | copy-start | bytes 1572868
  9.5 39.1 %copy-start.19 = (s32[512]{0:T(512)}, s32[512]{0:T(512)S(1)}, u32[]{:S(2)}) copy-start(s32[512]{0:T(512)S(1)} %compare_select_fusion.2) | copy-start | bytes 6148
  12.6 13.7 %all-to-all-start = ((s32[16,1,64]{2,1,0:T(1,128)}), s32[16,1,64]{2,1,0:T(1,128)S(1)}, u32[]{:S(2)}, u32[]{:S(2)}) async-start(s32[16,1,64]{2,1,0:T(1,128)} %all_to_all.15), calls=%async_computation | async-start | bytes 16384 | tf_op jit(solution)/shard_map/all_to_all | solution.py:162
  26.3 41.9 %copy-start.9 = (bf16[256,768]{1,0:T(8,128)(2,1)S(1)}, bf16[256,768]{1,0:T(8,128)(2,1)}, u32[]{:S(2)}) copy-start(bf16[256,768]{1,0:T(8,128)(2,1)} %param.12) | copy-start | bytes 1179652
  26.3 41.9 %copy-start.17 = (f32[256]{0:T(256)S(1)}, f32[256]{0:T(256)}, u32[]{:S(2)}) copy-start(f32[256]{0:T(256)} %param.16) | copy-start | bytes 3076
  26.3 18.1 %all-to-all-start.2 = ((bf16[16,64,256]{2,1,0:T(8,128)(2,1)}), bf16[16,64,256]{2,1,0:T(8,128)(2,1)S(1)}, u32[]{:S(2)}, u32[]{:S(2)}) async-start(bf16[16,64,256]{2,1,0:T(8,128)(2,1)} %bitcast.5), calls=%async_computation.2 | async-start | bytes 1048576 | tf_op jit(solution)/shard_map/all_to_all | solution.py:148
  44.4 18.5 %all-to-all-start.1 = ((bf16[16,64,256]{2,1,0:T(8,128)(2,1)}), bf16[16,64,256]{2,1,0:T(8,128)(2,1)S(1)}, u32[]{:S(2)}, u32[]{:S(2)}) async-start(bf16[16,64,256]{2,1,0:T(8,128)(2,1)} %bitcast.3), calls=%async_computation.1 | async-start | bytes 1048576 | tf_op jit(solution)/shard_map/all_to_all | solution.py:155
  48.5 67.8 %reduce-scatter.7.cloned.1.call-start = ((), (), s32[]{:S(2)}) async-start(), calls=%async_computation.9 | async-start | bytes 327680 | tf_op jit(solution)/shard_map/reduce_scatter | solution.py:196
  70.0 3.5 %copy-start.4 = (bf16[2,256,1,8,32]{1,0,4,3,2:T(2,128)(2,1)}, bf16[2,256,1,8,32]{1,0,4,3,2:T(2,128)(2,1)S(1)}, u32[]{:S(2)}) copy-start(bf16[2,256,1,8,32]{1,0,4,3,2:T(2,128)(2,1)S(1)} %get-tuple-element.40) | copy-start | bytes 786436
  70.0 3.5 %copy-start.6 = (bf16[2,256,1,8,32]{1,0,4,3,2:T(2,128)(2,1)}, bf16[2,256,1,8,32]{1,0,4,3,2:T(2,128)(2,1)S(1)}, u32[]{:S(2)}) copy-start(bf16[2,256,1,8,32]{1,0,4,3,2:T(2,128)(2,1)S(1)} %get-tuple-element.41) | copy-start | bytes 786436
  70.1 3.5 %copy-start.11 = (bf16[2,256,1,8,32]{1,0,4,3,2:T(2,128)(2,1)}, bf16[2,256,1,8,32]{1,0,4,3,2:T(2,128)(2,1)S(1)}, u32[]{:S(2)}) copy-start(bf16[2,256,1,8,32]{1,0,4,3,2:T(2,128)(2,1)S(1)} %get-tuple-element.42) | copy-start | bytes 786436
  74.2 3.0 %copy-start.8 = (bf16[256,256]{1,0:T(8,128)(2,1)S(1)}, bf16[256,256]{1,0:T(8,128)(2,1)}, u32[]{:S(2)}) copy-start(bf16[256,256]{1,0:T(8,128)(2,1)} %param.13) | copy-start | bytes 393220
  84.1 3.8 %copy-start.1 = (f32[2,8,256,256]{2,3,1,0:T(8,128)S(1)}, f32[2,8,256,256]{2,3,1,0:T(8,128)}, u32[]{:S(2)}) copy-start(f32[2,8,256,256]{2,3,1,0:T(8,128)} %get-tuple-element.48) | copy-start | bytes 12582916
  84.1 3.8 %copy-start.12 = (bf16[2,256,1,8,32]{1,0,4,3,2:T(2,128)(2,1)S(1)}, bf16[2,256,1,8,32]{1,0,4,3,2:T(2,128)(2,1)}, u32[]{:S(2)}) copy-start(bf16[2,256,1,8,32]{1,0,4,3,2:T(2,128)(2,1)} %copy-done.11) | copy-start | bytes 786436
  84.1 3.8 %copy-start.16 = (f32[2,8,256]{2,1,0:T(8,128)S(1)}, f32[2,8,256]{2,1,0:T(8,128)}, u32[]{:S(2)}) copy-start(f32[2,8,256]{2,1,0:T(8,128)} %copy-done.15) | copy-start | bytes 49156
  90.7 51.5 %reduce-scatter.5.cloned.1.call-start = ((), (), s32[]{:S(2)}) async-start(), calls=%async_computation.8 | async-start | bytes 983040 | tf_op jit(solution)/shard_map/reduce_scatter | solution.py:195
  90.8 4.3 %copy-start.7 = (bf16[2,256,1,8,32]{1,0,4,3,2:T(2,128)(2,1)S(1)}, bf16[2,256,1,8,32]{1,0,4,3,2:T(2,128)(2,1)}, u32[]{:S(2)}) copy-start(bf16[2,256,1,8,32]{1,0,4,3,2:T(2,128)(2,1)} %copy-done.6) | copy-start | bytes 786436
  99.8 72.2 %reduce-scatter.11.cloned.1.call-start = ((), (), s32[]{:S(2)}) async-start(), calls=%async_computation.11 | async-start | bytes 1310720 | tf_op jit(solution)/shard_map/reduce_scatter | solution.py:198
  103.6 96.4 %reduce-scatter.9.cloned.1.call-start = ((), (), s32[]{:S(2)}) async-start(), calls=%async_computation.10 | async-start | bytes 1310720 | tf_op jit(solution)/shard_map/reduce_scatter | solution.py:197
  107.1 92.9 %copy-start.23 = (u32[32]{0:T(128)S(1)}, u32[32]{0:T(128)}, u32[]{:S(2)}) copy-start(u32[32]{0:T(128)} %constant.110) | copy-start | bytes 388
  107.1 94.2 %copy-start.20 = (s32[512]{0:T(512)S(1)}, s32[512]{0:T(512)}, u32[]{:S(2)}) copy-start(s32[512]{0:T(512)} %copy-done.19) | copy-start | bytes 6148
  107.1 94.2 %copy-start.21 = (f32[256]{0:T(256)S(1)}, f32[256]{0:T(256)}, u32[]{:S(2)}) copy-start(f32[256]{0:T(256)} %get-tuple-element.28) | copy-start | bytes 3076
  112.1 105.3 %all-to-all-start.3 = ((bf16[16,64,256]{2,1,0:T(8,128)(2,1)}), bf16[16,64,256]{2,1,0:T(8,128)(2,1)S(1)}, u32[]{:S(2)}, u32[]{:S(2)}) async-start(bf16[16,64,256]{2,1,0:T(8,128)(2,1)} %bitcast.18), calls=%async_computation.3 | async-start | bytes 1048576 | tf_op jit(solution)/shard_map/all_to_all | solution.py:185
  116.2 120.2 %all-reduce.7.cloned.1.call-start = ((), (), s32[]{:S(2)}) async-start(), calls=%async_computation.12 | async-start | bytes 1572864 | tf_op jit(solution)/shard_map/psum | solution.py:202
  (9 other events, 10.6 us)
Sparse Core Ops, SparseCore 0:
  90.8 19.1 reduce-scatter.6
  112.4 29.7 reduce-scatter.4
  144.6 27.4 reduce-scatter.10
  174.2 25.7 reduce-scatter.8
  202.6 33.6 all-reduce.6
where the time goes:
time: 250 us; the launch traced here: 249 us
  waiting for transfers between devices  122 us (49%)
  local copies, waits for them, and re-layouts  36.2 us (14%)
  matrix products  26.9 us (11%)
  starting transfers between devices  19.6 us (8%)
  blocking collectives  15.4 us (6%)
  between operations  15 us (6%)
  other arithmetic  14.5 us (6%)
    reduce_scatter x1, waiting for transfers between devices, local(): lax.psum_scatter(grad_down, 'leaf', scatter_dimension=0, tiled=True)  29.9 us
    reduce_scatter x1, waiting for transfers between devices, local(): lax.psum_scatter(grad_up, 'leaf', scatter_dimension=0, tiled=True)  28 us
    reduce_scatter x1, waiting for transfers between devices, local(): lax.psum_scatter(grad_qkv, 'leaf', scatter_dimension=0, tiled=True)  25.9 us
    psum x1, waiting for transfers between devices, local(): lax.psum((shares[0], shares[1], shares[2], shares[3], shares[4], shares[5...  16.4 us
    all_to_all x1, waiting for transfers between devices, local(): lax.all_to_all(send_points.reshape(peer_count, capacity, feat_width), ('l...  10.9 us
    unnamed x1, blocking collectives  9.39 us
    all_to_all x1, waiting for transfers between devices, local(): lax.all_to_all(send_cot.reshape(peer_count, capacity, feat_width), ('leaf...  7.91 us
    all_to_all x1, starting transfers between devices, local(): lax.all_to_all(send_target.reshape(peer_count, capacity), ('leaf', 'sampl...  7.36 us
  transfers between devices with their start and end apart: 9, of which 7 were waited for; matrix products, arithmetic and copies ran while one was open for 15% of the time, Pallas kernels for 0%

commit v1 on v0

v1 whole, which is shorter than its diff:
```python
import functools
import math

import jax
import jax.numpy as jnp
from jax import lax
from jax.experimental import pallas as pl
from jax.experimental.pallas import tpu as pltpu
from jax.sharding import PartitionSpec as P

HEADS = 8
BALL = 256
HEAD_DIM = 32
GROUP = 128
META = 16

EPSILON = 1e-06
GELU_COEF = math.sqrt(2.0 / math.pi)
ATT_SCALE = HEAD_DIM ** (-0.5)
BF16 = jnp.bfloat16
F32 = jnp.float32


def mm(a, b):
    return lax.dot_general(a, b, (((1,), (0,)), ((), ())), preferred_element_type=F32)


def mm_nt(a, b):
    return lax.dot_general(a, b, (((1,), (1,)), ((), ())), preferred_element_type=F32)


def mm_tn(a, b):
    return lax.dot_general(a, b, (((0,), (0,)), ((), ())), preferred_element_type=F32)


def iota(shape, dim):
    return lax.broadcasted_iota(jnp.int32, shape, dim)


def one_hot(positions, shape, dim):
    return jnp.where(iota(shape, dim) == positions, 1.0, 0.0).astype(BF16)


def column_of(row):
    return jnp.broadcast_to(row, (128, row.shape[1])).T


def lane_tile(column, width):
    return jnp.concatenate([column] * (width // 128), axis=1)


class Arriving:
    def __init__(self, ref, copies):
        self.ref, self.copies, self.shape = ref, copies, ref.shape

    def __getitem__(self, where):
        for copy in self.copies:
            copy.wait()
        self.copies = []
        return self.ref[where]


class Leaving:
    def __init__(self, ref, out_ref, sems):
        self.ref, self.out_ref, self.sems, self.shape, self.dtype = ref, out_ref, sems, ref.shape, ref.dtype
        self.copies, self.sent = [], 0

    def __getitem__(self, where):
        return self.ref[where]

    def __setitem__(self, where, value):
        self.ref[where] = value

    def send(self, upto=None):
        upto = self.shape[0] if upto is None else upto
        if upto > self.sent:
            part = pl.ds(self.sent, upto - self.sent)
            copy = pltpu.make_async_copy(self.ref.at[part], self.out_ref.at[part], self.sems.at[len(self.copies)])
            copy.start()
            self.copies.append(copy)
            self.sent = upto


def send(ref, upto=None):
    if isinstance(ref, Leaving):
        ref.send(upto)


def pack_points_kernel(peers, cap, direct, dest_ref, points_ref, slot_ref, *out_refs):
    rows = points_ref.shape[0]
    slots = peers * cap
    dest = dest_ref[...]
    shift = rows.bit_length() - 1
    owner = lax.shift_right_logical(dest, shift)
    target = jnp.bitwise_and(dest, rows - 1)
    owned = jnp.where(iota((peers, rows), 0) == owner, 1.0, 0.0)
    upto = jnp.where(iota((rows, rows), 0) <= iota((rows, rows), 1), 1.0, 0.0).astype(BF16)
    counts = mm(owned.astype(BF16), upto)
    rank = (jnp.sum(counts * owned, axis=0, keepdims=True) - 1.0).astype(jnp.int32)
    slot = owner * cap + rank
    slot_ref[...] = slot
    packed = mm(one_hot(slot, (slots, rows), 0), points_ref[...]).astype(BF16)
    within = one_hot(rank, (cap, rows), 0)
    within = jnp.concatenate([within] * (128 // cap), axis=0)
    high = (lax.shift_right_logical(target, 4) + 1).astype(F32)
    low = jnp.bitwise_and(target, 15).astype(F32)
    high_rows = mm_nt((owned * high).astype(BF16), within)
    low_rows = mm_nt((owned * low).astype(BF16), within)
    if direct:
        (msg_ref,) = out_refs
        msg_ref[:, :cap, :] = packed[:, :128].reshape(peers, cap, 128)
        msg_ref[:, cap : 2 * cap, :] = packed[:, 128:].reshape(peers, cap, 128)
        first = iota((META, 128), 0) == 0
        for peer in range(peers):
            block = jnp.where(first, high_rows[peer : peer + 1], low_rows[peer : peer + 1])
            msg_ref[peer, 2 * cap :, :] = block.astype(BF16)
    else:
        packed_ref, high_ref, low_ref = out_refs
        packed_ref[...] = packed
        high_ref[...] = high_rows
        low_ref[...] = low_rows


def partner(step):
    return (lax.axis_index("leaf") * lax.axis_size("sample") + lax.axis_index("sample")) ^ step


def pack_cot_kernel(slot_ref, cot_ref, *refs):
    rows = cot_ref.shape[0]
    if len(refs) == 1:
        (packed_ref,) = refs
        packed_ref[...] = mm(one_hot(slot_ref[...], (packed_ref.shape[0], rows), 0), cot_ref[...]).astype(BF16)
        return
    *block_refs, packed_ref = refs
    peers, cap, width = packed_ref.shape
    packed = mm(one_hot(slot_ref[...], (peers * cap, rows), 0), cot_ref[...]).astype(BF16)
    packed_ref[...] = packed.reshape(peers, cap, width)
    for step, ref in enumerate(block_refs):
        for mate in range(2):
            ref[mate] = packed_ref[partner(2 * step + mate)]


def regroup_kernel(*refs):
    *pair_refs, mine_ref, mate_ref = refs
    for step, ref in enumerate(pair_refs):
        mine_ref[step] = ref[0]
        mate_ref[step] = ref[1]


def group_heads(rows):
    heads = range(GROUP // HEAD_DIM)
    return jnp.concatenate([head_rows(rows[h * HEAD_DIM : (h + 1) * HEAD_DIM], h) for h in heads], axis=1)


def head_rows(rows, head):
    width = rows.shape[1]
    at = (head * HEAD_DIM) % GROUP
    parts = []
    if at:
        parts.append(jnp.zeros((at, width), rows.dtype))
    parts.append(rows)
    if at + HEAD_DIM < GROUP:
        parts.append(jnp.zeros((GROUP - at - HEAD_DIM, width), rows.dtype))
    return jnp.concatenate(parts, axis=0)


def unpack_points_kernel(cap, peers, direct, *refs):
    if not direct:
        recv_ref, high_ref, low_ref = refs[:3]
        recv = recv_ref[...]
        high_rows, low_rows = high_ref[...], low_ref[...]
    else:
        msg_ref = refs[0]
        left = msg_ref[:, :cap, :].reshape(peers * cap, 128)
        right = msg_ref[:, cap : 2 * cap, :].reshape(peers * cap, 128)
        recv = jnp.concatenate([left, right], axis=1)
        tails = [msg_ref[peer, 2 * cap :, :].astype(F32) for peer in range(peers)]
        high_rows = jnp.concatenate([tail[0:1] for tail in tails], axis=0)
        low_rows = jnp.concatenate([tail[1:2] for tail in tails], axis=0)
    target_ref, target_col_ref, rotated_ref = refs[-3:]
    rows = rotated_ref.shape[1]
    slots = peers * cap
    targets = (high_rows - 1.0) * 16.0 + low_rows
    per_row = 128 // cap
    own_lane = iota((per_row, 128), 1) // cap == iota((per_row, 128), 0)
    pieces = []
    for group in range(slots // 128):
        block = targets[group * per_row : (group + 1) * per_row]
        pieces.append(jnp.sum(jnp.where(own_lane, block, 0.0), axis=0, keepdims=True))
    target = jnp.concatenate(pieces, axis=1)
    target_ref[...] = target.astype(jnp.int32)
    target_col_ref[...] = column_of(target).astype(jnp.int32)
    rotated_ref[...] = mm(one_hot(target.astype(jnp.int32), (rows, slots), 0), recv).T


def forward_kernel(
    rotated_ref, w_qkv_ref, w_out_ref, w_up_ref, gain_attn_ref, gain_mlp_ref,
    qkv_t_ref, kv_ref, scales_ref, norm_one_ref, normed_one_ref, attended_ref, norm_two_ref, normed_two_ref,
    hidden_ref, slope_ref, gain_attn_col_ref, gain_mlp_col_ref, *probs_refs,
):
    rot_t = rotated_ref[...]
    width, rows = rot_t.shape
    gain_attn_col = column_of(gain_attn_ref[...])
    gain_attn_col_ref[...] = gain_attn_col
    gain_mlp_col = column_of(gain_mlp_ref[...])
    gain_mlp_col_ref[...] = gain_mlp_col
    scale_one = lax.rsqrt(jnp.mean(rot_t * rot_t, axis=0, keepdims=True) + EPSILON)
    norm_one = rot_t * scale_one
    norm_one_ref[...] = norm_one
    normed_one = (norm_one * lane_tile(gain_attn_col, rows)).astype(BF16)
    normed_one_ref[...] = normed_one
    qkv_t = mm_tn(w_qkv_ref[...], normed_one).astype(BF16)
    qkv_t_ref[...] = qkv_t
    kv_ref[...] = qkv_t[width:].astype(F32).T.astype(BF16)

    for ball in range(rows // BALL):
        at = ball * BALL
        cols = slice(at, at + BALL)
        for group in range(0, width, GROUP):
            queries = group_heads(qkv_t_ref[group : group + GROUP, cols])
            scores = mm(kv_ref[cols, group : group + GROUP], queries) * ATT_SCALE
            top = jnp.max(scores, axis=0, keepdims=True)
            weights = jnp.exp(scores - top)
            probs = weights * (1.0 / jnp.sum(weights, axis=0, keepdims=True))
            probs_refs[ball][group // GROUP] = probs
            probs_low = probs.astype(BF16)
            for head in range(GROUP // HEAD_DIM):
                own = slice(group + head * HEAD_DIM, group + (head + 1) * HEAD_DIM)
                values = qkv_t_ref[2 * width + own.start : 2 * width + own.stop, cols]
                attended_ref[own, cols] = mm(values, probs_low[:, head * BALL : (head + 1) * BALL]).astype(BF16)

    middle = rot_t + mm_tn(w_out_ref[...], attended_ref[...])
    scale_two = lax.rsqrt(jnp.mean(middle * middle, axis=0, keepdims=True) + EPSILON)
    norm_two = middle * scale_two
    norm_two_ref[...] = norm_two
    normed_two = (norm_two * lane_tile(gain_mlp_col, rows)).astype(BF16)
    normed_two_ref[...] = normed_two
    scales_ref[...] = jnp.where(iota(scales_ref.shape, 0) == 0, scale_one, scale_two)
    step = 256
    for at in range(0, hidden_ref.shape[0], step):
        pre_act = mm_tn(w_up_ref[:, at : at + step], normed_two)
        square = pre_act * pre_act
        tanh_val = jnp.tanh(GELU_COEF * (pre_act + 0.044715 * pre_act * square))
        half = 0.5 * (1.0 + tanh_val)
        hidden_ref[at : at + step, :] = (pre_act * half).astype(BF16)
        slope_ref[at : at + step, :] = half + 0.5 * pre_act * (1.0 - tanh_val * tanh_val) * (
            GELU_COEF * (1.0 + 3.0 * 0.044715 * square)
        )


def norm_backward(grad_normed, norm, scale, gain):
    inner = grad_normed * gain
    return scale * (inner - norm * jnp.mean(inner * norm, axis=0, keepdims=True))


def gain_row(product):
    width = product.shape[1]
    partial = product[:, :128]
    for at in range(128, width, 128):
        partial = partial + product[:, at : at + 128]
    return jnp.sum(partial.T, axis=0, keepdims=True)


def place_blocks(blocks_ref, values, first_row, leaf_size, sample_size):
    step = values.shape[0] // (leaf_size * sample_size)
    for block in range(leaf_size * sample_size):
        leaf, sample = divmod(block, sample_size)
        blocks_ref[sample, leaf, first_row : first_row + step, :] = values[block * step : (block + 1) * step]


def part_blocks(blocks_ref, keep_ref, send_ref):
    low = lax.rem(lax.axis_index("sample"), 2)
    for high in range(keep_ref.shape[0]):
        keep_ref[high] = blocks_ref[2 * high + low]
        send_ref[high] = blocks_ref[2 * high + 1 - low].astype(BF16)


def mlp_weights_kernel(
    arranged, direct, target_ref, hidden_ref, slope_ref, normed_two_ref, w_down_ref, *refs
):
    width, rows = normed_two_ref.shape
    if direct:
        mine_ref, mate_ref, *refs, landing_ref = refs
        for step in range(mine_ref.shape[0]):
            landing_ref[partner(2 * step)] = mine_ref[step]
            landing_ref[partner(2 * step + 1)] = mate_ref[step]
        recv_ref = landing_ref
    else:
        recv_ref, *refs = refs
    grad_pre_ref, cot_t_ref, *mat_refs = refs
    recv = recv_ref[...].reshape(-1, width)
    cot_f = mm(one_hot(target_ref[...], (rows, recv.shape[0]), 0), recv)
    cot = cot_f.astype(BF16)
    cot_t = cot_f.T
    cot_t_ref[...] = cot_t
    cot_t_low = cot_t.astype(BF16)
    normed_two = normed_two_ref[...]
    step = 256
    if arranged:
        keep_ref, send_ref, blocks_ref = mat_refs
        leaf_size, sample_size = lax.axis_size("leaf"), lax.axis_size("sample")
        up_rows = width // leaf_size
        down_rows = hidden_ref.shape[0] // (leaf_size * sample_size)
    else:
        grad_up_ref, grad_down_ref = mat_refs
    for at in range(0, hidden_ref.shape[0], step):
        grad_down = mm(hidden_ref[at : at + step, :], cot)
        grad_pre = (mm(w_down_ref[at : at + step, :], cot_t_low) * slope_ref[at : at + step, :]).astype(BF16)
        grad_pre_ref[at : at + step, :] = grad_pre
        grad_up = mm_nt(normed_two, grad_pre)
        if arranged:
            for leaf in range(leaf_size):
                blocks_ref[at // step, leaf, :up_rows, :] = grad_up[leaf * up_rows : (leaf + 1) * up_rows]
            for block in range(step // down_rows):
                leaf, sample = divmod(at // down_rows + block, sample_size)
                piece = grad_down[block * down_rows : (block + 1) * down_rows]
                blocks_ref[sample, leaf, up_rows:, :] = piece
        else:
            grad_down_ref[at : at + step, :] = grad_down.astype(BF16)
            grad_up_ref[:, at : at + step] = grad_up.astype(BF16)
    if arranged:
        part_blocks(blocks_ref, keep_ref, send_ref)


def mlp_inputs_kernel(
    grad_pre_ref, cot_t_ref, norm_two_ref, scales_ref, attended_ref, w_up_ref, w_out_ref, gain_mlp_ref,
    grad_gain_ref, grad_middle_ref, grad_att_ref, grad_out_ref,
):
    grad_normed = mm(w_up_ref[...], grad_pre_ref[...])
    norm_two = norm_two_ref[...]
    grad_gain_ref[...] = gain_row(grad_normed * norm_two)
    gain = lane_tile(gain_mlp_ref[...], norm_two.shape[1])
    grad_middle = cot_t_ref[...] + norm_backward(grad_normed, norm_two, scales_ref[1:2, :], gain)
    grad_middle_ref[...] = grad_middle
    grad_middle_low = grad_middle.astype(BF16)
    grad_att_ref[...] = mm(w_out_ref[...], grad_middle_low).astype(BF16)
    grad_out_ref[...] = mm_nt(attended_ref[...], grad_middle_low)


def ball_backward(ball, qkv_t_ref, kv_ref, probs_ref, grad_att_ref, grad_rows_ref):
    width = qkv_t_ref.shape[0] // 3
    cols = slice(ball * BALL, (ball + 1) * BALL)
    for group in range(0, width, GROUP):
        upstream = grad_att_ref[group : group + GROUP, cols]
        probs = probs_ref[group // GROUP]
        grad_probs = mm(kv_ref[cols, width + group : width + group + GROUP], group_heads(upstream))
        delta = jnp.sum(grad_probs * probs, axis=0, keepdims=True)
        grad_scores = (probs * (grad_probs - delta)).astype(BF16)
        probs_low = probs.astype(BF16)
        for head in range(GROUP // HEAD_DIM):
            first = group + head * HEAD_DIM
            own, own_key, own_value = (slice(at + first, at + first + HEAD_DIM) for at in (0, width, 2 * width))
            part = slice(head * BALL, (head + 1) * BALL)
            scores_of = grad_scores[:, part]
            grad_rows_ref[own, cols] = (mm(qkv_t_ref[own_key, cols], scores_of) * ATT_SCALE).astype(BF16)
            grad_rows_ref[own_key, cols] = (mm_nt(qkv_t_ref[own, cols], scores_of) * ATT_SCALE).astype(BF16)
            grad_rows_ref[own_value, cols] = mm_nt(grad_att_ref[own, cols], probs_low[:, part]).astype(BF16)


def attention_backward_kernel(
    arranged,
    qkv_t_ref, kv_ref, scales_ref, grad_att_ref, grad_middle_ref, norm_one_ref, normed_one_ref,
    w_qkv_ref, gain_attn_ref, target_col_ref, gain_two_ref, grad_out_ref, *refs,
):
    width, rows = norm_one_ref.shape
    probs_refs, refs = refs[: rows // BALL], refs[rows // BALL :]
    back_ref, *mat_refs, grad_rows_ref = refs
    for ball, probs_ref in enumerate(probs_refs):
        ball_backward(ball, qkv_t_ref, kv_ref, probs_ref, grad_att_ref, grad_rows_ref)
    grad_rows = grad_rows_ref[...]
    grad_normed = mm(w_qkv_ref[...], grad_rows)
    norm_one = norm_one_ref[...]
    gain_one = gain_row(grad_normed * norm_one)
    gain = lane_tile(gain_attn_ref[...], rows)
    grad_rot = grad_middle_ref[...] + norm_backward(grad_normed, norm_one, scales_ref[0:1, :], gain)
    place = one_hot(lane_tile(target_col_ref[...], rows), (back_ref.shape[0], rows), 1)
    back_ref[...] = mm_nt(place, grad_rot.astype(BF16)).astype(BF16)
    normed_one = normed_one_ref[...]
    if not arranged:
        mat_refs[0][...] = mm_nt(normed_one, grad_rows).astype(BF16)
        mat_refs[1][...] = gain_one
        return
    keep_ref, send_ref, blocks_ref = mat_refs
    leaf_size, sample_size = lax.axis_size("leaf"), lax.axis_size("sample")
    step = width // (leaf_size * sample_size)
    for col in range(3):
        grad_qkv = mm_nt(normed_one, grad_rows[col * width : (col + 1) * width])
        place_blocks(blocks_ref, grad_qkv, (1 + col) * step, leaf_size, sample_size)
    place_blocks(blocks_ref, grad_out_ref[...], 0, leaf_size, sample_size)
    row = iota((META, width), 0)
    gains = jnp.where(row == 0, gain_one, jnp.where(row == 1, gain_two_ref[...], 0.0))
    for sample in range(sample_size):
        for leaf in range(leaf_size):
            blocks_ref[sample, leaf, 4 * step :, :] = gains
    part_blocks(blocks_ref, keep_ref, send_ref)


def unpack_kernel(slot_ref, returned_ref, out_ref):
    slots = returned_ref.shape[0]
    slot_col = column_of(slot_ref[...].astype(F32)).astype(jnp.int32)
    place = one_hot(lane_tile(slot_col, slots), (out_ref.shape[0], slots), 1)
    out_ref[...] = mm(place, returned_ref[...]).astype(BF16)


def halve_kernel(axis, bit, keep_ref, got_ref, keep_out_ref, send_out_ref):
    mine = lax.rem(lax.div(lax.axis_index(axis), bit), 2)
    for high in range(keep_out_ref.shape[0]):
        for ref, at in ((keep_out_ref, 2 * high + mine), (send_out_ref, 2 * high + 1 - mine)):
            ref[high] = (keep_ref[at] + got_ref[at].astype(F32)).astype(ref.dtype)


def finish_kernel(pairs, *refs):
    ins, (low_ref, gains_ref) = refs[: 2 * pairs], refs[2 * pairs :]
    start = 0
    for pair in range(pairs):
        total = ins[2 * pair][0] + ins[2 * pair + 1][0].astype(F32)
        if pair == pairs - 1:
            gains_ref[...] = total[-META:]
            total = total[:-META]
        low_ref[0, start : start + total.shape[0], :] = total.astype(BF16)
        start += total.shape[0]


def assemble_kernel(scale, offsets, gains_ref, mine_ref, mate_ref, up_ref, down_ref, out_ref, qkv_ref, gain_out_ref):
    size = 2 * len(offsets)
    width = mine_ref.shape[2]
    up_rows, down_rows, out_rows = up_ref.shape[0], down_ref.shape[0] // size, out_ref.shape[0] // size
    me = lax.axis_index("sample")

    def block(source, count):
        return pl.ds(pl.multiple_of(source * count, count), count)

    for index, offset in enumerate(offsets):
        for mate, ref in enumerate((mine_ref, mate_ref)):
            source = me ^ (offset + mate)
            part = ref[index].astype(F32) * scale
            at = up_rows
            up_ref[:, block(source, width)] = part[:at]
            down_ref[block(source, down_rows), :] = part[at : at + down_rows]
            at += down_rows
            out_ref[block(source, out_rows), :] = part[at : at + out_rows]
            at += out_rows
            for col in range(3):
                qkv_ref[block(source, out_rows), col * width : (col + 1) * width] = part[at : at + out_rows]
                at += out_rows
    gain_out_ref[...] = gains_ref[...] * scale


def permute(value, axis, size, bit):
    return lax.ppermute(value, axis, [(i, i ^ bit) for i in range(size)])


def halve(keep, got, axis, bit, name):
    shape = (keep.shape[0] // 2,) + keep.shape[1:]
    return call(functools.partial(halve_kernel, axis, bit), [(shape, F32), (shape, BF16)], name, 0.5, keep, got)


def halve_leaf(keep, got, name):
    leaf_size = lax.axis_size("leaf")
    keep, got = keep[0], got[0]
    bit = 1
    while bit < leaf_size:
        keep, leaving = halve(keep, got, "leaf", bit, name)
        got = permute(leaving, "leaf", leaf_size, bit)
        bit *= 2
    return keep, got


def call(kernel, outs, name, micros, *args, scratch=(), hbm_in=False, hbm_out=False, raw_in=0, raw_out=0, blocked=False, limit=16):
    moved = sum(arg.size * arg.dtype.itemsize for arg in args)
    moved += sum(math.prod(shape) * jnp.dtype(dtype).itemsize for shape, dtype in outs)
    vmem = pl.BlockSpec() if blocked else pl.BlockSpec(memory_space=pltpu.VMEM)
    hbm = pl.BlockSpec(memory_space=pltpu.HBM)
    copied_in = len(args) - raw_in if hbm_in else 0
    copied_out = len(outs) - raw_out if hbm_out else 0
    parts = 2

    def body(*refs):
        ins, refs = list(refs[: len(args)]), refs[len(args) :]
        results, refs = list(refs[: len(outs)]), refs[len(outs) :]
        own, refs = refs[: len(scratch)], refs[len(scratch) :]
        in_bufs, refs = refs[:copied_in], refs[copied_in:]
        out_bufs, refs = refs[:copied_out], refs[copied_out:]
        for at, buf in enumerate(in_bufs):
            copy = pltpu.make_async_copy(ins[at], buf, refs[0].at[at])
            copy.start()
            ins[at] = Arriving(buf, [copy])
        for at, buf in enumerate(out_bufs):
            results[at] = Leaving(buf, results[at], refs[-1].at[at])
        kernel(*ins, *results, *own)
        for ref in ins:
            if isinstance(ref, Arriving):
                for copy in ref.copies:
                    copy.wait()
        for ref in results[:copied_out]:
            ref.send()
        for ref in results[:copied_out]:
            for copy in ref.copies:
                copy.wait()

    extra = [pltpu.VMEM(arg.shape, arg.dtype) for arg in args[:copied_in]]
    extra += [pltpu.VMEM(shape, dtype) for shape, dtype in outs[:copied_out]]
    if copied_in:
        extra.append(pltpu.SemaphoreType.DMA((copied_in,)))
    if copied_out:
        extra.append(pltpu.SemaphoreType.DMA((copied_out, parts)))
    return pl.pallas_call(
        body,
        out_shape=[jax.ShapeDtypeStruct(shape, dtype) for shape, dtype in outs],
        in_specs=[hbm if hbm_in else vmem] * (len(args) - raw_in) + [hbm] * raw_in,
        out_specs=[hbm if hbm_out else vmem] * (len(outs) - raw_out) + [hbm] * raw_out,
        scratch_shapes=list(scratch) + extra,
        compiler_params=pltpu.CompilerParams(vmem_limit_bytes=limit * 1024 * 1024),
        cost_estimate=pl.CostEstimate(flops=int(micros * 1.1e9), bytes_accessed=moved, transcendentals=0),
        name=name,
    )(*args)


def exchange(flat, axes, peers):
    moved = lax.all_to_all(
        flat.reshape((peers, -1) + flat.shape[1:]), axes, split_axis=0, concat_axis=0, tiled=True
    )
    return moved.reshape(flat.shape)


def local(points, cotangent, dest_pos, w_qkv, w_out, w_up, w_down, gain_attn, gain_mlp):
    rows, width = points.shape
    hidden_width = w_up.shape[1]
    axes = ("leaf", "sample")
    peers = lax.axis_size(axes)
    leaf_size, sample_size = lax.axis_size("leaf"), lax.axis_size("sample")
    cap = 2 * rows // peers
    slots = peers * cap
    balls = rows // BALL
    direct = cap % 16 == 0
    paired = leaf_size & (leaf_size - 1) == 0 and sample_size & (sample_size - 1) == 0 and sample_size > 1
    arranged = paired and width % (16 * peers) == 0 and hidden_width == sample_size * width and leaf_size <= 8
    inv_root = 1.0 / math.sqrt(rows * peers)

    msg_rows = 2 * cap + META
    if direct:
        outs = [((peers, msg_rows, 128), BF16)]
    else:
        outs = [((slots, width), BF16), ((peers, 128), F32), ((peers, 128), F32)]
    slot, *message = call(
        functools.partial(pack_points_kernel, peers, cap, direct),
        [((1, rows), jnp.int32)] + outs, "pack_points", 2, dest_pos.reshape(1, rows), points, hbm_in=True, hbm_out=True, limit=60,
    )
    if direct:
        forward_args = [exchange(message[0].reshape(-1, 128), axes, peers).reshape(peers, msg_rows, 128)]
    else:
        packed, high, low = message
        tail = jnp.stack([high, low], axis=1).astype(BF16)
        halves = packed.reshape(peers, cap, 2, 128).transpose(0, 2, 1, 3).reshape(peers, 2 * cap, 128)
        flat = jnp.concatenate([halves, tail], axis=1).reshape(-1, 128)
        arrived = exchange(flat, axes, peers).reshape(peers, 2 * cap + 2, 128)
        halves = arrived[:, : 2 * cap].reshape(peers, 2, cap, 128).transpose(0, 2, 1, 3).reshape(slots, width)
        forward_args = [halves, arrived[:, 2 * cap].astype(F32), arrived[:, 2 * cap + 1].astype(F32)]
    by_permute = direct and paired and peers <= 16
    if by_permute:
        packed_cot = call(
            pack_cot_kernel, [((2, cap, width), BF16)] * (peers // 2), "pack_cot", 1, slot, cotangent,
            scratch=[pltpu.VMEM((peers, cap, width), BF16)],
        )
        pairs = [packed_cot[0]] + [permute(packed_cot[step], axes, peers, 2 * step) for step in range(1, peers // 2)]
        *pairs[1:3], forward_args[0] = lax.optimization_barrier((*pairs[1:3], forward_args[0]))
    else:
        (packed_cot,) = call(pack_cot_kernel, [((slots, width), BF16)], "pack_cot", 1, slot, cotangent)
        arrived_cot = [exchange(packed_cot, axes, peers)]
    target, target_col, rotated = call(
        functools.partial(unpack_points_kernel, cap, peers, direct),
        [((1, slots), jnp.int32), ((slots, 128), jnp.int32), ((width, rows), F32)],
        "unpack_points", 2, *forward_args,
    )
    (
        qkv_t, kv, scales, norm_one, normed_one, attended, norm_two, normed_two, hidden, slope,
        gain_attn_col, gain_mlp_col, *probs,
    ) = call(
        forward_kernel,
        [
            ((3 * width, rows), BF16), ((rows, 2 * width), BF16), ((8, rows), F32),
            ((width, rows), F32), ((width, rows), BF16), ((width, rows), BF16),
            ((width, rows), F32), ((width, rows), BF16),
            ((hidden_width, rows), BF16), ((hidden_width, rows), F32), ((width, 128), F32), ((width, 128), F32),
        ] + [((width // GROUP, BALL, GROUP // HEAD_DIM * BALL), F32)] * balls,
        "forward", 7, rotated, w_qkv, w_out, w_up, gain_attn.reshape(1, width), gain_mlp.reshape(1, width),
    )
    if by_permute:
        scales, *pairs = lax.optimization_barrier((scales, *pairs))
        half = ((peers // 2, cap, width), BF16)
        mine, for_mate = call(regroup_kernel, [half] * 2, "regroup", 0.3, *pairs)
        arrived_cot = [mine, permute(for_mate, axes, peers, 1)]
    mlp_scratch, qkv_scratch = [], []
    if arranged:
        halved = (sample_size // 2, leaf_size)
        mlp_rows = width // leaf_size + hidden_width // peers
        qkv_rows = 4 * width // peers + META
        mlp_mats = [(halved + (mlp_rows, width), F32), (halved + (mlp_rows, width), BF16)]
        qkv_mats = [(halved + (qkv_rows, width), F32), (halved + (qkv_rows, width), BF16)]
        mlp_scratch = [pltpu.VMEM((sample_size, leaf_size, mlp_rows, width), F32)]
        qkv_scratch = [pltpu.VMEM((sample_size, leaf_size, qkv_rows, width), F32)]
    else:
        mlp_mats = [(w_up.shape, BF16), (w_down.shape, BF16)]
        qkv_mats = [(w_qkv.shape, BF16), ((1, width), F32)]
    grad_pre, cot_t, *mlp_grads = call(
        functools.partial(mlp_weights_kernel, arranged, by_permute),
        [((hidden_width, rows), BF16), ((width, rows), F32)] + mlp_mats,
        "mlp_weights", 2.5, target, hidden, slope, normed_two, w_down, *arrived_cot,
        scratch=mlp_scratch + ([pltpu.VMEM((peers, cap, width), BF16)] if by_permute else []),
    )
    gain_two, grad_middle, grad_att, grad_out = call(
        mlp_inputs_kernel,
        [((1, width), F32), ((width, rows), F32), ((width, rows), BF16), ((width, width), F32)],
        "mlp_inputs", 1.5, grad_pre, cot_t, norm_two, scales, attended, w_up, w_out, gain_mlp_col,
    )
    if arranged:
        keep_mlp, send_mlp = mlp_grads
        got_mlp = permute(send_mlp, "sample", sample_size, 1)
        bit = 2
        while bit < sample_size:
            keep_mlp, send_mlp = halve(keep_mlp, got_mlp, "sample", bit, "halve_mlp")
            grad_att, send_mlp = lax.optimization_barrier((grad_att, send_mlp))
            got_mlp = permute(send_mlp, "sample", sample_size, bit)
            bit *= 2
    back, *qkv_grads = call(
        functools.partial(attention_backward_kernel, arranged),
        [((slots, width), BF16)] + qkv_mats, "attention_backward", 6,
        qkv_t, kv, scales, grad_att, grad_middle, norm_one, normed_one,
        w_qkv, gain_attn_col, target_col, gain_two, grad_out, *probs,
        scratch=qkv_scratch + [pltpu.VMEM((3 * width, rows), BF16)],
    )
    if arranged:
        back, got_mlp = lax.optimization_barrier((back, got_mlp))
    returned = exchange(back, axes, peers)
    (grad_points,) = call(unpack_kernel, [((rows, width), BF16)], "unpack", 1, slot, returned, blocked=True)
    if not arranged:
        up_sum, down_sum, out_sum = reduce_mats([*mlp_grads, grad_out])
        qkv_sum, gain_sum = reduce_mats([qkv_grads[0]], jnp.concatenate([qkv_grads[1], gain_two], axis=0))
        return (
            grad_points, qkv_sum * inv_root, out_sum * inv_root, up_sum * inv_root, down_sum * inv_root,
            gain_sum[0] * inv_root, gain_sum[1] * inv_root,
        )
    keep_qkv, send_qkv = qkv_grads
    got_qkv = permute(send_qkv, "sample", sample_size, 1)
    bit = 2
    while bit < sample_size:
        keep_qkv, send_qkv = halve(keep_qkv, got_qkv, "sample", bit, "halve_qkv")
        got_qkv = permute(send_qkv, "sample", sample_size, bit)
        bit *= 2
    low, gains = call(
        functools.partial(finish_kernel, 2),
        [((1, mlp_rows + qkv_rows - META, width), BF16), ((META, width), F32)], "finish", 0.5,
        *halve_leaf(keep_mlp, got_mlp, "leaf_mlp"), *halve_leaf(keep_qkv, got_qkv, "leaf_qkv"),
    )
    offsets = [0]
    bit = sample_size // 2
    while bit > 1:
        low = jnp.concatenate([low, permute(low, "sample", sample_size, bit)], axis=0)
        offsets += [offset ^ bit for offset in offsets]
        bit //= 2
    mate = permute(low, "sample", sample_size, 1)
    grad_points, gains = lax.optimization_barrier((grad_points, gains))
    share = width // leaf_size
    up_sum, down_sum, out_sum, qkv_sum, gain_sum = call(
        functools.partial(assemble_kernel, inv_root, offsets),
        [
            ((share, hidden_width), F32), ((hidden_width // leaf_size, width), F32), ((share, width), F32),
            ((share, 3 * width), F32), ((META, width), F32),
        ],
        "assemble", 1, gains, low, mate, blocked=True,
    )
    gains = lax.dynamic_slice(gain_sum, (0, lax.axis_index("leaf") * share), (2, share))
    return (grad_points, qkv_sum, out_sum, up_sum, down_sum, gains[0], gains[1])


def reduce_mats(mats, gains=None):
    leaf_size = lax.axis_size("leaf")
    sample_size = lax.axis_size("sample")
    me = lax.axis_index("sample")
    pieces = []
    for mat in mats:
        pieces.append(mat.reshape(leaf_size, sample_size, -1, 128).transpose(1, 0, 2, 3))
    if gains is not None:
        gain_block = gains.reshape(2, leaf_size, -1).transpose(1, 0, 2).reshape(1, leaf_size, 1, -1)
        gain_block = jnp.pad(gain_block, ((0, 0), (0, 0), (0, 15), (0, 128 - gain_block.shape[3])))
        pieces.append(jnp.broadcast_to(gain_block, (sample_size,) + gain_block.shape[1:]))
    current = jnp.concatenate(pieces, axis=2).astype(jnp.bfloat16)
    bit = 1
    while bit < sample_size:
        split = current.reshape((current.shape[0] // 2, 2) + current.shape[1:])
        mine = (me // bit) % 2
        keep = lax.dynamic_index_in_dim(split, mine, 1, keepdims=False)
        send = lax.dynamic_index_in_dim(split, 1 - mine, 1, keepdims=False)
        got = lax.ppermute(send, "sample", [(i, i ^ bit) for i in range(sample_size)])
        current = (keep.astype(jnp.float32) + got.astype(jnp.float32)).astype(jnp.bfloat16)
        bit *= 2
    current = lax.all_to_all(current[0], "leaf", split_axis=0, concat_axis=0, tiled=True)
    total = jnp.sum(current.astype(jnp.float32), axis=0)
    low = total.astype(jnp.bfloat16)
    gathered = jnp.zeros((sample_size,) + low.shape, jnp.bfloat16)
    for step in range(sample_size):
        got = low if step == 0 else lax.ppermute(low, "sample", [(i, i ^ step) for i in range(sample_size)])
        gathered = lax.dynamic_update_index_in_dim(gathered, got, me ^ step, 0)
    results = []
    start = 0
    for mat in mats:
        rows = mat.size // (leaf_size * sample_size * 128)
        part = gathered[:, start : start + rows].astype(jnp.float32)
        results.append(part.reshape(mat.shape[0] // leaf_size, mat.shape[1]))
        start += rows
    if gains is not None:
        width = gains.shape[1] // leaf_size
        results.append(total[start, : 2 * width].reshape(2, width))
    return results


def solution(mesh):
    in_specs = (
        P(("groups", "leaf", "sample"), None),
        P(("groups", "leaf", "sample"), None),
        P(("groups", "leaf", "sample")),
        P(),
        P(),
        P(),
        P(),
        P(),
        P(),
    )
    out_specs = (
        P(("groups", "leaf", "sample"), None),
        P(("groups", "leaf"), None),
        P(("groups", "leaf"), None),
        P(("groups", "leaf"), None),
        P(("groups", "leaf"), None),
        P(("groups", "leaf")),
        P(("groups", "leaf")),
    )
    return jax.shard_map(local, mesh=mesh, in_specs=in_specs, out_specs=out_specs, check_vma=False)
```

time: 250 us -> 87.5 us (0.35)
  waiting for transfers between devices: 122 us -> 27.8 us
  local copies, waits for them, and re-layouts: 36.2 us -> 1.32 us
  matrix products: 26.9 us -> 0 us
  starting transfers between devices: 19.6 us -> 38.5 us
  Pallas kernels: 0 us -> 18.6 us
  blocking collectives: 15.4 us -> 0 us
  other arithmetic: 14.5 us -> 0 us
  between operations: 15 us -> 0.88 us
    reduce_scatter x4 -> x0, waiting for transfers between devices: 83.8 us -> none  [the longest x1 29.9 us: local(): lax.psum_scatter(grad_down, 'leaf', scatter_dimension=0, tiled=True)]
    ppermute x0 -> x18, waiting for transfers between devices: none -> 27.8 us  [permute(): return lax.ppermute(value, axis, [(i, i ^ bit) for i in range(size)])]
    ppermute x0 -> x18, starting transfers between devices: none -> 26.2 us  [permute(): return lax.ppermute(value, axis, [(i, i ^ bit) for i in range(size)])]
    dot_general x16 -> x0, matrix products: 23.4 us -> none  [the longest x1 3.77 us: ball_backward(): jnp.einsum('ghqk,gqhd->gkhd', probs_low, upstream, preferred_element_type...]
    all_to_all x4 -> x2, waiting for transfers between devices: 21.6 us -> 0.01 us  [exchange(): lax.all_to_all(flat.reshape((peers, -1) + flat.shape[1:]), axes, split_ax...]
    scatter x7 -> x0, local copies, waits for them, and re-layouts: 19.9 us -> none  [the longest x2 7.08 us: local(): jnp.zeros((peer_count * capacity, feat_width), jnp.bfloat16).at[slot_index]]
    pallas_call x0 -> x17, Pallas kernels: none -> 18.6 us  [call(): pl.pallas_call(body, out_shape=[jax.ShapeDtypeStruct(shape, dtype) for sh...]
    psum x1 -> x0, waiting for transfers between devices: 16.4 us -> none  [local(): lax.psum((shares[0], shares[1], shares[2], shares[3], shares[4], shares[5...]
  transfers between devices with their start and end apart: 9 -> 20, of which waited for: 7 -> 12; matrix products, arithmetic and copies ran while one was open for 15% -> 0% of each run, Pallas kernels for 0% -> 14%
where the time goes in v1:
time: 87.5 us; the launch traced here: 87.1 us
  starting transfers between devices  38.5 us (44%)
  waiting for transfers between devices  27.8 us (32%)
  Pallas kernels  18.6 us (21%)
  local copies, waits for them, and re-layouts  1.32 us (2%)
  between operations  0.88 us (1%)
    ppermute x18, waiting for transfers between devices, permute(): return lax.ppermute(value, axis, [(i, i ^ bit) for i in range(size)])  27.8 us
    ppermute x18, starting transfers between devices, permute(): return lax.ppermute(value, axis, [(i, i ^ bit) for i in range(size)])  26.2 us
    pallas_call x17, Pallas kernels, call(): pl.pallas_call(body, out_shape=[jax.ShapeDtypeStruct(shape, dtype) for sh...  18.6 us
    all_to_all x2, starting transfers between devices, exchange(): lax.all_to_all(flat.reshape((peers, -1) + flat.shape[1:]), axes, split_ax...  12.3 us
  transfers between devices with their start and end apart: 20, of which 12 were waited for; matrix products, arithmetic and copies ran while one was open for 0% of the time, Pallas kernels for 14%

profile of v1, /device:TPU:0, one launch (start us, length us, event | category | flops | bytes accessed | tf_op | source)
XLA Modules:
  0.0 87.1 jit_solution(17698963808710977561)
XLA Ops:
  0.6 2.6 %pack_points.1 = (s32[1,512]{1,0:T(1,128)}, bf16[16,144,128]{2,1,0:T(8,128)(2,1)}) custom-call(s32[1,512]{1,0:T(1,128)} %bitcast.20, bf16[512,256]{1,0:T(8,128)(2,1)} %refs_1_.3), custom_call_target="tpu_custom_call" | custom-call | flops 2200000000 | bytes 856064 | tf_op jit(solution)/shard_map/pack_points/pallas_call | solution.py:507
  3.2 7.4 %all-to-all-start = ((bf16[16,144,128]{2,1,0:T(8,128)(2,1)}), bf16[16,144,128]{2,1,0:T(8,128)(2,1)S(1)}, u32[]{:S(2)}, u32[]{:S(2)}) async-start(bf16[16,144,128]{2,1,0:T(8,128)(2,1)} %get-tuple-element.87), calls=%async_computation | async-start | bytes 1179648 | tf_op jit(solution)/shard_map/all_to_all | solution.py:520
  11.8 2.0 %collective-permute-start = (bf16[2,64,256]{2,1,0:T(8,128)(2,1)S(1)}, bf16[2,64,256]{2,1,0:T(8,128)(2,1)S(1)}, u32[]{:S(2)}, u32[]{:S(2)}) collective-permute-start(bf16[2,64,256]{2,1,0:T(8,128)(2,1)S(1)} %get-tuple-element.85), channel_id=1, source_target_pairs={{0,2},{1,3},{2,0},{3,1},{4,6},{5,7},{6,4},{7,5},{8,10},{9,11},{10,... | collective-permute-start | bytes 196616 | tf_op jit(solution)/shard_map/ppermute | solution.py:450
  13.7 1.5 %collective-permute-start.1 = (bf16[2,64,256]{2,1,0:T(8,128)(2,1)S(1)}, bf16[2,64,256]{2,1,0:T(8,128)(2,1)S(1)}, u32[]{:S(2)}, u32[]{:S(2)}) collective-permute-start(bf16[2,64,256]{2,1,0:T(8,128)(2,1)S(1)} %get-tuple-element.86), channel_id=1, source_target_pairs={{0,4},{1,5},{2,6},{3,7},{4,0},{5,1},{6,2},{7,3},{8,12},{9,13},{10,... | collective-permute-start | bytes 196616 | tf_op jit(solution)/shard_map/ppermute | solution.py:450
  15.3 2.8 %collective-permute-start.3 = (bf16[2,64,256]{2,1,0:T(8,128)(2,1)S(1)}, bf16[2,64,256]{2,1,0:T(8,128)(2,1)S(1)}, u32[]{:S(2)}, u32[]{:S(2)}) collective-permute-start(bf16[2,64,256]{2,1,0:T(8,128)(2,1)S(1)} %get-tuple-element.97), channel_id=1, source_target_pairs={{0,8},{1,9},{2,10},{3,11},{4,12},{5,13},{6,14},{7,15},{8,0},{9,1},... | collective-permute-start | bytes 196616 | tf_op jit(solution)/shard_map/ppermute | solution.py:450
  19.6 3.3 %collective-permute-start.5 = (bf16[2,64,256]{2,1,0:T(8,128)(2,1)S(1)}, bf16[2,64,256]{2,1,0:T(8,128)(2,1)S(1)}, u32[]{:S(2)}, u32[]{:S(2)}) collective-permute-start(bf16[2,64,256]{2,1,0:T(8,128)(2,1)S(1)} %get-tuple-element.99), channel_id=1, source_target_pairs={{0,12},{1,13},{2,14},{3,15},{4,8},{5,9},{6,10},{7,11},{8,4},{9,5},... | collective-permute-start | bytes 196616 | tf_op jit(solution)/shard_map/ppermute | solution.py:450
  23.6 4.0 %collective-permute-start.6 = (bf16[2,64,256]{2,1,0:T(8,128)(2,1)S(1)}, bf16[2,64,256]{2,1,0:T(8,128)(2,1)S(1)}, u32[]{:S(2)}, u32[]{:S(2)}) collective-permute-start(bf16[2,64,256]{2,1,0:T(8,128)(2,1)S(1)} %get-tuple-element.100), channel_id=1, source_target_pairs={{0,14},{1,15},{2,12},{3,13},{4,10},{5,11},{6,8},{7,9},{8,6},{9,7},... | collective-permute-start | bytes 196616 | tf_op jit(solution)/shard_map/ppermute | solution.py:450
  28.1 4.5 %forward.1 = (bf16[768,512]{1,0:T(8,128)(2,1)S(1)}, bf16[512,512]{1,0:T(8,128)(2,1)S(1)}, f32[8,512]{1,0:T(8,128)S(1)}, f32[256,512]{1,0:T(8,128)S(1)}, bf16[256...) custom-call(f32[256,512]{1,0:T(8,128)S(1)} %get-tuple-element.89.ref, ...), custom_call_target="tpu_custom_call" | custom-call | flops 7699999744 | bytes 12339200 | tf_op jit(solution)/shard_map/forward/pallas_call | solution.py:507
  32.7 2.1 %collective-permute-done.3.refs_4_ = bf16[2,64,256]{2,1,0:T(8,128)(2,1)S(1)} collective-permute-done((bf16[2,64,256]{2,1,0:T(8,128)(2,1)S(1)}, bf16[2,64,256]{2,1,0:T(8,128)(2,1)S(1)}, u32[]{:S(2)}, u32[]{:S(2)}) %collective-permute-start.3) | collective-permute-done | bytes 65568 | tf_op jit(solution)/shard_map/ppermute | solution.py:450
  34.8 2.3 %collective-permute-done.4.refs_5_ = bf16[2,64,256]{2,1,0:T(8,128)(2,1)S(1)} collective-permute-done((bf16[2,64,256]{2,1,0:T(8,128)(2,1)S(1)}, bf16[2,64,256]{2,1,0:T(8,128)(2,1)S(1)}, u32[]{:S(2)}, u32[]{:S(2)}) %collective-permute-start.4) | collective-permute-done | bytes 65568 | tf_op jit(solution)/shard_map/ppermute | solution.py:450
  37.3 1.5 %collective-permute-done.7.refs_6_ = bf16[8,64,256]{2,1,0:T(8,128)(2,1)S(1)} collective-permute-done((bf16[8,64,256]{2,1,0:T(8,128)(2,1)S(1)}, bf16[8,64,256]{2,1,0:T(8,128)(2,1)S(1)}, u32[]{:S(2)}, u32[]{:S(2)}) %collective-permute-start.7) | collective-permute-done | bytes 262176 | tf_op jit(solution)/shard_map/ppermute | solution.py:450
  38.8 2.6 %mlp_weights.1 = (bf16[1024,512]{1,0:T(8,128)(2,1)S(1)}, f32[256,512]{1,0:T(8,128)S(1)}, f32[2,4,128,256]{3,2,1,0:T(8,128)S(1)}, bf16[2,4,128,256]{3,2,1,0:T(8,128)(2,1)S(1)}) custom-call(s32[1,1024]{1,0:T(1,128)S(1)} %get-tuple-element.102.refs_0_, bf16[1024,512]{1,0:T(8,128)(2,1)S(1)} %get-tuple-element.103.refs_1_, ...), custom_call_target="tpu_custom_call" | custom-call | flops 2750000128 | bytes 7606272 | tf_op jit(solution)/shard_map/mlp_weights/pallas_call | solution.py:507
  44.0 4.6 %attention_backward.1 = (bf16[1024,256]{1,0:T(8,128)(2,1)}, f32[2,4,80,256]{3,2,1,0:T(8,128)S(1)}, bf16[2,4,80,256]{3,2,1,0:T(8,128)(2,1)S(1)}) custom-call(bf16[768,512]{1,0:T(8,128)(2,1)S(1)} %get-tuple-element.90.refs_0_, bf16[512,512]{1,0:T(8,128)(2,1)S(1)} %get-tuple-element.91.refs_1_, f32[8,512]{1,0:T(8,128)S(1)} %get-tuple-element.101.refs_3_.refs_2_, ...), custom_call_target="tpu_custom_call" | custom-call | flops 6600000000 | bytes 9913344 | tf_op jit(solution)/shard_map/attention_backward/pallas_call | solution.py:507
  48.6 3.3 %collective-permute-done.9 = bf16[1,4,128,256]{3,2,1,0:T(8,128)(2,1)S(1)} collective-permute-done((bf16[1,4,128,256]{3,2,1,0:T(8,128)(2,1)S(1)}, bf16[1,4,128,256]{3,2,1,0:T(8,128)(2,1)S(1)}, u32[]{:S(2)}, u32[]{:S(2)}) %collective-permute-start.9) | collective-permute-done | bytes 262176 | tf_op jit(solution)/shard_map/ppermute | solution.py:450
  51.9 4.9 %all-to-all-start.1 = ((bf16[16,64,256]{2,1,0:T(8,128)(2,1)}), bf16[16,64,256]{2,1,0:T(8,128)(2,1)S(1)}, u32[]{:S(2)}, u32[]{:S(2)}) async-start(bf16[16,64,256]{2,1,0:T(8,128)(2,1)} %bitcast.3), calls=%async_computation.1 | async-start | bytes 1048576 | tf_op jit(solution)/shard_map/all_to_all | solution.py:520
  56.9 2.0 %collective-permute-start.13 = (bf16[1,4,80,256]{3,2,1,0:T(8,128)(2,1)S(1)}, bf16[1,4,80,256]{3,2,1,0:T(8,128)(2,1)S(1)}, u32[]{:S(2)}, u32[]{:S(2)}) collective-permute-start(bf16[1,4,80,256]{3,2,1,0:T(8,128)(2,1)S(1)} %get-tuple-element.147), channel_id=1, source_target_pairs={{0,2},{1,3},{2,0},{3,1},{4,6},{5,7},{6,4},{7,5},{8,10},{9,11},{10,... | collective-permute-start | bytes 491528 | tf_op jit(solution)/shard_map/ppermute | solution.py:450
  58.9 1.5 %collective-permute-start.10 = (bf16[2,128,256]{2,1,0:T(8,128)(2,1)S(1)}, bf16[2,128,256]{2,1,0:T(8,128)(2,1)S(1)}, u32[]{:S(2)}, u32[]{:S(2)}) collective-permute-start(bf16[2,128,256]{2,1,0:T(8,128)(2,1)S(1)} %get-tuple-element.141), channel_id=1, source_target_pairs={{0,4},{4,0},{8,12},{12,8},{1,5},{5,1},{9,13},{13,9},{2,6},{6,2},{1... | collective-permute-start | bytes 393224 | tf_op jit(solution)/shard_map/ppermute | solution.py:450
  60.5 7.3 %collective-permute-done.13 = bf16[1,4,80,256]{3,2,1,0:T(8,128)(2,1)S(1)} collective-permute-done((bf16[1,4,80,256]{3,2,1,0:T(8,128)(2,1)S(1)}, bf16[1,4,80,256]{3,2,1,0:T(8,128)(2,1)S(1)}, u32[]{:S(2)}, u32[]{:S(2)}) %collective-permute-start.13) | collective-permute-done | bytes 163872 | tf_op jit(solution)/shard_map/ppermute | solution.py:450
  68.8 2.8 %collective-permute-done.10.refs_1_ = bf16[2,128,256]{2,1,0:T(8,128)(2,1)S(1)} collective-permute-done((bf16[2,128,256]{2,1,0:T(8,128)(2,1)S(1)}, bf16[2,128,256]{2,1,0:T(8,128)(2,1)S(1)}, u32[]{:S(2)}, u32[]{:S(2)}) %collective-permute-start.10) | collective-permute-done | bytes 131104 | tf_op jit(solution)/shard_map/ppermute | solution.py:450
  71.7 2.5 %collective-permute-start.11 = (bf16[1,128,256]{2,1,0:T(8,128)(2,1)S(1)}, bf16[1,128,256]{2,1,0:T(8,128)(2,1)S(1)}, u32[]{:S(2)}, u32[]{:S(2)}) collective-permute-start(bf16[1,128,256]{2,1,0:T(8,128)(2,1)S(1)} %get-tuple-element.143), channel_id=1, source_target_pairs={{0,8},{4,12},{8,0},{12,4},{1,9},{5,13},{9,1},{13,5},{2,10},{6,14},... | collective-permute-start | bytes 196616 | tf_op jit(solution)/shard_map/ppermute | solution.py:450
  74.2 1.5 %collective-permute-start.15 = (bf16[1,80,256]{2,1,0:T(8,128)(2,1)S(1)}, bf16[1,80,256]{2,1,0:T(8,128)(2,1)S(1)}, u32[]{:S(2)}, u32[]{:S(2)}) collective-permute-start(bf16[1,80,256]{2,1,0:T(8,128)(2,1)S(1)} %get-tuple-element.151), channel_id=1, source_target_pairs={{0,8},{4,12},{8,0},{12,4},{1,9},{5,13},{9,1},{13,5},{2,10},{6,14},... | collective-permute-start | bytes 122888 | tf_op jit(solution)/shard_map/ppermute | solution.py:450
  75.7 2.3 %collective-permute-done.11.refs_1_ = bf16[1,128,256]{2,1,0:T(8,128)(2,1)S(1)} collective-permute-done((bf16[1,128,256]{2,1,0:T(8,128)(2,1)S(1)}, bf16[1,128,256]{2,1,0:T(8,128)(2,1)S(1)}, u32[]{:S(2)}, u32[]{:S(2)}) %collective-permute-start.11) | collective-permute-done | bytes 65568 | tf_op jit(solution)/shard_map/ppermute | solution.py:450
  79.4 1.6 %collective-permute-start.16 = (bf16[1,192,256]{2,1,0:T(8,128)(2,1)S(1)}, bf16[1,192,256]{2,1,0:T(8,128)(2,1)S(1)}, u32[]{:S(2)}, u32[]{:S(2)}) collective-permute-start(bf16[1,192,256]{2,1,0:T(8,128)(2,1)S(1)} %get-tuple-element.155), channel_id=1, source_target_pairs={{0,2},{1,3},{2,0},{3,1},{4,6},{5,7},{6,4},{7,5},{8,10},{9,11},{10,... | collective-permute-start | bytes 294920 | tf_op jit(solution)/shard_map/ppermute | solution.py:450
  81.0 3.1 %collective-permute-done.16 = bf16[1,192,256]{2,1,0:T(8,128)(2,1)S(1)} collective-permute-done((bf16[1,192,256]{2,1,0:T(8,128)(2,1)S(1)}, bf16[1,192,256]{2,1,0:T(8,128)(2,1)S(1)}, u32[]{:S(2)}, u32[]{:S(2)}) %collective-permute-start.16) | collective-permute-done | bytes 98336 | tf_op jit(solution)/shard_map/ppermute | solution.py:450
  (55 shorter events, 12.4 us)
Async XLA Ops:
  0.6 10.0 %copy-start.3 = (bf16[512,256]{1,0:T(8,128)(2,1)S(1)}, bf16[512,256]{1,0:T(8,128)(2,1)}, u32[]{:S(2)}) copy-start(bf16[512,256]{1,0:T(8,128)(2,1)} %refs_1_.4) | copy-start | bytes 786436
  3.2 24.3 %all-to-all-start = ((bf16[16,144,128]{2,1,0:T(8,128)(2,1)}), bf16[16,144,128]{2,1,0:T(8,128)(2,1)S(1)}, u32[]{:S(2)}, u32[]{:S(2)}) async-start(bf16[16,144,128]{2,1,0:T(8,128)(2,1)} %get-tuple-element.87), calls=%async_computation | async-start | bytes 1179648 | tf_op jit(solution)/shard_map/all_to_all | solution.py:520
  11.8 7.8 %collective-permute-start = (bf16[2,64,256]{2,1,0:T(8,128)(2,1)S(1)}, bf16[2,64,256]{2,1,0:T(8,128)(2,1)S(1)}, u32[]{:S(2)}, u32[]{:S(2)}) collective-permute-start(bf16[2,64,256]{2,1,0:T(8,128)(2,1)S(1)} %get-tuple-element.85), channel_id=1, source_target_pairs={{0,2},{1,3},{2,0},{3,1},{4,6},{5,7},{6,4},{7,5},{8,10},{9,11},{10,... | collective-permute-start | bytes 196616 | tf_op jit(solution)/shard_map/ppermute | solution.py:450
  13.7 9.8 %collective-permute-start.1 = (bf16[2,64,256]{2,1,0:T(8,128)(2,1)S(1)}, bf16[2,64,256]{2,1,0:T(8,128)(2,1)S(1)}, u32[]{:S(2)}, u32[]{:S(2)}) collective-permute-start(bf16[2,64,256]{2,1,0:T(8,128)(2,1)S(1)} %get-tuple-element.86), channel_id=1, source_target_pairs={{0,4},{1,5},{2,6},{3,7},{4,0},{5,1},{6,2},{7,3},{8,12},{9,13},{10,... | collective-permute-start | bytes 196616 | tf_op jit(solution)/shard_map/ppermute | solution.py:450
  15.2 17.5 %collective-permute-start.2 = (bf16[2,64,256]{2,1,0:T(8,128)(2,1)S(1)}, bf16[2,64,256]{2,1,0:T(8,128)(2,1)S(1)}, u32[]{:S(2)}, u32[]{:S(2)}) collective-permute-start(bf16[2,64,256]{2,1,0:T(8,128)(2,1)S(1)} %get-tuple-element.96), channel_id=1, source_target_pairs={{0,6},{1,7},{2,4},{3,5},{4,2},{5,3},{6,0},{7,1},{8,14},{9,15},{10,... | collective-permute-start | bytes 196616 | tf_op jit(solution)/shard_map/ppermute | solution.py:450
  15.3 19.5 %collective-permute-start.3 = (bf16[2,64,256]{2,1,0:T(8,128)(2,1)S(1)}, bf16[2,64,256]{2,1,0:T(8,128)(2,1)S(1)}, u32[]{:S(2)}, u32[]{:S(2)}) collective-permute-start(bf16[2,64,256]{2,1,0:T(8,128)(2,1)S(1)} %get-tuple-element.97), channel_id=1, source_target_pairs={{0,8},{1,9},{2,10},{3,11},{4,12},{5,13},{6,14},{7,15},{8,0},{9,1},... | collective-permute-start | bytes 196616 | tf_op jit(solution)/shard_map/ppermute | solution.py:450
  18.1 19.0 %collective-permute-start.4 = (bf16[2,64,256]{2,1,0:T(8,128)(2,1)S(1)}, bf16[2,64,256]{2,1,0:T(8,128)(2,1)S(1)}, u32[]{:S(2)}, u32[]{:S(2)}) collective-permute-start(bf16[2,64,256]{2,1,0:T(8,128)(2,1)S(1)} %get-tuple-element.98), channel_id=1, source_target_pairs={{0,10},{1,11},{2,8},{3,9},{4,14},{5,15},{6,12},{7,13},{8,2},{9,3},... | collective-permute-start | bytes 196616 | tf_op jit(solution)/shard_map/ppermute | solution.py:450
  19.6 17.6 %collective-permute-start.5 = (bf16[2,64,256]{2,1,0:T(8,128)(2,1)S(1)}, bf16[2,64,256]{2,1,0:T(8,128)(2,1)S(1)}, u32[]{:S(2)}, u32[]{:S(2)}) collective-permute-start(bf16[2,64,256]{2,1,0:T(8,128)(2,1)S(1)} %get-tuple-element.99), channel_id=1, source_target_pairs={{0,12},{1,13},{2,14},{3,15},{4,8},{5,9},{6,10},{7,11},{8,4},{9,5},... | collective-permute-start | bytes 196616 | tf_op jit(solution)/shard_map/ppermute | solution.py:450
  23.6 4.6 %copy-start.6 = (f32[256]{0:T(256)S(1)}, f32[256]{0:T(256)}, u32[]{:S(2)}) copy-start(f32[256]{0:T(256)} %param.17) | copy-start | bytes 3076
  23.6 13.6 %collective-permute-start.6 = (bf16[2,64,256]{2,1,0:T(8,128)(2,1)S(1)}, bf16[2,64,256]{2,1,0:T(8,128)(2,1)S(1)}, u32[]{:S(2)}, u32[]{:S(2)}) collective-permute-start(bf16[2,64,256]{2,1,0:T(8,128)(2,1)S(1)} %get-tuple-element.100), channel_id=1, source_target_pairs={{0,14},{1,15},{2,12},{3,13},{4,10},{5,11},{6,8},{7,9},{8,6},{9,7},... | collective-permute-start | bytes 196616 | tf_op jit(solution)/shard_map/ppermute | solution.py:450
  28.1 10.7 %copy-start = (bf16[1024,256]{1,0:T(8,128)(2,1)S(1)}, bf16[1024,256]{1,0:T(8,128)(2,1)}, u32[]{:S(2)}) copy-start(bf16[1024,256]{1,0:T(8,128)(2,1)} %refs_4_.1) | copy-start | bytes 1572868
  37.2 1.6 %collective-permute-start.7 = (bf16[8,64,256]{2,1,0:T(8,128)(2,1)S(1)}, bf16[8,64,256]{2,1,0:T(8,128)(2,1)S(1)}, u32[]{:S(2)}, u32[]{:S(2)}) collective-permute-start(bf16[8,64,256]{2,1,0:T(8,128)(2,1)S(1)} %get-tuple-element.115), channel_id=1, source_target_pairs={{0,1},{1,0},{2,3},{3,2},{4,5},{5,4},{6,7},{7,6},{8,9},{9,8},{10,11... | collective-permute-start | bytes 786440 | tf_op jit(solution)/shard_map/ppermute | solution.py:450
  41.4 2.0 %collective-permute-start.8 = (bf16[2,4,128,256]{3,2,1,0:T(8,128)(2,1)S(1)}, bf16[2,4,128,256]{3,2,1,0:T(8,128)(2,1)S(1)}, u32[]{:S(2)}, u32[]{:S(2)}) collective-permute-start(bf16[2,4,128,256]{3,2,1,0:T(8,128)(2,1)S(1)} %get-tuple-element.123), channel_id=1, source_target_pairs={{0,1},{1,0},{2,3},{3,2},{4,5},{5,4},{6,7},{7,6},{8,9},{9,8},{10,11... | collective-permute-start | bytes 1572872 | tf_op jit(solution)/shard_map/ppermute | solution.py:450
  43.4 8.4 %collective-permute-start.9 = (bf16[1,4,128,256]{3,2,1,0:T(8,128)(2,1)S(1)}, bf16[1,4,128,256]{3,2,1,0:T(8,128)(2,1)S(1)}, u32[]{:S(2)}, u32[]{:S(2)}) collective-permute-start(bf16[1,4,128,256]{3,2,1,0:T(8,128)(2,1)S(1)} %get-tuple-element.136), channel_id=1, source_target_pairs={{0,2},{1,3},{2,0},{3,1},{4,6},{5,7},{6,4},{7,5},{8,10},{9,11},{10,... | collective-permute-start | bytes 786440 | tf_op jit(solution)/shard_map/ppermute | solution.py:450
  48.6 8.2 %collective-permute-start.12 = (bf16[2,4,80,256]{3,2,1,0:T(8,128)(2,1)S(1)}, bf16[2,4,80,256]{3,2,1,0:T(8,128)(2,1)S(1)}, u32[]{:S(2)}, u32[]{:S(2)}) collective-permute-start(bf16[2,4,80,256]{3,2,1,0:T(8,128)(2,1)S(1)} %get-tuple-element.145), channel_id=1, source_target_pairs={{0,1},{1,0},{2,3},{3,2},{4,5},{5,4},{6,7},{7,6},{8,9},{9,8},{10,11... | collective-permute-start | bytes 983048 | tf_op jit(solution)/shard_map/ppermute | solution.py:450
  51.9 32.3 %all-to-all-start.1 = ((bf16[16,64,256]{2,1,0:T(8,128)(2,1)}), bf16[16,64,256]{2,1,0:T(8,128)(2,1)S(1)}, u32[]{:S(2)}, u32[]{:S(2)}) async-start(bf16[16,64,256]{2,1,0:T(8,128)(2,1)} %bitcast.3), calls=%async_computation.1 | async-start | bytes 1048576 | tf_op jit(solution)/shard_map/all_to_all | solution.py:520
  56.9 10.8 %collective-permute-start.13 = (bf16[1,4,80,256]{3,2,1,0:T(8,128)(2,1)S(1)}, bf16[1,4,80,256]{3,2,1,0:T(8,128)(2,1)S(1)}, u32[]{:S(2)}, u32[]{:S(2)}) collective-permute-start(bf16[1,4,80,256]{3,2,1,0:T(8,128)(2,1)S(1)} %get-tuple-element.147), channel_id=1, source_target_pairs={{0,2},{1,3},{2,0},{3,1},{4,6},{5,7},{6,4},{7,5},{8,10},{9,11},{10,... | collective-permute-start | bytes 491528 | tf_op jit(solution)/shard_map/ppermute | solution.py:450
  58.9 12.7 %collective-permute-start.10 = (bf16[2,128,256]{2,1,0:T(8,128)(2,1)S(1)}, bf16[2,128,256]{2,1,0:T(8,128)(2,1)S(1)}, u32[]{:S(2)}, u32[]{:S(2)}) collective-permute-start(bf16[2,128,256]{2,1,0:T(8,128)(2,1)S(1)} %get-tuple-element.141), channel_id=1, source_target_pairs={{0,4},{4,0},{8,12},{12,8},{1,5},{5,1},{9,13},{13,9},{2,6},{6,2},{1... | collective-permute-start | bytes 393224 | tf_op jit(solution)/shard_map/ppermute | solution.py:450
  67.8 6.5 %collective-permute-start.14 = (bf16[2,80,256]{2,1,0:T(8,128)(2,1)S(1)}, bf16[2,80,256]{2,1,0:T(8,128)(2,1)S(1)}, u32[]{:S(2)}, u32[]{:S(2)}) collective-permute-start(bf16[2,80,256]{2,1,0:T(8,128)(2,1)S(1)} %get-tuple-element.149), channel_id=1, source_target_pairs={{0,4},{4,0},{8,12},{12,8},{1,5},{5,1},{9,13},{13,9},{2,6},{6,2},{1... | collective-permute-start | bytes 245768 | tf_op jit(solution)/shard_map/ppermute | solution.py:450
  71.7 6.3 %collective-permute-start.11 = (bf16[1,128,256]{2,1,0:T(8,128)(2,1)S(1)}, bf16[1,128,256]{2,1,0:T(8,128)(2,1)S(1)}, u32[]{:S(2)}, u32[]{:S(2)}) collective-permute-start(bf16[1,128,256]{2,1,0:T(8,128)(2,1)S(1)} %get-tuple-element.143), channel_id=1, source_target_pairs={{0,8},{4,12},{8,0},{12,4},{1,9},{5,13},{9,1},{13,5},{2,10},{6,14},... | collective-permute-start | bytes 196616 | tf_op jit(solution)/shard_map/ppermute | solution.py:450
  74.2 10.0 %copy-start.8 = (s32[1,512]{1,0:T(1,128)S(1)}, s32[1,512]{1,0:T(1,128)}, u32[]{:S(2)}) copy-start(s32[1,512]{1,0:T(1,128)} %get-tuple-element.84.refs_0_) | copy-start | bytes 6148
  74.2 5.1 %collective-permute-start.15 = (bf16[1,80,256]{2,1,0:T(8,128)(2,1)S(1)}, bf16[1,80,256]{2,1,0:T(8,128)(2,1)S(1)}, u32[]{:S(2)}, u32[]{:S(2)}) collective-permute-start(bf16[1,80,256]{2,1,0:T(8,128)(2,1)S(1)} %get-tuple-element.151), channel_id=1, source_target_pairs={{0,8},{4,12},{8,0},{12,4},{1,9},{5,13},{9,1},{13,5},{2,10},{6,14},... | collective-permute-start | bytes 122888 | tf_op jit(solution)/shard_map/ppermute | solution.py:450
  79.4 4.7 %collective-permute-start.16 = (bf16[1,192,256]{2,1,0:T(8,128)(2,1)S(1)}, bf16[1,192,256]{2,1,0:T(8,128)(2,1)S(1)}, u32[]{:S(2)}, u32[]{:S(2)}) collective-permute-start(bf16[1,192,256]{2,1,0:T(8,128)(2,1)S(1)} %get-tuple-element.155), channel_id=1, source_target_pairs={{0,2},{1,3},{2,0},{3,1},{4,6},{5,7},{6,4},{7,5},{8,10},{9,11},{10,... | collective-permute-start | bytes 294920 | tf_op jit(solution)/shard_map/ppermute | solution.py:450
  84.1 1.5 %collective-permute-start.17 = (bf16[2,192,256]{2,1,0:T(8,128)(2,1)S(1)}, bf16[2,192,256]{2,1,0:T(8,128)(2,1)S(1)}, u32[]{:S(2)}, u32[]{:S(2)}) collective-permute-start(bf16[2,192,256]{2,1,0:T(8,128)(2,1)S(1)} %constant_dynamic-update-slice_fusion.refs_1_), channel_id=1, source_target_pairs={{0,1},{1,0},{2,3},{3,2},{4,5},{5,4},{6,7},{7,6},{8,9},{9,8},{10,11... | collective-permute-start | bytes 589832 | tf_op jit(solution)/shard_map/ppermute | solution.py:450
  (5 other events, 18.8 us)

commit v2 on v1

--- a/solution.py
+++ b/solution.py
@@ -13,6 +13,7 @@
 HEAD_DIM = 32
 GROUP = 128
 META = 16
+GAINS = 8
 
 EPSILON = 1e-06
 GELU_COEF = math.sqrt(2.0 / math.pi)
@@ -387,7 +388,7 @@
         grad_qkv = mm_nt(normed_one, grad_rows[col * width : (col + 1) * width])
         place_blocks(blocks_ref, grad_qkv, (1 + col) * step, leaf_size, sample_size)
     place_blocks(blocks_ref, grad_out_ref[...], 0, leaf_size, sample_size)
-    row = iota((META, width), 0)
+    row = iota((GAINS, width), 0)
     gains = jnp.where(row == 0, gain_one, jnp.where(row == 1, gain_two_ref[...], 0.0))
     for sample in range(sample_size):
         for leaf in range(leaf_size):
@@ -409,19 +410,24 @@
             ref[high] = (keep_ref[at] + got_ref[at].astype(F32)).astype(ref.dtype)
 
 
-def finish_kernel(pairs, *refs):
-    ins, (low_ref, gains_ref) = refs[: 2 * pairs], refs[2 * pairs :]
+def join_kernel(bit, *refs):
+    ins, (keep_out_ref, send_out_ref) = refs[:-2], refs[-2:]
+    mine = lax.rem(lax.div(lax.axis_index("leaf"), bit), 2)
     start = 0
-    for pair in range(pairs):
-        total = ins[2 * pair][0] + ins[2 * pair + 1][0].astype(F32)
-        if pair == pairs - 1:
-            gains_ref[...] = total[-META:]
-            total = total[:-META]
-        low_ref[0, start : start + total.shape[0], :] = total.astype(BF16)
-        start += total.shape[0]
-
-
-def assemble_kernel(scale, offsets, gains_ref, mine_ref, mate_ref, up_ref, down_ref, out_ref, qkv_ref, gain_out_ref):
+    for keep_ref, got_ref in zip(ins[::2], ins[1::2]):
+        rows = pl.ds(start, keep_ref.shape[1])
+        for ref, at in ((keep_out_ref, mine), (send_out_ref, 1 - mine)):
+            ref[rows, :] = (keep_ref[at] + got_ref[at].astype(F32)).astype(ref.dtype)
+        start += keep_ref.shape[1]
+
+
+def finish_kernel(keep_ref, got_ref, low_ref, gains_ref):
+    total = keep_ref[...] + got_ref[...].astype(F32)
+    gains_ref[...] = total[-GAINS:]
+    low_ref[0] = total[:-GAINS].astype(BF16)
+
+
+def assemble_kernel(scale, offsets, mine_ref, mate_ref, up_ref, down_ref, out_ref, qkv_ref):
     size = 2 * len(offsets)
     width = mine_ref.shape[2]
     up_rows, down_rows, out_rows = up_ref.shape[0], down_ref.shape[0] // size, out_ref.shape[0] // size
@@ -443,7 +449,6 @@
             for col in range(3):
                 qkv_ref[block(source, out_rows), col * width : (col + 1) * width] = part[at : at + out_rows]
                 at += out_rows
-    gain_out_ref[...] = gains_ref[...] * scale
 
 
 def permute(value, axis, size, bit):
@@ -453,17 +458,6 @@
 def halve(keep, got, axis, bit, name):
     shape = (keep.shape[0] // 2,) + keep.shape[1:]
     return call(functools.partial(halve_kernel, axis, bit), [(shape, F32), (shape, BF16)], name, 0.5, keep, got)
-
-
-def halve_leaf(keep, got, name):
-    leaf_size = lax.axis_size("leaf")
-    keep, got = keep[0], got[0]
-    bit = 1
-    while bit < leaf_size:
-        keep, leaving = halve(keep, got, "leaf", bit, name)
-        got = permute(leaving, "leaf", leaf_size, bit)
-        bit *= 2
-    return keep, got
 
 
 def call(kernel, outs, name, micros, *args, scratch=(), hbm_in=False, hbm_out=False, raw_in=0, raw_out=0, blocked=False, limit=16):
@@ -533,7 +527,7 @@
     slots = peers * cap
     balls = rows // BALL
     direct = cap % 16 == 0
-    paired = leaf_size & (leaf_size - 1) == 0 and sample_size & (sample_size - 1) == 0 and sample_size > 1
+    paired = leaf_size & (leaf_size - 1) == 0 and sample_size & (sample_size - 1) == 0 and min(leaf_size, sample_size) > 1
     arranged = paired and width % (16 * peers) == 0 and hidden_width == sample_size * width and leaf_size <= 8
     inv_root = 1.0 / math.sqrt(rows * peers)
 
@@ -594,7 +588,7 @@
     if arranged:
         halved = (sample_size // 2, leaf_size)
         mlp_rows = width // leaf_size + hidden_width // peers
-        qkv_rows = 4 * width // peers + META
+        qkv_rows = 4 * width // peers + GAINS
         mlp_mats = [(halved + (mlp_rows, width), F32), (halved + (mlp_rows, width), BF16)]
         qkv_mats = [(halved + (qkv_rows, width), F32), (halved + (qkv_rows, width), BF16)]
         mlp_scratch = [pltpu.VMEM((sample_size, leaf_size, mlp_rows, width), F32)]
@@ -629,11 +623,9 @@
         w_qkv, gain_attn_col, target_col, gain_two, grad_out, *probs,
         scratch=qkv_scratch + [pltpu.VMEM((3 * width, rows), BF16)],
     )
-    if arranged:
-        back, got_mlp = lax.optimization_barrier((back, got_mlp))
-    returned = exchange(back, axes, peers)
-    (grad_points,) = call(unpack_kernel, [((rows, width), BF16)], "unpack", 1, slot, returned, blocked=True)
     if not arranged:
+        returned = exchange(back, axes, peers)
+        (grad_points,) = call(unpack_kernel, [((rows, width), BF16)], "unpack", 1, slot, returned, blocked=True)
         up_sum, down_sum, out_sum = reduce_mats([*mlp_grads, grad_out])
         qkv_sum, gain_sum = reduce_mats([qkv_grads[0]], jnp.concatenate([qkv_grads[1], gain_two], axis=0))
         return (
@@ -642,15 +634,32 @@
         )
     keep_qkv, send_qkv = qkv_grads
     got_qkv = permute(send_qkv, "sample", sample_size, 1)
+    got_qkv = lax.optimization_barrier((got_qkv, got_mlp))[0]
     bit = 2
     while bit < sample_size:
         keep_qkv, send_qkv = halve(keep_qkv, got_qkv, "sample", bit, "halve_qkv")
         got_qkv = permute(send_qkv, "sample", sample_size, bit)
         bit *= 2
+    keep_mlp, got_mlp, keep_qkv, got_qkv = keep_mlp[0], got_mlp[0], keep_qkv[0], got_qkv[0]
+    bit = 1
+    while bit * 2 < leaf_size:
+        keep_mlp, leaving = halve(keep_mlp, got_mlp, "leaf", bit, "leaf_mlp")
+        if bit == 1:
+            back = lax.optimization_barrier((back, leaving, send_qkv))[0]
+        got_mlp = permute(leaving, "leaf", leaf_size, bit)
+        keep_qkv, leaving = halve(keep_qkv, got_qkv, "leaf", bit, "leaf_qkv")
+        got_qkv = permute(leaving, "leaf", leaf_size, bit)
+        bit *= 2
+    joined = (mlp_rows + qkv_rows, width)
+    keep, leaving = call(
+        functools.partial(join_kernel, bit), [(joined, F32), (joined, BF16)], "leaf_last", 0.5,
+        keep_mlp, got_mlp, keep_qkv, got_qkv,
+    )
+    got = permute(leaving, "leaf", leaf_size, bit)
+    returned = exchange(back, axes, peers)
+    (grad_points,) = call(unpack_kernel, [((rows, width), BF16)], "unpack", 1, slot, returned, blocked=True)
     low, gains = call(
-        functools.partial(finish_kernel, 2),
-        [((1, mlp_rows + qkv_rows - META, width), BF16), ((META, width), F32)], "finish", 0.5,
-        *halve_leaf(keep_mlp, got_mlp, "leaf_mlp"), *halve_leaf(keep_qkv, got_qkv, "leaf_qkv"),
+        finish_kernel, [((1, mlp_rows + qkv_rows - GAINS, width), BF16), ((GAINS, width), F32)], "finish", 0.5, keep, got
     )
     offsets = [0]
     bit = sample_size // 2
@@ -659,18 +668,19 @@
         offsets += [offset ^ bit for offset in offsets]
         bit //= 2
     mate = permute(low, "sample", sample_size, 1)
-    grad_points, gains = lax.optimization_barrier((grad_points, gains))
     share = width // leaf_size
-    up_sum, down_sum, out_sum, qkv_sum, gain_sum = call(
+    gains = lax.dynamic_slice(gains, (0, lax.axis_index("leaf") * share), (2, share)) * inv_root
+    gain_one, gain_two = gains[0], gains[1]
+    grad_points, gain_one, gain_two, mate = lax.optimization_barrier((grad_points, gain_one, gain_two, mate))
+    up_sum, down_sum, out_sum, qkv_sum = call(
         functools.partial(assemble_kernel, inv_root, offsets),
         [
             ((share, hidden_width), F32), ((hidden_width // leaf_size, width), F32), ((share, width), F32),
-            ((share, 3 * width), F32), ((META, width), F32),
+            ((share, 3 * width), F32),
         ],
-        "assemble", 1, gains, low, mate, blocked=True,
-    )
-    gains = lax.dynamic_slice(gain_sum, (0, lax.axis_index("leaf") * share), (2, share))
-    return (grad_points, qkv_sum, out_sum, up_sum, down_sum, gains[0], gains[1])
+        "assemble", 1, low, mate, blocked=True,
+    )
+    return (grad_points, qkv_sum, out_sum, up_sum, down_sum, gain_one, gain_two)
 
 
 def reduce_mats(mats, gains=None):

time: 87.5 us -> 94.2 us (1.077)
  waiting for transfers between devices: 27.8 us -> 37.1 us
  starting transfers between devices: 38.5 us -> 35.8 us
    ppermute x18 -> x17, waiting for transfers between devices: 27.8 us -> 37.1 us  [permute(): return lax.ppermute(value, axis, [(i, i ^ bit) for i in range(size)])]
    ppermute x18 -> x17, starting transfers between devices: 26.2 us -> 23.2 us  [permute(): return lax.ppermute(value, axis, [(i, i ^ bit) for i in range(size)])]
    pallas_call x17 -> x16, Pallas kernels: 18.6 us -> 18.6 us  [call(): pl.pallas_call(body, out_shape=[jax.ShapeDtypeStruct(shape, dtype) for sh...]
  transfers between devices with their start and end apart: 20 -> 19, of which waited for: 12 -> 10; matrix products, arithmetic and copies ran while one was open for 0% -> 1% of each run, Pallas kernels for 14% -> 8%
where the time goes in v2:
time: 94.2 us; the launch traced here: 93.8 us
  waiting for transfers between devices  37.1 us (39%)
  starting transfers between devices  35.8 us (38%)
  Pallas kernels  18.6 us (20%)
  local copies, waits for them, and re-layouts  1.25 us (1%)
    ppermute x17, waiting for transfers between devices, permute(): return lax.ppermute(value, axis, [(i, i ^ bit) for i in range(size)])  37.1 us
    ppermute x17, starting transfers between devices, permute(): return lax.ppermute(value, axis, [(i, i ^ bit) for i in range(size)])  23.2 us
    pallas_call x16, Pallas kernels, call(): pl.pallas_call(body, out_shape=[jax.ShapeDtypeStruct(shape, dtype) for sh...  18.6 us
    all_to_all x2, starting transfers between devices, exchange(): lax.all_to_all(flat.reshape((peers, -1) + flat.shape[1:]), axes, split_ax...  12.6 us
  transfers between devices with their start and end apart: 19, of which 10 were waited for; matrix products, arithmetic and copies ran while one was open for 1% of the time, Pallas kernels for 8%

profile of v2, /device:TPU:0, one launch (start us, length us, event | category | flops | bytes accessed | tf_op | source)
XLA Modules:
  0.0 93.8 jit_solution(14939581830589630206)
XLA Ops:
  0.6 2.6 %pack_points.1 = (s32[1,512]{1,0:T(1,128)}, bf16[16,144,128]{2,1,0:T(8,128)(2,1)}) custom-call(s32[1,512]{1,0:T(1,128)} %bitcast.20, bf16[512,256]{1,0:T(8,128)(2,1)} %refs_1_.3), custom_call_target="tpu_custom_call" | custom-call | flops 2200000000 | bytes 856064 | tf_op jit(solution)/shard_map/pack_points/pallas_call | solution.py:501
  3.2 7.4 %all-to-all-start = ((bf16[16,144,128]{2,1,0:T(8,128)(2,1)}), bf16[16,144,128]{2,1,0:T(8,128)(2,1)S(1)}, u32[]{:S(2)}, u32[]{:S(2)}) async-start(bf16[16,144,128]{2,1,0:T(8,128)(2,1)} %get-tuple-element.86), calls=%async_computation | async-start | bytes 1179648 | tf_op jit(solution)/shard_map/all_to_all | solution.py:514
  11.8 2.0 %collective-permute-start = (bf16[2,64,256]{2,1,0:T(8,128)(2,1)S(1)}, bf16[2,64,256]{2,1,0:T(8,128)(2,1)S(1)}, u32[]{:S(2)}, u32[]{:S(2)}) collective-permute-start(bf16[2,64,256]{2,1,0:T(8,128)(2,1)S(1)} %get-tuple-element.84), channel_id=1, source_target_pairs={{0,2},{1,3},{2,0},{3,1},{4,6},{5,7},{6,4},{7,5},{8,10},{9,11},{10,... | collective-permute-start | bytes 196616 | tf_op jit(solution)/shard_map/ppermute | solution.py:455
  13.8 1.5 %collective-permute-start.1 = (bf16[2,64,256]{2,1,0:T(8,128)(2,1)S(1)}, bf16[2,64,256]{2,1,0:T(8,128)(2,1)S(1)}, u32[]{:S(2)}, u32[]{:S(2)}) collective-permute-start(bf16[2,64,256]{2,1,0:T(8,128)(2,1)S(1)} %get-tuple-element.85), channel_id=1, source_target_pairs={{0,4},{1,5},{2,6},{3,7},{4,0},{5,1},{6,2},{7,3},{8,12},{9,13},{10,... | collective-permute-start | bytes 196616 | tf_op jit(solution)/shard_map/ppermute | solution.py:455
  15.3 2.8 %collective-permute-start.3 = (bf16[2,64,256]{2,1,0:T(8,128)(2,1)S(1)}, bf16[2,64,256]{2,1,0:T(8,128)(2,1)S(1)}, u32[]{:S(2)}, u32[]{:S(2)}) collective-permute-start(bf16[2,64,256]{2,1,0:T(8,128)(2,1)S(1)} %get-tuple-element.96), channel_id=1, source_target_pairs={{0,8},{1,9},{2,10},{3,11},{4,12},{5,13},{6,14},{7,15},{8,0},{9,1},... | collective-permute-start | bytes 196616 | tf_op jit(solution)/shard_map/ppermute | solution.py:455
  18.1 1.5 %collective-permute-start.4 = (bf16[2,64,256]{2,1,0:T(8,128)(2,1)S(1)}, bf16[2,64,256]{2,1,0:T(8,128)(2,1)S(1)}, u32[]{:S(2)}, u32[]{:S(2)}) collective-permute-start(bf16[2,64,256]{2,1,0:T(8,128)(2,1)S(1)} %get-tuple-element.97), channel_id=1, source_target_pairs={{0,10},{1,11},{2,8},{3,9},{4,14},{5,15},{6,12},{7,13},{8,2},{9,3},... | collective-permute-start | bytes 196616 | tf_op jit(solution)/shard_map/ppermute | solution.py:455
  19.6 3.3 %collective-permute-start.5 = (bf16[2,64,256]{2,1,0:T(8,128)(2,1)S(1)}, bf16[2,64,256]{2,1,0:T(8,128)(2,1)S(1)}, u32[]{:S(2)}, u32[]{:S(2)}) collective-permute-start(bf16[2,64,256]{2,1,0:T(8,128)(2,1)S(1)} %get-tuple-element.98), channel_id=1, source_target_pairs={{0,12},{1,13},{2,14},{3,15},{4,8},{5,9},{6,10},{7,11},{8,4},{9,5},... | collective-permute-start | bytes 196616 | tf_op jit(solution)/shard_map/ppermute | solution.py:455
  23.6 4.0 %collective-permute-start.6 = (bf16[2,64,256]{2,1,0:T(8,128)(2,1)S(1)}, bf16[2,64,256]{2,1,0:T(8,128)(2,1)S(1)}, u32[]{:S(2)}, u32[]{:S(2)}) collective-permute-start(bf16[2,64,256]{2,1,0:T(8,128)(2,1)S(1)} %get-tuple-element.99), channel_id=1, source_target_pairs={{0,14},{1,15},{2,12},{3,13},{4,10},{5,11},{6,8},{7,9},{8,6},{9,7},... | collective-permute-start | bytes 196616 | tf_op jit(solution)/shard_map/ppermute | solution.py:455
  28.1 4.5 %forward.1 = (bf16[768,512]{1,0:T(8,128)(2,1)S(1)}, bf16[512,512]{1,0:T(8,128)(2,1)S(1)}, f32[8,512]{1,0:T(8,128)S(1)}, f32[256,512]{1,0:T(8,128)S(1)}, bf16[256...) custom-call(f32[256,512]{1,0:T(8,128)S(1)} %get-tuple-element.88.ref, ...), custom_call_target="tpu_custom_call" | custom-call | flops 7699999744 | bytes 12339200 | tf_op jit(solution)/shard_map/forward/pallas_call | solution.py:501
  32.7 2.1 %collective-permute-done.3.refs_4_ = bf16[2,64,256]{2,1,0:T(8,128)(2,1)S(1)} collective-permute-done((bf16[2,64,256]{2,1,0:T(8,128)(2,1)S(1)}, bf16[2,64,256]{2,1,0:T(8,128)(2,1)S(1)}, u32[]{:S(2)}, u32[]{:S(2)}) %collective-permute-start.3) | collective-permute-done | bytes 65568 | tf_op jit(solution)/shard_map/ppermute | solution.py:455
  34.8 2.3 %collective-permute-done.4.refs_5_ = bf16[2,64,256]{2,1,0:T(8,128)(2,1)S(1)} collective-permute-done((bf16[2,64,256]{2,1,0:T(8,128)(2,1)S(1)}, bf16[2,64,256]{2,1,0:T(8,128)(2,1)S(1)}, u32[]{:S(2)}, u32[]{:S(2)}) %collective-permute-start.4) | collective-permute-done | bytes 65568 | tf_op jit(solution)/shard_map/ppermute | solution.py:455
  37.3 1.5 %collective-permute-done.7.refs_6_ = bf16[8,64,256]{2,1,0:T(8,128)(2,1)S(1)} collective-permute-done((bf16[8,64,256]{2,1,0:T(8,128)(2,1)S(1)}, bf16[8,64,256]{2,1,0:T(8,128)(2,1)S(1)}, u32[]{:S(2)}, u32[]{:S(2)}) %collective-permute-start.7) | collective-permute-done | bytes 262176 | tf_op jit(solution)/shard_map/ppermute | solution.py:455
  38.8 2.6 %mlp_weights.1 = (bf16[1024,512]{1,0:T(8,128)(2,1)S(1)}, f32[256,512]{1,0:T(8,128)S(1)}, f32[2,4,128,256]{3,2,1,0:T(8,128)S(1)}, bf16[2,4,128,256]{3,2,1,0:T(8,128)(2,1)S(1)}) custom-call(s32[1,1024]{1,0:T(1,128)S(1)} %get-tuple-element.101.refs_0_, bf16[1024,512]{1,0:T(8,128)(2,1)S(1)} %get-tuple-element.102.refs_1_, ...), custom_call_target="tpu_custom_call" | custom-call | flops 2750000128 | bytes 7606272 | tf_op jit(solution)/shard_map/mlp_weights/pallas_call | solution.py:501
  43.5 4.6 %attention_backward.1 = (bf16[1024,256]{1,0:T(8,128)(2,1)}, f32[2,4,72,256]{3,2,1,0:T(8,128)S(1)}, bf16[2,4,72,256]{3,2,1,0:T(8,128)(2,1)S(1)}) custom-call(bf16[768,512]{1,0:T(8,128)(2,1)S(1)} %get-tuple-element.89.refs_0_, bf16[512,512]{1,0:T(8,128)(2,1)S(1)} %get-tuple-element.90.refs_1_, f32[8,512]{1,0:T(8,128)S(1)} %get-tuple-element.100.refs_3_.refs_2_, ...), custom_call_target="tpu_custom_call" | custom-call | flops 6600000000 | bytes 9815040 | tf_op jit(solution)/shard_map/attention_backward/pallas_call | solution.py:501
  48.7 8.0 %collective-permute-done.9 = bf16[1,4,128,256]{3,2,1,0:T(8,128)(2,1)S(1)} collective-permute-done((bf16[1,4,128,256]{3,2,1,0:T(8,128)(2,1)S(1)}, bf16[1,4,128,256]{3,2,1,0:T(8,128)(2,1)S(1)}, u32[]{:S(2)}, u32[]{:S(2)}) %collective-permute-start.9) | collective-permute-done | bytes 262176 | tf_op jit(solution)/shard_map/ppermute | solution.py:455
  57.5 5.2 %all-to-all-start.1 = ((bf16[16,64,256]{2,1,0:T(8,128)(2,1)}), bf16[16,64,256]{2,1,0:T(8,128)(2,1)S(1)}, u32[]{:S(2)}, u32[]{:S(2)}) async-start(bf16[16,64,256]{2,1,0:T(8,128)(2,1)} %bitcast.5), calls=%async_computation.1 | async-start | bytes 1048576 | tf_op jit(solution)/shard_map/all_to_all | solution.py:514
  62.7 1.9 %collective-permute-start.11 = (bf16[2,128,256]{2,1,0:T(8,128)(2,1)S(1)}, bf16[2,128,256]{2,1,0:T(8,128)(2,1)S(1)}, u32[]{:S(2)}, u32[]{:S(2)}) collective-permute-start(bf16[2,128,256]{2,1,0:T(8,128)(2,1)S(1)} %get-tuple-element.137), channel_id=1, source_target_pairs={{0,4},{4,0},{8,12},{12,8},{1,5},{5,1},{9,13},{13,9},{2,6},{6,2},{1... | collective-permute-start | bytes 393224 | tf_op jit(solution)/shard_map/ppermute | solution.py:455
  65.2 12.4 %collective-permute-done.11.refs_1_ = bf16[2,128,256]{2,1,0:T(8,128)(2,1)S(1)} collective-permute-done((bf16[2,128,256]{2,1,0:T(8,128)(2,1)S(1)}, bf16[2,128,256]{2,1,0:T(8,128)(2,1)S(1)}, u32[]{:S(2)}, u32[]{:S(2)}) %collective-permute-start.11) | collective-permute-done | bytes 131104 | tf_op jit(solution)/shard_map/ppermute | solution.py:455
  77.5 1.1 %collective-permute-done.13.refs_3_ = bf16[2,72,256]{2,1,0:T(8,128)(2,1)S(1)} collective-permute-done((bf16[2,72,256]{2,1,0:T(8,128)(2,1)S(1)}, bf16[2,72,256]{2,1,0:T(8,128)(2,1)S(1)}, u32[]{:S(2)}, u32[]{:S(2)}) %collective-permute-start.13) | collective-permute-done | bytes 73760 | tf_op jit(solution)/shard_map/ppermute | solution.py:455
  78.7 2.5 %collective-permute-start.14 = (bf16[200,256]{1,0:T(8,128)(2,1)S(1)}, bf16[200,256]{1,0:T(8,128)(2,1)S(1)}, u32[]{:S(2)}, u32[]{:S(2)}) collective-permute-start(bf16[200,256]{1,0:T(8,128)(2,1)S(1)} %get-tuple-element.148), channel_id=1, source_target_pairs={{0,8},{4,12},{8,0},{12,4},{1,9},{5,13},{9,1},{13,5},{2,10},{6,14},... | collective-permute-start | bytes 307208 | tf_op jit(solution)/shard_map/ppermute | solution.py:455
  81.2 5.0 %collective-permute-done.14.refs_1_ = bf16[200,256]{1,0:T(8,128)(2,1)S(1)} collective-permute-done((bf16[200,256]{1,0:T(8,128)(2,1)S(1)}, bf16[200,256]{1,0:T(8,128)(2,1)S(1)}, u32[]{:S(2)}, u32[]{:S(2)}) %collective-permute-start.14) | collective-permute-done | bytes 102432 | tf_op jit(solution)/shard_map/ppermute | solution.py:455
  86.3 1.5 %collective-permute-start.15 = (bf16[1,192,256]{2,1,0:T(8,128)(2,1)S(1)}, bf16[1,192,256]{2,1,0:T(8,128)(2,1)S(1)}, u32[]{:S(2)}, u32[]{:S(2)}) collective-permute-start(bf16[1,192,256]{2,1,0:T(8,128)(2,1)S(1)} %get-tuple-element.150), channel_id=1, source_target_pairs={{0,2},{1,3},{2,0},{3,1},{4,6},{5,7},{6,4},{7,5},{8,10},{9,11},{10,... | collective-permute-start | bytes 294920 | tf_op jit(solution)/shard_map/ppermute | solution.py:455
  87.9 3.1 %collective-permute-done.15 = bf16[1,192,256]{2,1,0:T(8,128)(2,1)S(1)} collective-permute-done((bf16[1,192,256]{2,1,0:T(8,128)(2,1)S(1)}, bf16[1,192,256]{2,1,0:T(8,128)(2,1)S(1)}, u32[]{:S(2)}, u32[]{:S(2)}) %collective-permute-start.15) | collective-permute-done | bytes 98336 | tf_op jit(solution)/shard_map/ppermute | solution.py:455
  91.6 1.2 %unpack.1 = bf16[512,256]{1,0:T(8,128)(2,1)} custom-call(s32[1,512]{1,0:T(1,128)S(1)} %copy-done.8, bf16[1024,256]{1,0:T(8,128)(2,1)S(1)} %bitcast.13), custom_call_target="tpu_custom_call" | custom-call | flops 1100000000 | bytes 788480 | tf_op jit(solution)/shard_map/unpack/pallas_call | solution.py:501
  (52 shorter events, 8.3 us)
Async XLA Ops:
  0.6 10.0 %copy-start.3 = (bf16[512,256]{1,0:T(8,128)(2,1)S(1)}, bf16[512,256]{1,0:T(8,128)(2,1)}, u32[]{:S(2)}) copy-start(bf16[512,256]{1,0:T(8,128)(2,1)} %refs_1_.4) | copy-start | bytes 786436
  3.2 24.3 %all-to-all-start = ((bf16[16,144,128]{2,1,0:T(8,128)(2,1)}), bf16[16,144,128]{2,1,0:T(8,128)(2,1)S(1)}, u32[]{:S(2)}, u32[]{:S(2)}) async-start(bf16[16,144,128]{2,1,0:T(8,128)(2,1)} %get-tuple-element.86), calls=%async_computation | async-start | bytes 1179648 | tf_op jit(solution)/shard_map/all_to_all | solution.py:514
  11.8 7.8 %collective-permute-start = (bf16[2,64,256]{2,1,0:T(8,128)(2,1)S(1)}, bf16[2,64,256]{2,1,0:T(8,128)(2,1)S(1)}, u32[]{:S(2)}, u32[]{:S(2)}) collective-permute-start(bf16[2,64,256]{2,1,0:T(8,128)(2,1)S(1)} %get-tuple-element.84), channel_id=1, source_target_pairs={{0,2},{1,3},{2,0},{3,1},{4,6},{5,7},{6,4},{7,5},{8,10},{9,11},{10,... | collective-permute-start | bytes 196616 | tf_op jit(solution)/shard_map/ppermute | solution.py:455
  13.8 9.8 %collective-permute-start.1 = (bf16[2,64,256]{2,1,0:T(8,128)(2,1)S(1)}, bf16[2,64,256]{2,1,0:T(8,128)(2,1)S(1)}, u32[]{:S(2)}, u32[]{:S(2)}) collective-permute-start(bf16[2,64,256]{2,1,0:T(8,128)(2,1)S(1)} %get-tuple-element.85), channel_id=1, source_target_pairs={{0,4},{1,5},{2,6},{3,7},{4,0},{5,1},{6,2},{7,3},{8,12},{9,13},{10,... | collective-permute-start | bytes 196616 | tf_op jit(solution)/shard_map/ppermute | solution.py:455
  15.2 17.5 %collective-permute-start.2 = (bf16[2,64,256]{2,1,0:T(8,128)(2,1)S(1)}, bf16[2,64,256]{2,1,0:T(8,128)(2,1)S(1)}, u32[]{:S(2)}, u32[]{:S(2)}) collective-permute-start(bf16[2,64,256]{2,1,0:T(8,128)(2,1)S(1)} %get-tuple-element.95), channel_id=1, source_target_pairs={{0,6},{1,7},{2,4},{3,5},{4,2},{5,3},{6,0},{7,1},{8,14},{9,15},{10,... | collective-permute-start | bytes 196616 | tf_op jit(solution)/shard_map/ppermute | solution.py:455
  15.3 19.5 %collective-permute-start.3 = (bf16[2,64,256]{2,1,0:T(8,128)(2,1)S(1)}, bf16[2,64,256]{2,1,0:T(8,128)(2,1)S(1)}, u32[]{:S(2)}, u32[]{:S(2)}) collective-permute-start(bf16[2,64,256]{2,1,0:T(8,128)(2,1)S(1)} %get-tuple-element.96), channel_id=1, source_target_pairs={{0,8},{1,9},{2,10},{3,11},{4,12},{5,13},{6,14},{7,15},{8,0},{9,1},... | collective-permute-start | bytes 196616 | tf_op jit(solution)/shard_map/ppermute | solution.py:455
  18.1 19.0 %collective-permute-start.4 = (bf16[2,64,256]{2,1,0:T(8,128)(2,1)S(1)}, bf16[2,64,256]{2,1,0:T(8,128)(2,1)S(1)}, u32[]{:S(2)}, u32[]{:S(2)}) collective-permute-start(bf16[2,64,256]{2,1,0:T(8,128)(2,1)S(1)} %get-tuple-element.97), channel_id=1, source_target_pairs={{0,10},{1,11},{2,8},{3,9},{4,14},{5,15},{6,12},{7,13},{8,2},{9,3},... | collective-permute-start | bytes 196616 | tf_op jit(solution)/shard_map/ppermute | solution.py:455
  19.6 17.5 %collective-permute-start.5 = (bf16[2,64,256]{2,1,0:T(8,128)(2,1)S(1)}, bf16[2,64,256]{2,1,0:T(8,128)(2,1)S(1)}, u32[]{:S(2)}, u32[]{:S(2)}) collective-permute-start(bf16[2,64,256]{2,1,0:T(8,128)(2,1)S(1)} %get-tuple-element.98), channel_id=1, source_target_pairs={{0,12},{1,13},{2,14},{3,15},{4,8},{5,9},{6,10},{7,11},{8,4},{9,5},... | collective-permute-start | bytes 196616 | tf_op jit(solution)/shard_map/ppermute | solution.py:455
  23.6 4.5 %copy-start.5 = (f32[256]{0:T(256)S(1)}, f32[256]{0:T(256)}, u32[]{:S(2)}) copy-start(f32[256]{0:T(256)} %param.16) | copy-start | bytes 3076
  23.6 4.6 %copy-start.6 = (f32[256]{0:T(256)S(1)}, f32[256]{0:T(256)}, u32[]{:S(2)}) copy-start(f32[256]{0:T(256)} %param.17) | copy-start | bytes 3076
  23.6 13.6 %collective-permute-start.6 = (bf16[2,64,256]{2,1,0:T(8,128)(2,1)S(1)}, bf16[2,64,256]{2,1,0:T(8,128)(2,1)S(1)}, u32[]{:S(2)}, u32[]{:S(2)}) collective-permute-start(bf16[2,64,256]{2,1,0:T(8,128)(2,1)S(1)} %get-tuple-element.99), channel_id=1, source_target_pairs={{0,14},{1,15},{2,12},{3,13},{4,10},{5,11},{6,8},{7,9},{8,6},{9,7},... | collective-permute-start | bytes 196616 | tf_op jit(solution)/shard_map/ppermute | solution.py:455
  28.1 10.7 %copy-start = (bf16[1024,256]{1,0:T(8,128)(2,1)S(1)}, bf16[1024,256]{1,0:T(8,128)(2,1)}, u32[]{:S(2)}) copy-start(bf16[1024,256]{1,0:T(8,128)(2,1)} %refs_4_.1) | copy-start | bytes 1572868
  37.2 1.6 %collective-permute-start.7 = (bf16[8,64,256]{2,1,0:T(8,128)(2,1)S(1)}, bf16[8,64,256]{2,1,0:T(8,128)(2,1)S(1)}, u32[]{:S(2)}, u32[]{:S(2)}) collective-permute-start(bf16[8,64,256]{2,1,0:T(8,128)(2,1)S(1)} %get-tuple-element.114), channel_id=1, source_target_pairs={{0,1},{1,0},{2,3},{3,2},{4,5},{5,4},{6,7},{7,6},{8,9},{9,8},{10,11... | collective-permute-start | bytes 786440 | tf_op jit(solution)/shard_map/ppermute | solution.py:455
  41.4 2.0 %collective-permute-start.8 = (bf16[2,4,128,256]{3,2,1,0:T(8,128)(2,1)S(1)}, bf16[2,4,128,256]{3,2,1,0:T(8,128)(2,1)S(1)}, u32[]{:S(2)}, u32[]{:S(2)}) collective-permute-start(bf16[2,4,128,256]{3,2,1,0:T(8,128)(2,1)S(1)} %get-tuple-element.122), channel_id=1, source_target_pairs={{0,1},{1,0},{2,3},{3,2},{4,5},{5,4},{6,7},{7,6},{8,9},{9,8},{10,11... | collective-permute-start | bytes 1572872 | tf_op jit(solution)/shard_map/ppermute | solution.py:455
  48.0 8.7 %collective-permute-start.10 = (bf16[2,4,72,256]{3,2,1,0:T(8,128)(2,1)S(1)}, bf16[2,4,72,256]{3,2,1,0:T(8,128)(2,1)S(1)}, u32[]{:S(2)}, u32[]{:S(2)}) collective-permute-start(bf16[2,4,72,256]{3,2,1,0:T(8,128)(2,1)S(1)} %get-tuple-element.139), channel_id=1, source_target_pairs={{0,1},{1,0},{2,3},{3,2},{4,5},{5,4},{6,7},{7,6},{8,9},{9,8},{10,11... | collective-permute-start | bytes 884744 | tf_op jit(solution)/shard_map/ppermute | solution.py:455
  48.2 8.5 %collective-permute-start.9 = (bf16[1,4,128,256]{3,2,1,0:T(8,128)(2,1)S(1)}, bf16[1,4,128,256]{3,2,1,0:T(8,128)(2,1)S(1)}, u32[]{:S(2)}, u32[]{:S(2)}) collective-permute-start(bf16[1,4,128,256]{3,2,1,0:T(8,128)(2,1)S(1)} %get-tuple-element.136), channel_id=1, source_target_pairs={{0,2},{1,3},{2,0},{3,1},{4,6},{5,7},{6,4},{7,5},{8,10},{9,11},{10,... | collective-permute-start | bytes 786440 | tf_op jit(solution)/shard_map/ppermute | solution.py:455
  56.8 7.8 %collective-permute-start.12 = (bf16[1,4,72,256]{3,2,1,0:T(8,128)(2,1)S(1)}, bf16[1,4,72,256]{3,2,1,0:T(8,128)(2,1)S(1)}, u32[]{:S(2)}, u32[]{:S(2)}) collective-permute-start(bf16[1,4,72,256]{3,2,1,0:T(8,128)(2,1)S(1)} %get-tuple-element.141), channel_id=1, source_target_pairs={{0,2},{1,3},{2,0},{3,1},{4,6},{5,7},{6,4},{7,5},{8,10},{9,11},{10,... | collective-permute-start | bytes 442376 | tf_op jit(solution)/shard_map/ppermute | solution.py:455
  57.5 34.1 %all-to-all-start.1 = ((bf16[16,64,256]{2,1,0:T(8,128)(2,1)}), bf16[16,64,256]{2,1,0:T(8,128)(2,1)S(1)}, u32[]{:S(2)}, u32[]{:S(2)}) async-start(bf16[16,64,256]{2,1,0:T(8,128)(2,1)} %bitcast.5), calls=%async_computation.1 | async-start | bytes 1048576 | tf_op jit(solution)/shard_map/all_to_all | solution.py:514
  62.7 14.8 %collective-permute-start.11 = (bf16[2,128,256]{2,1,0:T(8,128)(2,1)S(1)}, bf16[2,128,256]{2,1,0:T(8,128)(2,1)S(1)}, u32[]{:S(2)}, u32[]{:S(2)}) collective-permute-start(bf16[2,128,256]{2,1,0:T(8,128)(2,1)S(1)} %get-tuple-element.137), channel_id=1, source_target_pairs={{0,4},{4,0},{8,12},{12,8},{1,5},{5,1},{9,13},{13,9},{2,6},{6,2},{1... | collective-permute-start | bytes 393224 | tf_op jit(solution)/shard_map/ppermute | solution.py:455
  64.7 14.0 %collective-permute-start.13 = (bf16[2,72,256]{2,1,0:T(8,128)(2,1)S(1)}, bf16[2,72,256]{2,1,0:T(8,128)(2,1)S(1)}, u32[]{:S(2)}, u32[]{:S(2)}) collective-permute-start(bf16[2,72,256]{2,1,0:T(8,128)(2,1)S(1)} %get-tuple-element.146), channel_id=1, source_target_pairs={{0,4},{4,0},{8,12},{12,8},{1,5},{5,1},{9,13},{13,9},{2,6},{6,2},{1... | collective-permute-start | bytes 221192 | tf_op jit(solution)/shard_map/ppermute | solution.py:455
  78.7 13.0 %copy-start.8 = (s32[1,512]{1,0:T(1,128)S(1)}, s32[1,512]{1,0:T(1,128)}, u32[]{:S(2)}) copy-start(s32[1,512]{1,0:T(1,128)} %get-tuple-element.83.refs_0_) | copy-start | bytes 6148
  78.7 7.6 %collective-permute-start.14 = (bf16[200,256]{1,0:T(8,128)(2,1)S(1)}, bf16[200,256]{1,0:T(8,128)(2,1)S(1)}, u32[]{:S(2)}, u32[]{:S(2)}) collective-permute-start(bf16[200,256]{1,0:T(8,128)(2,1)S(1)} %get-tuple-element.148), channel_id=1, source_target_pairs={{0,8},{4,12},{8,0},{12,4},{1,9},{5,13},{9,1},{13,5},{2,10},{6,14},... | collective-permute-start | bytes 307208 | tf_op jit(solution)/shard_map/ppermute | solution.py:455
  86.3 4.7 %collective-permute-start.15 = (bf16[1,192,256]{2,1,0:T(8,128)(2,1)S(1)}, bf16[1,192,256]{2,1,0:T(8,128)(2,1)S(1)}, u32[]{:S(2)}, u32[]{:S(2)}) collective-permute-start(bf16[1,192,256]{2,1,0:T(8,128)(2,1)S(1)} %get-tuple-element.150), channel_id=1, source_target_pairs={{0,2},{1,3},{2,0},{3,1},{4,6},{5,7},{6,4},{7,5},{8,10},{9,11},{10,... | collective-permute-start | bytes 294920 | tf_op jit(solution)/shard_map/ppermute | solution.py:455
  91.0 1.8 %collective-permute-start.16 = (bf16[2,192,256]{2,1,0:T(8,128)(2,1)S(1)}, bf16[2,192,256]{2,1,0:T(8,128)(2,1)S(1)}, u32[]{:S(2)}, u32[]{:S(2)}) collective-permute-start(bf16[2,192,256]{2,1,0:T(8,128)(2,1)S(1)} %constant_dynamic-update-slice_fusion.refs_0_), channel_id=1, source_target_pairs={{0,1},{1,0},{2,3},{3,2},{4,5},{5,4},{6,7},{7,6},{8,9},{9,8},{10,11... | collective-permute-start | bytes 589832 | tf_op jit(solution)/shard_map/ppermute | solution.py:455
  (4 other events, 14.3 us)

commit v3 on v2

--- a/solution.py
+++ b/solution.py
@@ -455,9 +455,9 @@
     return lax.ppermute(value, axis, [(i, i ^ bit) for i in range(size)])
 
 
-def halve(keep, got, axis, bit, name):
+def halve(keep, got, axis, bit, name, micros=0.5):
     shape = (keep.shape[0] // 2,) + keep.shape[1:]
-    return call(functools.partial(halve_kernel, axis, bit), [(shape, F32), (shape, BF16)], name, 0.5, keep, got)
+    return call(functools.partial(halve_kernel, axis, bit), [(shape, F32), (shape, BF16)], name, micros, keep, got)
 
 
 def call(kernel, outs, name, micros, *args, scratch=(), hbm_in=False, hbm_out=False, raw_in=0, raw_out=0, blocked=False, limit=16):
@@ -634,18 +634,24 @@
         )
     keep_qkv, send_qkv = qkv_grads
     got_qkv = permute(send_qkv, "sample", sample_size, 1)
-    got_qkv = lax.optimization_barrier((got_qkv, got_mlp))[0]
+    keep_mlp, got_mlp = keep_mlp[0], got_mlp[0]
+    leaving = None
+    if leaf_size > 2:
+        keep_mlp, leaving = halve(keep_mlp, got_mlp, "leaf", 1, "leaf_mlp", 1.0)
+        got_qkv, leaving = lax.optimization_barrier((got_qkv, leaving))
     bit = 2
     while bit < sample_size:
         keep_qkv, send_qkv = halve(keep_qkv, got_qkv, "sample", bit, "halve_qkv")
         got_qkv = permute(send_qkv, "sample", sample_size, bit)
         bit *= 2
-    keep_mlp, got_mlp, keep_qkv, got_qkv = keep_mlp[0], got_mlp[0], keep_qkv[0], got_qkv[0]
+    keep_qkv, got_qkv = keep_qkv[0], got_qkv[0]
+    back = lax.optimization_barrier((back, got_mlp if leaving is None else leaving, send_qkv))[0]
+    returned = exchange(back, axes, peers)
+    (grad_points,) = call(unpack_kernel, [((rows, width), BF16)], "unpack", 1, slot, returned, blocked=True)
     bit = 1
     while bit * 2 < leaf_size:
-        keep_mlp, leaving = halve(keep_mlp, got_mlp, "leaf", bit, "leaf_mlp")
-        if bit == 1:
-            back = lax.optimization_barrier((back, leaving, send_qkv))[0]
+        if bit > 1:
+            keep_mlp, leaving = halve(keep_mlp, got_mlp, "leaf", bit, "leaf_mlp")
         got_mlp = permute(leaving, "leaf", leaf_size, bit)
         keep_qkv, leaving = halve(keep_qkv, got_qkv, "leaf", bit, "leaf_qkv")
         got_qkv = permute(leaving, "leaf", leaf_size, bit)
@@ -656,10 +662,8 @@
         keep_mlp, got_mlp, keep_qkv, got_qkv,
     )
     got = permute(leaving, "leaf", leaf_size, bit)
-    returned = exchange(back, axes, peers)
-    (grad_points,) = call(unpack_kernel, [((rows, width), BF16)], "unpack", 1, slot, returned, blocked=True)
     low, gains = call(
-        finish_kernel, [((1, mlp_rows + qkv_rows - GAINS, width), BF16), ((GAINS, width), F32)], "finish", 0.5, keep, got
+        finish_kernel, [((1, mlp_rows + qkv_rows - GAINS, width), BF16), ((GAINS, width), F32)], "finish", 3.5, keep, got
     )
     offsets = [0]
     bit = sample_size // 2
@@ -671,7 +675,7 @@
     share = width // leaf_size
     gains = lax.dynamic_slice(gains, (0, lax.axis_index("leaf") * share), (2, share)) * inv_root
     gain_one, gain_two = gains[0], gains[1]
-    grad_points, gain_one, gain_two, mate = lax.optimization_barrier((grad_points, gain_one, gain_two, mate))
+    gain_one, gain_two, mate = lax.optimization_barrier((gain_one, gain_two, mate))
     up_sum, down_sum, out_sum, qkv_sum = call(
         functools.partial(assemble_kernel, inv_root, offsets),
         [

time: 94.2 us -> 84.9 us (0.901)
  waiting for transfers between devices: 37.1 us -> 25.7 us
  starting transfers between devices: 35.8 us -> 38.1 us
    ppermute x17, waiting for transfers between devices: 37.1 us -> 22.4 us  [permute(): return lax.ppermute(value, axis, [(i, i ^ bit) for i in range(size)])]
    all_to_all x2, waiting for transfers between devices: 0.01 us -> 3.28 us  [exchange(): lax.all_to_all(flat.reshape((peers, -1) + flat.shape[1:]), axes, split_ax...]
    ppermute x17, starting transfers between devices: 23.2 us -> 26.5 us  [permute(): return lax.ppermute(value, axis, [(i, i ^ bit) for i in range(size)])]
    all_to_all x2, starting transfers between devices: 12.6 us -> 11.6 us  [exchange(): lax.all_to_all(flat.reshape((peers, -1) + flat.shape[1:]), axes, split_ax...]
  transfers between devices with their start and end apart: 19 -> 19, of which waited for: 10 -> 11; matrix products, arithmetic and copies ran while one was open for 1% -> 1% of each run, Pallas kernels for 8% -> 14%
where the time goes in v3:
time: 84.9 us; the launch traced here: 84.6 us
  starting transfers between devices  38.1 us (45%)
  waiting for transfers between devices  25.7 us (30%)
  Pallas kernels  18.6 us (22%)
  local copies, waits for them, and re-layouts  1.25 us (1%)
  between operations  0.86 us (1%)
    ppermute x17, starting transfers between devices, permute(): return lax.ppermute(value, axis, [(i, i ^ bit) for i in range(size)])  26.5 us
    ppermute x17, waiting for transfers between devices, permute(): return lax.ppermute(value, axis, [(i, i ^ bit) for i in range(size)])  22.4 us
    pallas_call x16, Pallas kernels, call(): pl.pallas_call(body, out_shape=[jax.ShapeDtypeStruct(shape, dtype) for sh...  18.6 us
    all_to_all x2, starting transfers between devices, exchange(): lax.all_to_all(flat.reshape((peers, -1) + flat.shape[1:]), axes, split_ax...  11.6 us
    all_to_all x2, waiting for transfers between devices, exchange(): lax.all_to_all(flat.reshape((peers, -1) + flat.shape[1:]), axes, split_ax...  3.28 us
  transfers between devices with their start and end apart: 19, of which 11 were waited for; matrix products, arithmetic and copies ran while one was open for 1% of the time, Pallas kernels for 14%

profile of v3, /device:TPU:0, one launch (start us, length us, event | category | flops | bytes accessed | tf_op | source)
XLA Modules:
  0.0 84.6 jit_solution(9770866178477343977)
XLA Ops:
  0.6 2.6 %pack_points.1 = (s32[1,512]{1,0:T(1,128)}, bf16[16,144,128]{2,1,0:T(8,128)(2,1)}) custom-call(s32[1,512]{1,0:T(1,128)} %bitcast.20, bf16[512,256]{1,0:T(8,128)(2,1)} %refs_1_.3), custom_call_target="tpu_custom_call" | custom-call | flops 2200000000 | bytes 856064 | tf_op jit(solution)/shard_map/pack_points/pallas_call | solution.py:501
  3.2 7.4 %all-to-all-start = ((bf16[16,144,128]{2,1,0:T(8,128)(2,1)}), bf16[16,144,128]{2,1,0:T(8,128)(2,1)S(1)}, u32[]{:S(2)}, u32[]{:S(2)}) async-start(bf16[16,144,128]{2,1,0:T(8,128)(2,1)} %get-tuple-element.86), calls=%async_computation | async-start | bytes 1179648 | tf_op jit(solution)/shard_map/all_to_all | solution.py:514
  11.8 2.0 %collective-permute-start = (bf16[2,64,256]{2,1,0:T(8,128)(2,1)S(1)}, bf16[2,64,256]{2,1,0:T(8,128)(2,1)S(1)}, u32[]{:S(2)}, u32[]{:S(2)}) collective-permute-start(bf16[2,64,256]{2,1,0:T(8,128)(2,1)S(1)} %get-tuple-element.84), channel_id=1, source_target_pairs={{0,2},{1,3},{2,0},{3,1},{4,6},{5,7},{6,4},{7,5},{8,10},{9,11},{10,... | collective-permute-start | bytes 196616 | tf_op jit(solution)/shard_map/ppermute | solution.py:455
  13.8 1.5 %collective-permute-start.1 = (bf16[2,64,256]{2,1,0:T(8,128)(2,1)S(1)}, bf16[2,64,256]{2,1,0:T(8,128)(2,1)S(1)}, u32[]{:S(2)}, u32[]{:S(2)}) collective-permute-start(bf16[2,64,256]{2,1,0:T(8,128)(2,1)S(1)} %get-tuple-element.85), channel_id=1, source_target_pairs={{0,4},{1,5},{2,6},{3,7},{4,0},{5,1},{6,2},{7,3},{8,12},{9,13},{10,... | collective-permute-start | bytes 196616 | tf_op jit(solution)/shard_map/ppermute | solution.py:455
  15.3 2.8 %collective-permute-start.3 = (bf16[2,64,256]{2,1,0:T(8,128)(2,1)S(1)}, bf16[2,64,256]{2,1,0:T(8,128)(2,1)S(1)}, u32[]{:S(2)}, u32[]{:S(2)}) collective-permute-start(bf16[2,64,256]{2,1,0:T(8,128)(2,1)S(1)} %get-tuple-element.96), channel_id=1, source_target_pairs={{0,8},{1,9},{2,10},{3,11},{4,12},{5,13},{6,14},{7,15},{8,0},{9,1},... | collective-permute-start | bytes 196616 | tf_op jit(solution)/shard_map/ppermute | solution.py:455
  18.1 1.5 %collective-permute-start.4 = (bf16[2,64,256]{2,1,0:T(8,128)(2,1)S(1)}, bf16[2,64,256]{2,1,0:T(8,128)(2,1)S(1)}, u32[]{:S(2)}, u32[]{:S(2)}) collective-permute-start(bf16[2,64,256]{2,1,0:T(8,128)(2,1)S(1)} %get-tuple-element.97), channel_id=1, source_target_pairs={{0,10},{1,11},{2,8},{3,9},{4,14},{5,15},{6,12},{7,13},{8,2},{9,3},... | collective-permute-start | bytes 196616 | tf_op jit(solution)/shard_map/ppermute | solution.py:455
  19.6 3.3 %collective-permute-start.5 = (bf16[2,64,256]{2,1,0:T(8,128)(2,1)S(1)}, bf16[2,64,256]{2,1,0:T(8,128)(2,1)S(1)}, u32[]{:S(2)}, u32[]{:S(2)}) collective-permute-start(bf16[2,64,256]{2,1,0:T(8,128)(2,1)S(1)} %get-tuple-element.98), channel_id=1, source_target_pairs={{0,12},{1,13},{2,14},{3,15},{4,8},{5,9},{6,10},{7,11},{8,4},{9,5},... | collective-permute-start | bytes 196616 | tf_op jit(solution)/shard_map/ppermute | solution.py:455
  23.6 4.0 %collective-permute-start.6 = (bf16[2,64,256]{2,1,0:T(8,128)(2,1)S(1)}, bf16[2,64,256]{2,1,0:T(8,128)(2,1)S(1)}, u32[]{:S(2)}, u32[]{:S(2)}) collective-permute-start(bf16[2,64,256]{2,1,0:T(8,128)(2,1)S(1)} %get-tuple-element.99), channel_id=1, source_target_pairs={{0,14},{1,15},{2,12},{3,13},{4,10},{5,11},{6,8},{7,9},{8,6},{9,7},... | collective-permute-start | bytes 196616 | tf_op jit(solution)/shard_map/ppermute | solution.py:455
  28.1 4.5 %forward.1 = (bf16[768,512]{1,0:T(8,128)(2,1)S(1)}, bf16[512,512]{1,0:T(8,128)(2,1)S(1)}, f32[8,512]{1,0:T(8,128)S(1)}, f32[256,512]{1,0:T(8,128)S(1)}, bf16[256...) custom-call(f32[256,512]{1,0:T(8,128)S(1)} %get-tuple-element.88.ref, ...), custom_call_target="tpu_custom_call" | custom-call | flops 7699999744 | bytes 12339200 | tf_op jit(solution)/shard_map/forward/pallas_call | solution.py:501
  32.7 2.1 %collective-permute-done.3.refs_4_ = bf16[2,64,256]{2,1,0:T(8,128)(2,1)S(1)} collective-permute-done((bf16[2,64,256]{2,1,0:T(8,128)(2,1)S(1)}, bf16[2,64,256]{2,1,0:T(8,128)(2,1)S(1)}, u32[]{:S(2)}, u32[]{:S(2)}) %collective-permute-start.3) | collective-permute-done | bytes 65568 | tf_op jit(solution)/shard_map/ppermute | solution.py:455
  34.8 2.3 %collective-permute-done.4.refs_5_ = bf16[2,64,256]{2,1,0:T(8,128)(2,1)S(1)} collective-permute-done((bf16[2,64,256]{2,1,0:T(8,128)(2,1)S(1)}, bf16[2,64,256]{2,1,0:T(8,128)(2,1)S(1)}, u32[]{:S(2)}, u32[]{:S(2)}) %collective-permute-start.4) | collective-permute-done | bytes 65568 | tf_op jit(solution)/shard_map/ppermute | solution.py:455
  37.3 1.5 %collective-permute-done.7.refs_6_ = bf16[8,64,256]{2,1,0:T(8,128)(2,1)S(1)} collective-permute-done((bf16[8,64,256]{2,1,0:T(8,128)(2,1)S(1)}, bf16[8,64,256]{2,1,0:T(8,128)(2,1)S(1)}, u32[]{:S(2)}, u32[]{:S(2)}) %collective-permute-start.7) | collective-permute-done | bytes 262176 | tf_op jit(solution)/shard_map/ppermute | solution.py:455
  38.8 2.6 %mlp_weights.1 = (bf16[1024,512]{1,0:T(8,128)(2,1)S(1)}, f32[256,512]{1,0:T(8,128)S(1)}, f32[2,4,128,256]{3,2,1,0:T(8,128)S(1)}, bf16[2,4,128,256]{3,2,1,0:T(8,128)(2,1)S(1)}) custom-call(s32[1,1024]{1,0:T(1,128)S(1)} %get-tuple-element.101.refs_0_, bf16[1024,512]{1,0:T(8,128)(2,1)S(1)} %get-tuple-element.102.refs_1_, ...), custom_call_target="tpu_custom_call" | custom-call | flops 2750000128 | bytes 7606272 | tf_op jit(solution)/shard_map/mlp_weights/pallas_call | solution.py:501
  44.0 4.6 %attention_backward.1 = (bf16[1024,256]{1,0:T(8,128)(2,1)}, f32[2,4,72,256]{3,2,1,0:T(8,128)S(1)}, bf16[2,4,72,256]{3,2,1,0:T(8,128)(2,1)S(1)}) custom-call(bf16[768,512]{1,0:T(8,128)(2,1)S(1)} %get-tuple-element.89.refs_0_, bf16[512,512]{1,0:T(8,128)(2,1)S(1)} %get-tuple-element.90.refs_1_, f32[8,512]{1,0:T(8,128)S(1)} %get-tuple-element.100.refs_3_.refs_2_, ...), custom_call_target="tpu_custom_call" | custom-call | flops 6600000000 | bytes 9815040 | tf_op jit(solution)/shard_map/attention_backward/pallas_call | solution.py:501
  48.6 3.3 %collective-permute-done.10 = bf16[1,4,128,256]{3,2,1,0:T(8,128)(2,1)S(1)} collective-permute-done((bf16[1,4,128,256]{3,2,1,0:T(8,128)(2,1)S(1)}, bf16[1,4,128,256]{3,2,1,0:T(8,128)(2,1)S(1)}, u32[]{:S(2)}, u32[]{:S(2)}) %collective-permute-start.10) | collective-permute-done | bytes 262176 | tf_op jit(solution)/shard_map/ppermute | solution.py:455
  52.6 2.9 %collective-permute-start.11 = (bf16[2,128,256]{2,1,0:T(8,128)(2,1)S(1)}, bf16[2,128,256]{2,1,0:T(8,128)(2,1)S(1)}, u32[]{:S(2)}, u32[]{:S(2)}) collective-permute-start(bf16[2,128,256]{2,1,0:T(8,128)(2,1)S(1)} %get-tuple-element.139), channel_id=1, source_target_pairs={{0,4},{4,0},{8,12},{12,8},{1,5},{5,1},{9,13},{13,9},{2,6},{6,2},{1... | collective-permute-start | bytes 393224 | tf_op jit(solution)/shard_map/ppermute | solution.py:455
  55.5 1.7 %collective-permute-done.12 = bf16[1,4,72,256]{3,2,1,0:T(8,128)(2,1)S(1)} collective-permute-done((bf16[1,4,72,256]{3,2,1,0:T(8,128)(2,1)S(1)}, bf16[1,4,72,256]{3,2,1,0:T(8,128)(2,1)S(1)}, u32[]{:S(2)}, u32[]{:S(2)}) %collective-permute-start.12) | collective-permute-done | bytes 147488 | tf_op jit(solution)/shard_map/ppermute | solution.py:455
  57.3 3.0 %collective-permute-start.13 = (bf16[2,72,256]{2,1,0:T(8,128)(2,1)S(1)}, bf16[2,72,256]{2,1,0:T(8,128)(2,1)S(1)}, u32[]{:S(2)}, u32[]{:S(2)}) collective-permute-start(bf16[2,72,256]{2,1,0:T(8,128)(2,1)S(1)} %get-tuple-element.147), channel_id=1, source_target_pairs={{0,4},{4,0},{8,12},{12,8},{1,5},{5,1},{9,13},{13,9},{2,6},{6,2},{1... | collective-permute-start | bytes 221192 | tf_op jit(solution)/shard_map/ppermute | solution.py:455
  60.3 2.3 %collective-permute-done.13.refs_3_ = bf16[2,72,256]{2,1,0:T(8,128)(2,1)S(1)} collective-permute-done((bf16[2,72,256]{2,1,0:T(8,128)(2,1)S(1)}, bf16[2,72,256]{2,1,0:T(8,128)(2,1)S(1)}, u32[]{:S(2)}, u32[]{:S(2)}) %collective-permute-start.13) | collective-permute-done | bytes 73760 | tf_op jit(solution)/shard_map/ppermute | solution.py:455
  62.6 2.0 %collective-permute-start.14 = (bf16[200,256]{1,0:T(8,128)(2,1)S(1)}, bf16[200,256]{1,0:T(8,128)(2,1)S(1)}, u32[]{:S(2)}, u32[]{:S(2)}) collective-permute-start(bf16[200,256]{1,0:T(8,128)(2,1)S(1)} %get-tuple-element.149), channel_id=1, source_target_pairs={{0,8},{4,12},{8,0},{12,4},{1,9},{5,13},{9,1},{13,5},{2,10},{6,14},... | collective-permute-start | bytes 307208 | tf_op jit(solution)/shard_map/ppermute | solution.py:455
  64.6 4.2 %all-to-all-start.1 = ((bf16[16,64,256]{2,1,0:T(8,128)(2,1)}), bf16[16,64,256]{2,1,0:T(8,128)(2,1)S(1)}, u32[]{:S(2)}, u32[]{:S(2)}) async-start(bf16[16,64,256]{2,1,0:T(8,128)(2,1)} %bitcast.5), calls=%async_computation.1 | async-start | bytes 1048576 | tf_op jit(solution)/shard_map/all_to_all | solution.py:514
  68.9 2.0 %collective-permute-start.15 = (bf16[1,192,256]{2,1,0:T(8,128)(2,1)S(1)}, bf16[1,192,256]{2,1,0:T(8,128)(2,1)S(1)}, u32[]{:S(2)}, u32[]{:S(2)}) collective-permute-start(bf16[1,192,256]{2,1,0:T(8,128)(2,1)S(1)} %get-tuple-element.150), channel_id=1, source_target_pairs={{0,2},{1,3},{2,0},{3,1},{4,6},{5,7},{6,4},{7,5},{8,10},{9,11},{10,... | collective-permute-start | bytes 294920 | tf_op jit(solution)/shard_map/ppermute | solution.py:455
  71.0 6.6 %collective-permute-done.15 = bf16[1,192,256]{2,1,0:T(8,128)(2,1)S(1)} collective-permute-done((bf16[1,192,256]{2,1,0:T(8,128)(2,1)S(1)}, bf16[1,192,256]{2,1,0:T(8,128)(2,1)S(1)}, u32[]{:S(2)}, u32[]{:S(2)}) %collective-permute-start.15) | collective-permute-done | bytes 98336 | tf_op jit(solution)/shard_map/ppermute | solution.py:455
  80.1 3.3 %all-to-all-done.1 = bf16[16,64,256]{2,1,0:T(8,128)(2,1)S(1)} async-done(((bf16[16,64,256]{2,1,0:T(8,128)(2,1)}), bf16[16,64,256]{2,1,0:T(8,128)(2,1)S(1)}, u32[]{:S(2)}, u32[]{:S(2)}) %all-to-all-start.1) | async-done | bytes 524320 | tf_op jit(solution)/shard_map/all_to_all | solution.py:514
  (52 shorter events, 9.8 us)
Async XLA Ops:
  0.6 10.0 %copy-start.3 = (bf16[512,256]{1,0:T(8,128)(2,1)S(1)}, bf16[512,256]{1,0:T(8,128)(2,1)}, u32[]{:S(2)}) copy-start(bf16[512,256]{1,0:T(8,128)(2,1)} %refs_1_.4) | copy-start | bytes 786436
  3.2 24.3 %all-to-all-start = ((bf16[16,144,128]{2,1,0:T(8,128)(2,1)}), bf16[16,144,128]{2,1,0:T(8,128)(2,1)S(1)}, u32[]{:S(2)}, u32[]{:S(2)}) async-start(bf16[16,144,128]{2,1,0:T(8,128)(2,1)} %get-tuple-element.86), calls=%async_computation | async-start | bytes 1179648 | tf_op jit(solution)/shard_map/all_to_all | solution.py:514
  11.8 7.8 %collective-permute-start = (bf16[2,64,256]{2,1,0:T(8,128)(2,1)S(1)}, bf16[2,64,256]{2,1,0:T(8,128)(2,1)S(1)}, u32[]{:S(2)}, u32[]{:S(2)}) collective-permute-start(bf16[2,64,256]{2,1,0:T(8,128)(2,1)S(1)} %get-tuple-element.84), channel_id=1, source_target_pairs={{0,2},{1,3},{2,0},{3,1},{4,6},{5,7},{6,4},{7,5},{8,10},{9,11},{10,... | collective-permute-start | bytes 196616 | tf_op jit(solution)/shard_map/ppermute | solution.py:455
  13.8 9.8 %collective-permute-start.1 = (bf16[2,64,256]{2,1,0:T(8,128)(2,1)S(1)}, bf16[2,64,256]{2,1,0:T(8,128)(2,1)S(1)}, u32[]{:S(2)}, u32[]{:S(2)}) collective-permute-start(bf16[2,64,256]{2,1,0:T(8,128)(2,1)S(1)} %get-tuple-element.85), channel_id=1, source_target_pairs={{0,4},{1,5},{2,6},{3,7},{4,0},{5,1},{6,2},{7,3},{8,12},{9,13},{10,... | collective-permute-start | bytes 196616 | tf_op jit(solution)/shard_map/ppermute | solution.py:455
  15.2 17.5 %collective-permute-start.2 = (bf16[2,64,256]{2,1,0:T(8,128)(2,1)S(1)}, bf16[2,64,256]{2,1,0:T(8,128)(2,1)S(1)}, u32[]{:S(2)}, u32[]{:S(2)}) collective-permute-start(bf16[2,64,256]{2,1,0:T(8,128)(2,1)S(1)} %get-tuple-element.95), channel_id=1, source_target_pairs={{0,6},{1,7},{2,4},{3,5},{4,2},{5,3},{6,0},{7,1},{8,14},{9,15},{10,... | collective-permute-start | bytes 196616 | tf_op jit(solution)/shard_map/ppermute | solution.py:455
  15.3 19.5 %collective-permute-start.3 = (bf16[2,64,256]{2,1,0:T(8,128)(2,1)S(1)}, bf16[2,64,256]{2,1,0:T(8,128)(2,1)S(1)}, u32[]{:S(2)}, u32[]{:S(2)}) collective-permute-start(bf16[2,64,256]{2,1,0:T(8,128)(2,1)S(1)} %get-tuple-element.96), channel_id=1, source_target_pairs={{0,8},{1,9},{2,10},{3,11},{4,12},{5,13},{6,14},{7,15},{8,0},{9,1},... | collective-permute-start | bytes 196616 | tf_op jit(solution)/shard_map/ppermute | solution.py:455
  18.1 19.0 %collective-permute-start.4 = (bf16[2,64,256]{2,1,0:T(8,128)(2,1)S(1)}, bf16[2,64,256]{2,1,0:T(8,128)(2,1)S(1)}, u32[]{:S(2)}, u32[]{:S(2)}) collective-permute-start(bf16[2,64,256]{2,1,0:T(8,128)(2,1)S(1)} %get-tuple-element.97), channel_id=1, source_target_pairs={{0,10},{1,11},{2,8},{3,9},{4,14},{5,15},{6,12},{7,13},{8,2},{9,3},... | collective-permute-start | bytes 196616 | tf_op jit(solution)/shard_map/ppermute | solution.py:455
  19.6 17.5 %collective-permute-start.5 = (bf16[2,64,256]{2,1,0:T(8,128)(2,1)S(1)}, bf16[2,64,256]{2,1,0:T(8,128)(2,1)S(1)}, u32[]{:S(2)}, u32[]{:S(2)}) collective-permute-start(bf16[2,64,256]{2,1,0:T(8,128)(2,1)S(1)} %get-tuple-element.98), channel_id=1, source_target_pairs={{0,12},{1,13},{2,14},{3,15},{4,8},{5,9},{6,10},{7,11},{8,4},{9,5},... | collective-permute-start | bytes 196616 | tf_op jit(solution)/shard_map/ppermute | solution.py:455
  23.6 4.5 %copy-start.5 = (f32[256]{0:T(256)S(1)}, f32[256]{0:T(256)}, u32[]{:S(2)}) copy-start(f32[256]{0:T(256)} %param.16) | copy-start | bytes 3076
  23.6 4.6 %copy-start.6 = (f32[256]{0:T(256)S(1)}, f32[256]{0:T(256)}, u32[]{:S(2)}) copy-start(f32[256]{0:T(256)} %param.17) | copy-start | bytes 3076
  23.6 13.6 %collective-permute-start.6 = (bf16[2,64,256]{2,1,0:T(8,128)(2,1)S(1)}, bf16[2,64,256]{2,1,0:T(8,128)(2,1)S(1)}, u32[]{:S(2)}, u32[]{:S(2)}) collective-permute-start(bf16[2,64,256]{2,1,0:T(8,128)(2,1)S(1)} %get-tuple-element.99), channel_id=1, source_target_pairs={{0,14},{1,15},{2,12},{3,13},{4,10},{5,11},{6,8},{7,9},{8,6},{9,7},... | collective-permute-start | bytes 196616 | tf_op jit(solution)/shard_map/ppermute | solution.py:455
  28.1 10.7 %copy-start = (bf16[1024,256]{1,0:T(8,128)(2,1)S(1)}, bf16[1024,256]{1,0:T(8,128)(2,1)}, u32[]{:S(2)}) copy-start(bf16[1024,256]{1,0:T(8,128)(2,1)} %refs_4_.1) | copy-start | bytes 1572868
  37.2 1.6 %collective-permute-start.7 = (bf16[8,64,256]{2,1,0:T(8,128)(2,1)S(1)}, bf16[8,64,256]{2,1,0:T(8,128)(2,1)S(1)}, u32[]{:S(2)}, u32[]{:S(2)}) collective-permute-start(bf16[8,64,256]{2,1,0:T(8,128)(2,1)S(1)} %get-tuple-element.114), channel_id=1, source_target_pairs={{0,1},{1,0},{2,3},{3,2},{4,5},{5,4},{6,7},{7,6},{8,9},{9,8},{10,11... | collective-permute-start | bytes 786440 | tf_op jit(solution)/shard_map/ppermute | solution.py:455
  41.4 2.0 %collective-permute-start.8 = (bf16[2,4,128,256]{3,2,1,0:T(8,128)(2,1)S(1)}, bf16[2,4,128,256]{3,2,1,0:T(8,128)(2,1)S(1)}, u32[]{:S(2)}, u32[]{:S(2)}) collective-permute-start(bf16[2,4,128,256]{3,2,1,0:T(8,128)(2,1)S(1)} %get-tuple-element.122), channel_id=1, source_target_pairs={{0,1},{1,0},{2,3},{3,2},{4,5},{5,4},{6,7},{7,6},{8,9},{9,8},{10,11... | collective-permute-start | bytes 1572872 | tf_op jit(solution)/shard_map/ppermute | solution.py:455
  43.5 8.5 %collective-permute-start.10 = (bf16[1,4,128,256]{3,2,1,0:T(8,128)(2,1)S(1)}, bf16[1,4,128,256]{3,2,1,0:T(8,128)(2,1)S(1)}, u32[]{:S(2)}, u32[]{:S(2)}) collective-permute-start(bf16[1,4,128,256]{3,2,1,0:T(8,128)(2,1)S(1)} %get-tuple-element.137), channel_id=1, source_target_pairs={{0,2},{1,3},{2,0},{3,1},{4,6},{5,7},{6,4},{7,5},{8,10},{9,11},{10,... | collective-permute-start | bytes 786440 | tf_op jit(solution)/shard_map/ppermute | solution.py:455
  48.6 3.3 %collective-permute-start.9 = (bf16[2,4,72,256]{3,2,1,0:T(8,128)(2,1)S(1)}, bf16[2,4,72,256]{3,2,1,0:T(8,128)(2,1)S(1)}, u32[]{:S(2)}, u32[]{:S(2)}) collective-permute-start(bf16[2,4,72,256]{3,2,1,0:T(8,128)(2,1)S(1)} %get-tuple-element.135), channel_id=1, source_target_pairs={{0,1},{1,0},{2,3},{3,2},{4,5},{5,4},{6,7},{7,6},{8,9},{9,8},{10,11... | collective-permute-start | bytes 884744 | tf_op jit(solution)/shard_map/ppermute | solution.py:455
  52.0 5.2 %collective-permute-start.12 = (bf16[1,4,72,256]{3,2,1,0:T(8,128)(2,1)S(1)}, bf16[1,4,72,256]{3,2,1,0:T(8,128)(2,1)S(1)}, u32[]{:S(2)}, u32[]{:S(2)}) collective-permute-start(bf16[1,4,72,256]{3,2,1,0:T(8,128)(2,1)S(1)} %get-tuple-element.142), channel_id=1, source_target_pairs={{0,2},{1,3},{2,0},{3,1},{4,6},{5,7},{6,4},{7,5},{8,10},{9,11},{10,... | collective-permute-start | bytes 442376 | tf_op jit(solution)/shard_map/ppermute | solution.py:455
  52.6 7.6 %collective-permute-start.11 = (bf16[2,128,256]{2,1,0:T(8,128)(2,1)S(1)}, bf16[2,128,256]{2,1,0:T(8,128)(2,1)S(1)}, u32[]{:S(2)}, u32[]{:S(2)}) collective-permute-start(bf16[2,128,256]{2,1,0:T(8,128)(2,1)S(1)} %get-tuple-element.139), channel_id=1, source_target_pairs={{0,4},{4,0},{8,12},{12,8},{1,5},{5,1},{9,13},{13,9},{2,6},{6,2},{1... | collective-permute-start | bytes 393224 | tf_op jit(solution)/shard_map/ppermute | solution.py:455
  57.3 5.3 %collective-permute-start.13 = (bf16[2,72,256]{2,1,0:T(8,128)(2,1)S(1)}, bf16[2,72,256]{2,1,0:T(8,128)(2,1)S(1)}, u32[]{:S(2)}, u32[]{:S(2)}) collective-permute-start(bf16[2,72,256]{2,1,0:T(8,128)(2,1)S(1)} %get-tuple-element.147), channel_id=1, source_target_pairs={{0,4},{4,0},{8,12},{12,8},{1,5},{5,1},{9,13},{13,9},{2,6},{6,2},{1... | collective-permute-start | bytes 221192 | tf_op jit(solution)/shard_map/ppermute | solution.py:455
  62.6 6.2 %collective-permute-start.14 = (bf16[200,256]{1,0:T(8,128)(2,1)S(1)}, bf16[200,256]{1,0:T(8,128)(2,1)S(1)}, u32[]{:S(2)}, u32[]{:S(2)}) collective-permute-start(bf16[200,256]{1,0:T(8,128)(2,1)S(1)} %get-tuple-element.149), channel_id=1, source_target_pairs={{0,8},{4,12},{8,0},{12,4},{1,9},{5,13},{9,1},{13,5},{2,10},{6,14},... | collective-permute-start | bytes 307208 | tf_op jit(solution)/shard_map/ppermute | solution.py:455
  64.6 18.7 %all-to-all-start.1 = ((bf16[16,64,256]{2,1,0:T(8,128)(2,1)}), bf16[16,64,256]{2,1,0:T(8,128)(2,1)S(1)}, u32[]{:S(2)}, u32[]{:S(2)}) async-start(bf16[16,64,256]{2,1,0:T(8,128)(2,1)} %bitcast.5), calls=%async_computation.1 | async-start | bytes 1048576 | tf_op jit(solution)/shard_map/all_to_all | solution.py:514
  68.9 8.7 %collective-permute-start.15 = (bf16[1,192,256]{2,1,0:T(8,128)(2,1)S(1)}, bf16[1,192,256]{2,1,0:T(8,128)(2,1)S(1)}, u32[]{:S(2)}, u32[]{:S(2)}) collective-permute-start(bf16[1,192,256]{2,1,0:T(8,128)(2,1)S(1)} %get-tuple-element.150), channel_id=1, source_target_pairs={{0,2},{1,3},{2,0},{3,1},{4,6},{5,7},{6,4},{7,5},{8,10},{9,11},{10,... | collective-permute-start | bytes 294920 | tf_op jit(solution)/shard_map/ppermute | solution.py:455
  71.0 12.4 %copy-start.8 = (s32[1,512]{1,0:T(1,128)S(1)}, s32[1,512]{1,0:T(1,128)}, u32[]{:S(2)}) copy-start(s32[1,512]{1,0:T(1,128)} %get-tuple-element.83.refs_0_) | copy-start | bytes 6148
  77.6 1.5 %collective-permute-start.16 = (bf16[2,192,256]{2,1,0:T(8,128)(2,1)S(1)}, bf16[2,192,256]{2,1,0:T(8,128)(2,1)S(1)}, u32[]{:S(2)}, u32[]{:S(2)}) collective-permute-start(bf16[2,192,256]{2,1,0:T(8,128)(2,1)S(1)} %constant_dynamic-update-slice_fusion.refs_0_), channel_id=1, source_target_pairs={{0,1},{1,0},{2,3},{3,2},{4,5},{5,4},{6,7},{7,6},{8,9},{9,8},{10,11... | collective-permute-start | bytes 589832 | tf_op jit(solution)/shard_map/ppermute | solution.py:455
  (4 other events, 14.3 us)

commit v4 on v3

--- a/solution.py
+++ b/solution.py
@@ -410,15 +410,29 @@
             ref[high] = (keep_ref[at] + got_ref[at].astype(F32)).astype(ref.dtype)
 
 
-def join_kernel(bit, *refs):
-    ins, (keep_out_ref, send_out_ref) = refs[:-2], refs[-2:]
-    mine = lax.rem(lax.div(lax.axis_index("leaf"), bit), 2)
+def quarter_kernel(keep_ref, got_ref, keep_out_ref, *send_refs):
+    mine = lax.rem(lax.div(lax.axis_index("sample"), 2), 2)
+    low = lax.rem(lax.axis_index("leaf"), 2)
+    places = ((mine, low), (1 - mine, low), (mine, 1 - low), (1 - mine, 1 - low))
+    for ref, (sample, leaf) in zip((keep_out_ref, *send_refs), places):
+        for high in range(ref.shape[0]):
+            total = keep_ref[sample, 2 * high + leaf] + got_ref[sample, 2 * high + leaf].astype(F32)
+            ref[high] = total.astype(ref.dtype)
+
+
+def join_kernel(counts, *refs):
+    ins, (keep_out_ref, send_out_ref) = list(refs[:-2]), refs[-2:]
+    mine = lax.rem(lax.div(lax.axis_index("leaf"), 2), 2)
     start = 0
-    for keep_ref, got_ref in zip(ins[::2], ins[1::2]):
-        rows = pl.ds(start, keep_ref.shape[1])
+    for count in counts:
+        part, ins = ins[:count], ins[count:]
+        rows = pl.ds(start, part[0].shape[1])
         for ref, at in ((keep_out_ref, mine), (send_out_ref, 1 - mine)):
-            ref[rows, :] = (keep_ref[at] + got_ref[at].astype(F32)).astype(ref.dtype)
-        start += keep_ref.shape[1]
+            total = part[0][at]
+            for got_ref in part[1:]:
+                total = total + got_ref[at].astype(F32)
+            ref[rows, :] = total.astype(ref.dtype)
+        start += part[0].shape[1]
 
 
 def finish_kernel(keep_ref, got_ref, low_ref, gains_ref):
@@ -528,7 +542,7 @@
     balls = rows // BALL
     direct = cap % 16 == 0
     paired = leaf_size & (leaf_size - 1) == 0 and sample_size & (sample_size - 1) == 0 and min(leaf_size, sample_size) > 1
-    arranged = paired and width % (16 * peers) == 0 and hidden_width == sample_size * width and leaf_size <= 8
+    arranged = paired and width % (16 * peers) == 0 and hidden_width == sample_size * width and (leaf_size, sample_size) == (4, 4)
     inv_root = 1.0 / math.sqrt(rows * peers)
 
     msg_rows = 2 * cap + META
@@ -634,34 +648,24 @@
         )
     keep_qkv, send_qkv = qkv_grads
     got_qkv = permute(send_qkv, "sample", sample_size, 1)
-    keep_mlp, got_mlp = keep_mlp[0], got_mlp[0]
-    leaving = None
-    if leaf_size > 2:
-        keep_mlp, leaving = halve(keep_mlp, got_mlp, "leaf", 1, "leaf_mlp", 1.0)
-        got_qkv, leaving = lax.optimization_barrier((got_qkv, leaving))
-    bit = 2
-    while bit < sample_size:
-        keep_qkv, send_qkv = halve(keep_qkv, got_qkv, "sample", bit, "halve_qkv")
-        got_qkv = permute(send_qkv, "sample", sample_size, bit)
-        bit *= 2
-    keep_qkv, got_qkv = keep_qkv[0], got_qkv[0]
-    back = lax.optimization_barrier((back, got_mlp if leaving is None else leaving, send_qkv))[0]
+    keep_mlp, leaving = halve(keep_mlp[0], got_mlp[0], "leaf", 1, "leaf_mlp", 1.0)
+    got_qkv, leaving = lax.optimization_barrier((got_qkv, leaving))
+    quarter = (leaf_size // 2, qkv_rows, width)
+    keep_qkv, send_sample, send_leaf, send_both = call(
+        quarter_kernel, [(quarter, F32)] + [(quarter, BF16)] * 3, "quarter_qkv", 0.5, keep_qkv, got_qkv
+    )
+    back = lax.optimization_barrier((back, leaving, send_sample))[0]
     returned = exchange(back, axes, peers)
     (grad_points,) = call(unpack_kernel, [((rows, width), BF16)], "unpack", 1, slot, returned, blocked=True)
-    bit = 1
-    while bit * 2 < leaf_size:
-        if bit > 1:
-            keep_mlp, leaving = halve(keep_mlp, got_mlp, "leaf", bit, "leaf_mlp")
-        got_mlp = permute(leaving, "leaf", leaf_size, bit)
-        keep_qkv, leaving = halve(keep_qkv, got_qkv, "leaf", bit, "leaf_qkv")
-        got_qkv = permute(leaving, "leaf", leaf_size, bit)
-        bit *= 2
     joined = (mlp_rows + qkv_rows, width)
     keep, leaving = call(
-        functools.partial(join_kernel, bit), [(joined, F32), (joined, BF16)], "leaf_last", 0.5,
-        keep_mlp, got_mlp, keep_qkv, got_qkv,
-    )
-    got = permute(leaving, "leaf", leaf_size, bit)
+        functools.partial(join_kernel, (2, 4)), [(joined, F32), (joined, BF16)], "leaf_last", 0.5,
+        keep_mlp, permute(leaving, "leaf", leaf_size, 1), keep_qkv,
+        permute(send_sample, "sample", sample_size, 2),
+        permute(send_leaf, "leaf", leaf_size, 1),
+        permute(send_both, axes, peers, sample_size + 2),
+    )
+    got = permute(leaving, "leaf", leaf_size, 2)
     low, gains = call(
         finish_kernel, [((1, mlp_rows + qkv_rows - GAINS, width), BF16), ((GAINS, width), F32)], "finish", 3.5, keep, got
     )

time: 84.9 us -> 83.7 us (0.986)
  starting transfers between devices: 38.1 us -> 37.1 us
    ppermute x17 -> x18, starting transfers between devices: 26.5 us -> 25.1 us  [permute(): return lax.ppermute(value, axis, [(i, i ^ bit) for i in range(size)])]
    ppermute x17 -> x18, waiting for transfers between devices: 22.4 us -> 22.2 us  [permute(): return lax.ppermute(value, axis, [(i, i ^ bit) for i in range(size)])]
    pallas_call x16 -> x15, Pallas kernels: 18.6 us -> 18.6 us  [call(): pl.pallas_call(body, out_shape=[jax.ShapeDtypeStruct(shape, dtype) for sh...]
  transfers between devices with their start and end apart: 19 -> 20, of which waited for: 11 -> 13; matrix products, arithmetic and copies ran while one was open for 1% -> 1% of each run, Pallas kernels for 14% -> 14%
where the time goes in v4:
time: 83.7 us; the launch traced here: 83.4 us
  starting transfers between devices  37.1 us (44%)
  waiting for transfers between devices  25.5 us (30%)
  Pallas kernels  18.6 us (22%)
  local copies, waits for them, and re-layouts  1.25 us (1%)
  between operations  0.85 us (1%)
    ppermute x18, starting transfers between devices, permute(): return lax.ppermute(value, axis, [(i, i ^ bit) for i in range(size)])  25.1 us
    ppermute x18, waiting for transfers between devices, permute(): return lax.ppermute(value, axis, [(i, i ^ bit) for i in range(size)])  22.2 us
    pallas_call x15, Pallas kernels, call(): pl.pallas_call(body, out_shape=[jax.ShapeDtypeStruct(shape, dtype) for sh...  18.6 us
    all_to_all x2, starting transfers between devices, exchange(): lax.all_to_all(flat.reshape((peers, -1) + flat.shape[1:]), axes, split_ax...  11.9 us
    all_to_all x2, waiting for transfers between devices, exchange(): lax.all_to_all(flat.reshape((peers, -1) + flat.shape[1:]), axes, split_ax...  3.28 us
  transfers between devices with their start and end apart: 20, of which 13 were waited for; matrix products, arithmetic and copies ran while one was open for 1% of the time, Pallas kernels for 14%

profile of v4, /device:TPU:0, one launch (start us, length us, event | category | flops | bytes accessed | tf_op | source)
XLA Modules:
  0.0 83.4 jit_solution(7058352748849220570)
XLA Ops:
  0.6 2.6 %pack_points.1 = (s32[1,512]{1,0:T(1,128)}, bf16[16,144,128]{2,1,0:T(8,128)(2,1)}) custom-call(s32[1,512]{1,0:T(1,128)} %bitcast.16, bf16[512,256]{1,0:T(8,128)(2,1)} %refs_1_.3), custom_call_target="tpu_custom_call" | custom-call | flops 2200000000 | bytes 856064 | tf_op jit(solution)/shard_map/pack_points/pallas_call | solution.py:515
  3.2 7.4 %all-to-all-start = ((bf16[16,144,128]{2,1,0:T(8,128)(2,1)}), bf16[16,144,128]{2,1,0:T(8,128)(2,1)S(1)}, u32[]{:S(2)}, u32[]{:S(2)}) async-start(bf16[16,144,128]{2,1,0:T(8,128)(2,1)} %get-tuple-element.86), calls=%async_computation | async-start | bytes 1179648 | tf_op jit(solution)/shard_map/all_to_all | solution.py:528
  11.8 2.0 %collective-permute-start = (bf16[2,64,256]{2,1,0:T(8,128)(2,1)S(1)}, bf16[2,64,256]{2,1,0:T(8,128)(2,1)S(1)}, u32[]{:S(2)}, u32[]{:S(2)}) collective-permute-start(bf16[2,64,256]{2,1,0:T(8,128)(2,1)S(1)} %get-tuple-element.84), channel_id=1, source_target_pairs={{0,2},{1,3},{2,0},{3,1},{4,6},{5,7},{6,4},{7,5},{8,10},{9,11},{10,... | collective-permute-start | bytes 196616 | tf_op jit(solution)/shard_map/ppermute | solution.py:469
  13.8 1.5 %collective-permute-start.1 = (bf16[2,64,256]{2,1,0:T(8,128)(2,1)S(1)}, bf16[2,64,256]{2,1,0:T(8,128)(2,1)S(1)}, u32[]{:S(2)}, u32[]{:S(2)}) collective-permute-start(bf16[2,64,256]{2,1,0:T(8,128)(2,1)S(1)} %get-tuple-element.85), channel_id=1, source_target_pairs={{0,4},{1,5},{2,6},{3,7},{4,0},{5,1},{6,2},{7,3},{8,12},{9,13},{10,... | collective-permute-start | bytes 196616 | tf_op jit(solution)/shard_map/ppermute | solution.py:469
  15.3 2.8 %collective-permute-start.3 = (bf16[2,64,256]{2,1,0:T(8,128)(2,1)S(1)}, bf16[2,64,256]{2,1,0:T(8,128)(2,1)S(1)}, u32[]{:S(2)}, u32[]{:S(2)}) collective-permute-start(bf16[2,64,256]{2,1,0:T(8,128)(2,1)S(1)} %get-tuple-element.96), channel_id=1, source_target_pairs={{0,8},{1,9},{2,10},{3,11},{4,12},{5,13},{6,14},{7,15},{8,0},{9,1},... | collective-permute-start | bytes 196616 | tf_op jit(solution)/shard_map/ppermute | solution.py:469
  18.1 1.5 %collective-permute-start.4 = (bf16[2,64,256]{2,1,0:T(8,128)(2,1)S(1)}, bf16[2,64,256]{2,1,0:T(8,128)(2,1)S(1)}, u32[]{:S(2)}, u32[]{:S(2)}) collective-permute-start(bf16[2,64,256]{2,1,0:T(8,128)(2,1)S(1)} %get-tuple-element.97), channel_id=1, source_target_pairs={{0,10},{1,11},{2,8},{3,9},{4,14},{5,15},{6,12},{7,13},{8,2},{9,3},... | collective-permute-start | bytes 196616 | tf_op jit(solution)/shard_map/ppermute | solution.py:469
  19.6 3.3 %collective-permute-start.5 = (bf16[2,64,256]{2,1,0:T(8,128)(2,1)S(1)}, bf16[2,64,256]{2,1,0:T(8,128)(2,1)S(1)}, u32[]{:S(2)}, u32[]{:S(2)}) collective-permute-start(bf16[2,64,256]{2,1,0:T(8,128)(2,1)S(1)} %get-tuple-element.98), channel_id=1, source_target_pairs={{0,12},{1,13},{2,14},{3,15},{4,8},{5,9},{6,10},{7,11},{8,4},{9,5},... | collective-permute-start | bytes 196616 | tf_op jit(solution)/shard_map/ppermute | solution.py:469
  23.6 4.0 %collective-permute-start.6 = (bf16[2,64,256]{2,1,0:T(8,128)(2,1)S(1)}, bf16[2,64,256]{2,1,0:T(8,128)(2,1)S(1)}, u32[]{:S(2)}, u32[]{:S(2)}) collective-permute-start(bf16[2,64,256]{2,1,0:T(8,128)(2,1)S(1)} %get-tuple-element.99), channel_id=1, source_target_pairs={{0,14},{1,15},{2,12},{3,13},{4,10},{5,11},{6,8},{7,9},{8,6},{9,7},... | collective-permute-start | bytes 196616 | tf_op jit(solution)/shard_map/ppermute | solution.py:469
  28.1 4.5 %forward.1 = (bf16[768,512]{1,0:T(8,128)(2,1)S(1)}, bf16[512,512]{1,0:T(8,128)(2,1)S(1)}, f32[8,512]{1,0:T(8,128)S(1)}, f32[256,512]{1,0:T(8,128)S(1)}, bf16[256...) custom-call(f32[256,512]{1,0:T(8,128)S(1)} %get-tuple-element.88.ref, ...), custom_call_target="tpu_custom_call" | custom-call | flops 7699999744 | bytes 12339200 | tf_op jit(solution)/shard_map/forward/pallas_call | solution.py:515
  32.7 2.1 %collective-permute-done.3.refs_4_ = bf16[2,64,256]{2,1,0:T(8,128)(2,1)S(1)} collective-permute-done((bf16[2,64,256]{2,1,0:T(8,128)(2,1)S(1)}, bf16[2,64,256]{2,1,0:T(8,128)(2,1)S(1)}, u32[]{:S(2)}, u32[]{:S(2)}) %collective-permute-start.3) | collective-permute-done | bytes 65568 | tf_op jit(solution)/shard_map/ppermute | solution.py:469
  34.8 2.3 %collective-permute-done.4.refs_5_ = bf16[2,64,256]{2,1,0:T(8,128)(2,1)S(1)} collective-permute-done((bf16[2,64,256]{2,1,0:T(8,128)(2,1)S(1)}, bf16[2,64,256]{2,1,0:T(8,128)(2,1)S(1)}, u32[]{:S(2)}, u32[]{:S(2)}) %collective-permute-start.4) | collective-permute-done | bytes 65568 | tf_op jit(solution)/shard_map/ppermute | solution.py:469
  37.3 1.5 %collective-permute-done.7.refs_6_ = bf16[8,64,256]{2,1,0:T(8,128)(2,1)S(1)} collective-permute-done((bf16[8,64,256]{2,1,0:T(8,128)(2,1)S(1)}, bf16[8,64,256]{2,1,0:T(8,128)(2,1)S(1)}, u32[]{:S(2)}, u32[]{:S(2)}) %collective-permute-start.7) | collective-permute-done | bytes 262176 | tf_op jit(solution)/shard_map/ppermute | solution.py:469
  38.8 2.6 %mlp_weights.1 = (bf16[1024,512]{1,0:T(8,128)(2,1)S(1)}, f32[256,512]{1,0:T(8,128)S(1)}, f32[2,4,128,256]{3,2,1,0:T(8,128)S(1)}, bf16[2,4,128,256]{3,2,1,0:T(8,128)(2,1)S(1)}) custom-call(s32[1,1024]{1,0:T(1,128)S(1)} %get-tuple-element.101.refs_0_, bf16[1024,512]{1,0:T(8,128)(2,1)S(1)} %get-tuple-element.102.refs_1_, ...), custom_call_target="tpu_custom_call" | custom-call | flops 2750000128 | bytes 7606272 | tf_op jit(solution)/shard_map/mlp_weights/pallas_call | solution.py:515
  44.0 4.6 %attention_backward.1 = (bf16[1024,256]{1,0:T(8,128)(2,1)}, f32[2,4,72,256]{3,2,1,0:T(8,128)S(1)}, bf16[2,4,72,256]{3,2,1,0:T(8,128)(2,1)S(1)}) custom-call(bf16[768,512]{1,0:T(8,128)(2,1)S(1)} %get-tuple-element.89.refs_0_, bf16[512,512]{1,0:T(8,128)(2,1)S(1)} %get-tuple-element.90.refs_1_, f32[8,512]{1,0:T(8,128)S(1)} %get-tuple-element.100.refs_3_.refs_2_, ...), custom_call_target="tpu_custom_call" | custom-call | flops 6600000000 | bytes 9815040 | tf_op jit(solution)/shard_map/attention_backward/pallas_call | solution.py:515
  48.6 3.3 %collective-permute-done.10 = bf16[1,4,128,256]{3,2,1,0:T(8,128)(2,1)S(1)} collective-permute-done((bf16[1,4,128,256]{3,2,1,0:T(8,128)(2,1)S(1)}, bf16[1,4,128,256]{3,2,1,0:T(8,128)(2,1)S(1)}, u32[]{:S(2)}, u32[]{:S(2)}) %collective-permute-start.10) | collective-permute-done | bytes 262176 | tf_op jit(solution)/shard_map/ppermute | solution.py:469
  52.0 3.0 %collective-permute-start.11 = (bf16[2,128,256]{2,1,0:T(8,128)(2,1)S(1)}, bf16[2,128,256]{2,1,0:T(8,128)(2,1)S(1)}, u32[]{:S(2)}, u32[]{:S(2)}) collective-permute-start(bf16[2,128,256]{2,1,0:T(8,128)(2,1)S(1)} %get-tuple-element.139), channel_id=1, source_target_pairs={{0,4},{4,0},{8,12},{12,8},{1,5},{5,1},{9,13},{13,9},{2,6},{6,2},{1... | collective-permute-start | bytes 393224 | tf_op jit(solution)/shard_map/ppermute | solution.py:469
  55.6 2.9 %collective-permute-start.14 = (bf16[2,72,256]{2,1,0:T(8,128)(2,1)S(1)}, bf16[2,72,256]{2,1,0:T(8,128)(2,1)S(1)}, u32[]{:S(2)}, u32[]{:S(2)}) collective-permute-start(bf16[2,72,256]{2,1,0:T(8,128)(2,1)S(1)} %get-tuple-element.147), channel_id=1, source_target_pairs={{0,6},{1,7},{2,4},{3,5},{4,2},{5,3},{6,0},{7,1},{8,14},{9,15},{10,... | collective-permute-start | bytes 221192 | tf_op jit(solution)/shard_map/ppermute | solution.py:469
  58.5 1.7 %collective-permute-done.12.refs_3_ = bf16[2,72,256]{2,1,0:T(8,128)(2,1)S(1)} collective-permute-done((bf16[2,72,256]{2,1,0:T(8,128)(2,1)S(1)}, bf16[2,72,256]{2,1,0:T(8,128)(2,1)S(1)}, u32[]{:S(2)}, u32[]{:S(2)}) %collective-permute-start.12) | collective-permute-done | bytes 73760 | tf_op jit(solution)/shard_map/ppermute | solution.py:469
  60.3 1.4 %collective-permute-done.14.refs_5_ = bf16[2,72,256]{2,1,0:T(8,128)(2,1)S(1)} collective-permute-done((bf16[2,72,256]{2,1,0:T(8,128)(2,1)S(1)}, bf16[2,72,256]{2,1,0:T(8,128)(2,1)S(1)}, u32[]{:S(2)}, u32[]{:S(2)}) %collective-permute-start.14) | collective-permute-done | bytes 73760 | tf_op jit(solution)/shard_map/ppermute | solution.py:469
  61.7 1.4 %collective-permute-start.15 = (bf16[200,256]{1,0:T(8,128)(2,1)S(1)}, bf16[200,256]{1,0:T(8,128)(2,1)S(1)}, u32[]{:S(2)}, u32[]{:S(2)}) collective-permute-start(bf16[200,256]{1,0:T(8,128)(2,1)S(1)} %get-tuple-element.149), channel_id=1, source_target_pairs={{0,8},{4,12},{8,0},{12,4},{1,9},{5,13},{9,1},{13,5},{2,10},{6,14},... | collective-permute-start | bytes 307208 | tf_op jit(solution)/shard_map/ppermute | solution.py:469
  63.1 4.6 %all-to-all-start.1 = ((bf16[16,64,256]{2,1,0:T(8,128)(2,1)}), bf16[16,64,256]{2,1,0:T(8,128)(2,1)S(1)}, u32[]{:S(2)}, u32[]{:S(2)}) async-start(bf16[16,64,256]{2,1,0:T(8,128)(2,1)} %bitcast.5), calls=%async_computation.1 | async-start | bytes 1048576 | tf_op jit(solution)/shard_map/all_to_all | solution.py:528
  68.5 1.2 %collective-permute-start.16 = (bf16[1,192,256]{2,1,0:T(8,128)(2,1)S(1)}, bf16[1,192,256]{2,1,0:T(8,128)(2,1)S(1)}, u32[]{:S(2)}, u32[]{:S(2)}) collective-permute-start(bf16[1,192,256]{2,1,0:T(8,128)(2,1)S(1)} %get-tuple-element.150), channel_id=1, source_target_pairs={{0,2},{1,3},{2,0},{3,1},{4,6},{5,7},{6,4},{7,5},{8,10},{9,11},{10,... | collective-permute-start | bytes 294920 | tf_op jit(solution)/shard_map/ppermute | solution.py:469
  69.8 6.6 %collective-permute-done.16 = bf16[1,192,256]{2,1,0:T(8,128)(2,1)S(1)} collective-permute-done((bf16[1,192,256]{2,1,0:T(8,128)(2,1)S(1)}, bf16[1,192,256]{2,1,0:T(8,128)(2,1)S(1)}, u32[]{:S(2)}, u32[]{:S(2)}) %collective-permute-start.16) | collective-permute-done | bytes 98336 | tf_op jit(solution)/shard_map/ppermute | solution.py:469
  78.9 3.3 %all-to-all-done.1 = bf16[16,64,256]{2,1,0:T(8,128)(2,1)S(1)} async-done(((bf16[16,64,256]{2,1,0:T(8,128)(2,1)}), bf16[16,64,256]{2,1,0:T(8,128)(2,1)S(1)}, u32[]{:S(2)}, u32[]{:S(2)}) %all-to-all-start.1) | async-done | bytes 524320 | tf_op jit(solution)/shard_map/all_to_all | solution.py:528
  (53 shorter events, 10.7 us)
Async XLA Ops:
  0.6 10.0 %copy-start.3 = (bf16[512,256]{1,0:T(8,128)(2,1)S(1)}, bf16[512,256]{1,0:T(8,128)(2,1)}, u32[]{:S(2)}) copy-start(bf16[512,256]{1,0:T(8,128)(2,1)} %refs_1_.4) | copy-start | bytes 786436
  3.2 24.3 %all-to-all-start = ((bf16[16,144,128]{2,1,0:T(8,128)(2,1)}), bf16[16,144,128]{2,1,0:T(8,128)(2,1)S(1)}, u32[]{:S(2)}, u32[]{:S(2)}) async-start(bf16[16,144,128]{2,1,0:T(8,128)(2,1)} %get-tuple-element.86), calls=%async_computation | async-start | bytes 1179648 | tf_op jit(solution)/shard_map/all_to_all | solution.py:528
  11.8 7.8 %collective-permute-start = (bf16[2,64,256]{2,1,0:T(8,128)(2,1)S(1)}, bf16[2,64,256]{2,1,0:T(8,128)(2,1)S(1)}, u32[]{:S(2)}, u32[]{:S(2)}) collective-permute-start(bf16[2,64,256]{2,1,0:T(8,128)(2,1)S(1)} %get-tuple-element.84), channel_id=1, source_target_pairs={{0,2},{1,3},{2,0},{3,1},{4,6},{5,7},{6,4},{7,5},{8,10},{9,11},{10,... | collective-permute-start | bytes 196616 | tf_op jit(solution)/shard_map/ppermute | solution.py:469
  13.8 9.8 %collective-permute-start.1 = (bf16[2,64,256]{2,1,0:T(8,128)(2,1)S(1)}, bf16[2,64,256]{2,1,0:T(8,128)(2,1)S(1)}, u32[]{:S(2)}, u32[]{:S(2)}) collective-permute-start(bf16[2,64,256]{2,1,0:T(8,128)(2,1)S(1)} %get-tuple-element.85), channel_id=1, source_target_pairs={{0,4},{1,5},{2,6},{3,7},{4,0},{5,1},{6,2},{7,3},{8,12},{9,13},{10,... | collective-permute-start | bytes 196616 | tf_op jit(solution)/shard_map/ppermute | solution.py:469
  15.2 17.5 %collective-permute-start.2 = (bf16[2,64,256]{2,1,0:T(8,128)(2,1)S(1)}, bf16[2,64,256]{2,1,0:T(8,128)(2,1)S(1)}, u32[]{:S(2)}, u32[]{:S(2)}) collective-permute-start(bf16[2,64,256]{2,1,0:T(8,128)(2,1)S(1)} %get-tuple-element.95), channel_id=1, source_target_pairs={{0,6},{1,7},{2,4},{3,5},{4,2},{5,3},{6,0},{7,1},{8,14},{9,15},{10,... | collective-permute-start | bytes 196616 | tf_op jit(solution)/shard_map/ppermute | solution.py:469
  15.3 19.5 %collective-permute-start.3 = (bf16[2,64,256]{2,1,0:T(8,128)(2,1)S(1)}, bf16[2,64,256]{2,1,0:T(8,128)(2,1)S(1)}, u32[]{:S(2)}, u32[]{:S(2)}) collective-permute-start(bf16[2,64,256]{2,1,0:T(8,128)(2,1)S(1)} %get-tuple-element.96), channel_id=1, source_target_pairs={{0,8},{1,9},{2,10},{3,11},{4,12},{5,13},{6,14},{7,15},{8,0},{9,1},... | collective-permute-start | bytes 196616 | tf_op jit(solution)/shard_map/ppermute | solution.py:469
  18.1 19.0 %collective-permute-start.4 = (bf16[2,64,256]{2,1,0:T(8,128)(2,1)S(1)}, bf16[2,64,256]{2,1,0:T(8,128)(2,1)S(1)}, u32[]{:S(2)}, u32[]{:S(2)}) collective-permute-start(bf16[2,64,256]{2,1,0:T(8,128)(2,1)S(1)} %get-tuple-element.97), channel_id=1, source_target_pairs={{0,10},{1,11},{2,8},{3,9},{4,14},{5,15},{6,12},{7,13},{8,2},{9,3},... | collective-permute-start | bytes 196616 | tf_op jit(solution)/shard_map/ppermute | solution.py:469
  19.6 17.5 %collective-permute-start.5 = (bf16[2,64,256]{2,1,0:T(8,128)(2,1)S(1)}, bf16[2,64,256]{2,1,0:T(8,128)(2,1)S(1)}, u32[]{:S(2)}, u32[]{:S(2)}) collective-permute-start(bf16[2,64,256]{2,1,0:T(8,128)(2,1)S(1)} %get-tuple-element.98), channel_id=1, source_target_pairs={{0,12},{1,13},{2,14},{3,15},{4,8},{5,9},{6,10},{7,11},{8,4},{9,5},... | collective-permute-start | bytes 196616 | tf_op jit(solution)/shard_map/ppermute | solution.py:469
  23.6 4.6 %copy-start.6 = (f32[256]{0:T(256)S(1)}, f32[256]{0:T(256)}, u32[]{:S(2)}) copy-start(f32[256]{0:T(256)} %param.17) | copy-start | bytes 3076
  23.6 13.6 %collective-permute-start.6 = (bf16[2,64,256]{2,1,0:T(8,128)(2,1)S(1)}, bf16[2,64,256]{2,1,0:T(8,128)(2,1)S(1)}, u32[]{:S(2)}, u32[]{:S(2)}) collective-permute-start(bf16[2,64,256]{2,1,0:T(8,128)(2,1)S(1)} %get-tuple-element.99), channel_id=1, source_target_pairs={{0,14},{1,15},{2,12},{3,13},{4,10},{5,11},{6,8},{7,9},{8,6},{9,7},... | collective-permute-start | bytes 196616 | tf_op jit(solution)/shard_map/ppermute | solution.py:469
  28.1 10.7 %copy-start = (bf16[1024,256]{1,0:T(8,128)(2,1)S(1)}, bf16[1024,256]{1,0:T(8,128)(2,1)}, u32[]{:S(2)}) copy-start(bf16[1024,256]{1,0:T(8,128)(2,1)} %refs_4_.1) | copy-start | bytes 1572868
  37.2 1.6 %collective-permute-start.7 = (bf16[8,64,256]{2,1,0:T(8,128)(2,1)S(1)}, bf16[8,64,256]{2,1,0:T(8,128)(2,1)S(1)}, u32[]{:S(2)}, u32[]{:S(2)}) collective-permute-start(bf16[8,64,256]{2,1,0:T(8,128)(2,1)S(1)} %get-tuple-element.114), channel_id=1, source_target_pairs={{0,1},{1,0},{2,3},{3,2},{4,5},{5,4},{6,7},{7,6},{8,9},{9,8},{10,11... | collective-permute-start | bytes 786440 | tf_op jit(solution)/shard_map/ppermute | solution.py:469
  41.4 2.0 %collective-permute-start.8 = (bf16[2,4,128,256]{3,2,1,0:T(8,128)(2,1)S(1)}, bf16[2,4,128,256]{3,2,1,0:T(8,128)(2,1)S(1)}, u32[]{:S(2)}, u32[]{:S(2)}) collective-permute-start(bf16[2,4,128,256]{3,2,1,0:T(8,128)(2,1)S(1)} %get-tuple-element.122), channel_id=1, source_target_pairs={{0,1},{1,0},{2,3},{3,2},{4,5},{5,4},{6,7},{7,6},{8,9},{9,8},{10,11... | collective-permute-start | bytes 1572872 | tf_op jit(solution)/shard_map/ppermute | solution.py:469
  43.5 8.5 %collective-permute-start.10 = (bf16[1,4,128,256]{3,2,1,0:T(8,128)(2,1)S(1)}, bf16[1,4,128,256]{3,2,1,0:T(8,128)(2,1)S(1)}, u32[]{:S(2)}, u32[]{:S(2)}) collective-permute-start(bf16[1,4,128,256]{3,2,1,0:T(8,128)(2,1)S(1)} %get-tuple-element.137), channel_id=1, source_target_pairs={{0,2},{1,3},{2,0},{3,1},{4,6},{5,7},{6,4},{7,5},{8,10},{9,11},{10,... | collective-permute-start | bytes 786440 | tf_op jit(solution)/shard_map/ppermute | solution.py:469
  48.6 3.3 %collective-permute-start.9 = (bf16[2,4,72,256]{3,2,1,0:T(8,128)(2,1)S(1)}, bf16[2,4,72,256]{3,2,1,0:T(8,128)(2,1)S(1)}, u32[]{:S(2)}, u32[]{:S(2)}) collective-permute-start(bf16[2,4,72,256]{3,2,1,0:T(8,128)(2,1)S(1)} %get-tuple-element.135), channel_id=1, source_target_pairs={{0,1},{1,0},{2,3},{3,2},{4,5},{5,4},{6,7},{7,6},{8,9},{9,8},{10,11... | collective-permute-start | bytes 884744 | tf_op jit(solution)/shard_map/ppermute | solution.py:469
  52.0 9.7 %collective-permute-start.11 = (bf16[2,128,256]{2,1,0:T(8,128)(2,1)S(1)}, bf16[2,128,256]{2,1,0:T(8,128)(2,1)S(1)}, u32[]{:S(2)}, u32[]{:S(2)}) collective-permute-start(bf16[2,128,256]{2,1,0:T(8,128)(2,1)S(1)} %get-tuple-element.139), channel_id=1, source_target_pairs={{0,4},{4,0},{8,12},{12,8},{1,5},{5,1},{9,13},{13,9},{2,6},{6,2},{1... | collective-permute-start | bytes 393224 | tf_op jit(solution)/shard_map/ppermute | solution.py:469
  55.0 5.2 %collective-permute-start.12 = (bf16[2,72,256]{2,1,0:T(8,128)(2,1)S(1)}, bf16[2,72,256]{2,1,0:T(8,128)(2,1)S(1)}, u32[]{:S(2)}, u32[]{:S(2)}) collective-permute-start(bf16[2,72,256]{2,1,0:T(8,128)(2,1)S(1)} %get-tuple-element.142), channel_id=1, source_target_pairs={{0,2},{1,3},{2,0},{3,1},{4,6},{5,7},{6,4},{7,5},{8,10},{9,11},{10,... | collective-permute-start | bytes 221192 | tf_op jit(solution)/shard_map/ppermute | solution.py:469
  55.6 4.7 %collective-permute-start.13 = (bf16[2,72,256]{2,1,0:T(8,128)(2,1)S(1)}, bf16[2,72,256]{2,1,0:T(8,128)(2,1)S(1)}, u32[]{:S(2)}, u32[]{:S(2)}) collective-permute-start(bf16[2,72,256]{2,1,0:T(8,128)(2,1)S(1)} %get-tuple-element.146), channel_id=1, source_target_pairs={{0,4},{4,0},{8,12},{12,8},{1,5},{5,1},{9,13},{13,9},{2,6},{6,2},{1... | collective-permute-start | bytes 221192 | tf_op jit(solution)/shard_map/ppermute | solution.py:469
  55.6 6.0 %collective-permute-start.14 = (bf16[2,72,256]{2,1,0:T(8,128)(2,1)S(1)}, bf16[2,72,256]{2,1,0:T(8,128)(2,1)S(1)}, u32[]{:S(2)}, u32[]{:S(2)}) collective-permute-start(bf16[2,72,256]{2,1,0:T(8,128)(2,1)S(1)} %get-tuple-element.147), channel_id=1, source_target_pairs={{0,6},{1,7},{2,4},{3,5},{4,2},{5,3},{6,0},{7,1},{8,14},{9,15},{10,... | collective-permute-start | bytes 221192 | tf_op jit(solution)/shard_map/ppermute | solution.py:469
  61.7 6.7 %collective-permute-start.15 = (bf16[200,256]{1,0:T(8,128)(2,1)S(1)}, bf16[200,256]{1,0:T(8,128)(2,1)S(1)}, u32[]{:S(2)}, u32[]{:S(2)}) collective-permute-start(bf16[200,256]{1,0:T(8,128)(2,1)S(1)} %get-tuple-element.149), channel_id=1, source_target_pairs={{0,8},{4,12},{8,0},{12,4},{1,9},{5,13},{9,1},{13,5},{2,10},{6,14},... | collective-permute-start | bytes 307208 | tf_op jit(solution)/shard_map/ppermute | solution.py:469
  63.1 19.0 %all-to-all-start.1 = ((bf16[16,64,256]{2,1,0:T(8,128)(2,1)}), bf16[16,64,256]{2,1,0:T(8,128)(2,1)S(1)}, u32[]{:S(2)}, u32[]{:S(2)}) async-start(bf16[16,64,256]{2,1,0:T(8,128)(2,1)} %bitcast.5), calls=%async_computation.1 | async-start | bytes 1048576 | tf_op jit(solution)/shard_map/all_to_all | solution.py:528
  68.5 7.9 %collective-permute-start.16 = (bf16[1,192,256]{2,1,0:T(8,128)(2,1)S(1)}, bf16[1,192,256]{2,1,0:T(8,128)(2,1)S(1)}, u32[]{:S(2)}, u32[]{:S(2)}) collective-permute-start(bf16[1,192,256]{2,1,0:T(8,128)(2,1)S(1)} %get-tuple-element.150), channel_id=1, source_target_pairs={{0,2},{1,3},{2,0},{3,1},{4,6},{5,7},{6,4},{7,5},{8,10},{9,11},{10,... | collective-permute-start | bytes 294920 | tf_op jit(solution)/shard_map/ppermute | solution.py:469
  69.8 12.4 %copy-start.8 = (s32[1,512]{1,0:T(1,128)S(1)}, s32[1,512]{1,0:T(1,128)}, u32[]{:S(2)}) copy-start(s32[1,512]{1,0:T(1,128)} %get-tuple-element.83.refs_0_) | copy-start | bytes 6148
  76.4 1.5 %collective-permute-start.17 = (bf16[2,192,256]{2,1,0:T(8,128)(2,1)S(1)}, bf16[2,192,256]{2,1,0:T(8,128)(2,1)S(1)}, u32[]{:S(2)}, u32[]{:S(2)}) collective-permute-start(bf16[2,192,256]{2,1,0:T(8,128)(2,1)S(1)} %constant_dynamic-update-slice_fusion.refs_0_), channel_id=1, source_target_pairs={{0,1},{1,0},{2,3},{3,2},{4,5},{5,4},{6,7},{7,6},{8,9},{9,8},{10,11... | collective-permute-start | bytes 589832 | tf_op jit(solution)/shard_map/ppermute | solution.py:469
  (5 other events, 18.8 us)

commit v5 on v4

--- a/solution.py
+++ b/solution.py
@@ -648,18 +648,18 @@
         )
     keep_qkv, send_qkv = qkv_grads
     got_qkv = permute(send_qkv, "sample", sample_size, 1)
+    back = lax.optimization_barrier((back, got_mlp))[0]
     keep_mlp, leaving = halve(keep_mlp[0], got_mlp[0], "leaf", 1, "leaf_mlp", 1.0)
     got_qkv, leaving = lax.optimization_barrier((got_qkv, leaving))
     quarter = (leaf_size // 2, qkv_rows, width)
     keep_qkv, send_sample, send_leaf, send_both = call(
         quarter_kernel, [(quarter, F32)] + [(quarter, BF16)] * 3, "quarter_qkv", 0.5, keep_qkv, got_qkv
     )
-    back = lax.optimization_barrier((back, leaving, send_sample))[0]
     returned = exchange(back, axes, peers)
     (grad_points,) = call(unpack_kernel, [((rows, width), BF16)], "unpack", 1, slot, returned, blocked=True)
     joined = (mlp_rows + qkv_rows, width)
     keep, leaving = call(
-        functools.partial(join_kernel, (2, 4)), [(joined, F32), (joined, BF16)], "leaf_last", 0.5,
+        functools.partial(join_kernel, (2, 4)), [(joined, F32), (joined, BF16)], "leaf_last", 0.1,
         keep_mlp, permute(leaving, "leaf", leaf_size, 1), keep_qkv,
         permute(send_sample, "sample", sample_size, 2),
         permute(send_leaf, "leaf", leaf_size, 1),
@@ -667,7 +667,7 @@
     )
     got = permute(leaving, "leaf", leaf_size, 2)
     low, gains = call(
-        finish_kernel, [((1, mlp_rows + qkv_rows - GAINS, width), BF16), ((GAINS, width), F32)], "finish", 3.5, keep, got
+        finish_kernel, [((1, mlp_rows + qkv_rows - GAINS, width), BF16), ((GAINS, width), F32)], "finish", 0.1, keep, got
     )
     offsets = [0]
     bit = sample_size // 2
@@ -675,6 +675,7 @@
         low = jnp.concatenate([low, permute(low, "sample", sample_size, bit)], axis=0)
         offsets += [offset ^ bit for offset in offsets]
         bit //= 2
+    low, grad_points = lax.optimization_barrier((low, grad_points))
     mate = permute(low, "sample", sample_size, 1)
     share = width // leaf_size
     gains = lax.dynamic_slice(gains, (0, lax.axis_index("leaf") * share), (2, share)) * inv_root

time: 83.7 us -> 91.6 us (1.094)
  waiting for transfers between devices: 25.5 us -> 33.2 us
    ppermute x18, waiting for transfers between devices: 22.2 us -> 33.2 us  [permute(): return lax.ppermute(value, axis, [(i, i ^ bit) for i in range(size)])]
    all_to_all x2, waiting for transfers between devices: 3.28 us -> 0.01 us  [exchange(): lax.all_to_all(flat.reshape((peers, -1) + flat.shape[1:]), axes, split_ax...]
  transfers between devices with their start and end apart: 20 -> 20, of which waited for: 13 -> 13; matrix products, arithmetic and copies ran while one was open for 1% -> 1% of each run, Pallas kernels for 14% -> 12%
where the time goes in v5:
time: 91.6 us; the launch traced here: 91.2 us
  starting transfers between devices  37.2 us (41%)
  waiting for transfers between devices  33.2 us (36%)
  Pallas kernels  18.6 us (20%)
  local copies, waits for them, and re-layouts  1.23 us (1%)
    ppermute x18, waiting for transfers between devices, permute(): return lax.ppermute(value, axis, [(i, i ^ bit) for i in range(size)])  33.2 us
    ppermute x18, starting transfers between devices, permute(): return lax.ppermute(value, axis, [(i, i ^ bit) for i in range(size)])  25 us
    pallas_call x15, Pallas kernels, call(): pl.pallas_call(body, out_shape=[jax.ShapeDtypeStruct(shape, dtype) for sh...  18.6 us
    all_to_all x2, starting transfers between devices, exchange(): lax.all_to_all(flat.reshape((peers, -1) + flat.shape[1:]), axes, split_ax...  12.3 us
  transfers between devices with their start and end apart: 20, of which 13 were waited for; matrix products, arithmetic and copies ran while one was open for 1% of the time, Pallas kernels for 12%

profile of v5, /device:TPU:0, one launch (start us, length us, event | category | flops | bytes accessed | tf_op | source)
XLA Modules:
  0.0 91.2 jit_solution(9734556173792492617)
XLA Ops:
  0.6 2.6 %pack_points.1 = (s32[1,512]{1,0:T(1,128)}, bf16[16,144,128]{2,1,0:T(8,128)(2,1)}) custom-call(s32[1,512]{1,0:T(1,128)} %bitcast.16, bf16[512,256]{1,0:T(8,128)(2,1)} %refs_1_.3), custom_call_target="tpu_custom_call" | custom-call | flops 2200000000 | bytes 856064 | tf_op jit(solution)/shard_map/pack_points/pallas_call | solution.py:515
  3.2 7.4 %all-to-all-start = ((bf16[16,144,128]{2,1,0:T(8,128)(2,1)}), bf16[16,144,128]{2,1,0:T(8,128)(2,1)S(1)}, u32[]{:S(2)}, u32[]{:S(2)}) async-start(bf16[16,144,128]{2,1,0:T(8,128)(2,1)} %get-tuple-element.88), calls=%async_computation | async-start | bytes 1179648 | tf_op jit(solution)/shard_map/all_to_all | solution.py:528
  11.8 2.0 %collective-permute-start = (bf16[2,64,256]{2,1,0:T(8,128)(2,1)S(1)}, bf16[2,64,256]{2,1,0:T(8,128)(2,1)S(1)}, u32[]{:S(2)}, u32[]{:S(2)}) collective-permute-start(bf16[2,64,256]{2,1,0:T(8,128)(2,1)S(1)} %get-tuple-element.86), channel_id=1, source_target_pairs={{0,2},{1,3},{2,0},{3,1},{4,6},{5,7},{6,4},{7,5},{8,10},{9,11},{10,... | collective-permute-start | bytes 196616 | tf_op jit(solution)/shard_map/ppermute | solution.py:469
  13.8 1.5 %collective-permute-start.1 = (bf16[2,64,256]{2,1,0:T(8,128)(2,1)S(1)}, bf16[2,64,256]{2,1,0:T(8,128)(2,1)S(1)}, u32[]{:S(2)}, u32[]{:S(2)}) collective-permute-start(bf16[2,64,256]{2,1,0:T(8,128)(2,1)S(1)} %get-tuple-element.87), channel_id=1, source_target_pairs={{0,4},{1,5},{2,6},{3,7},{4,0},{5,1},{6,2},{7,3},{8,12},{9,13},{10,... | collective-permute-start | bytes 196616 | tf_op jit(solution)/shard_map/ppermute | solution.py:469
  15.3 2.8 %collective-permute-start.3 = (bf16[2,64,256]{2,1,0:T(8,128)(2,1)S(1)}, bf16[2,64,256]{2,1,0:T(8,128)(2,1)S(1)}, u32[]{:S(2)}, u32[]{:S(2)}) collective-permute-start(bf16[2,64,256]{2,1,0:T(8,128)(2,1)S(1)} %get-tuple-element.100), channel_id=1, source_target_pairs={{0,8},{1,9},{2,10},{3,11},{4,12},{5,13},{6,14},{7,15},{8,0},{9,1},... | collective-permute-start | bytes 196616 | tf_op jit(solution)/shard_map/ppermute | solution.py:469
  18.1 1.5 %collective-permute-start.4 = (bf16[2,64,256]{2,1,0:T(8,128)(2,1)S(1)}, bf16[2,64,256]{2,1,0:T(8,128)(2,1)S(1)}, u32[]{:S(2)}, u32[]{:S(2)}) collective-permute-start(bf16[2,64,256]{2,1,0:T(8,128)(2,1)S(1)} %get-tuple-element.101), channel_id=1, source_target_pairs={{0,10},{1,11},{2,8},{3,9},{4,14},{5,15},{6,12},{7,13},{8,2},{9,3},... | collective-permute-start | bytes 196616 | tf_op jit(solution)/shard_map/ppermute | solution.py:469
  19.6 3.3 %collective-permute-start.5 = (bf16[2,64,256]{2,1,0:T(8,128)(2,1)S(1)}, bf16[2,64,256]{2,1,0:T(8,128)(2,1)S(1)}, u32[]{:S(2)}, u32[]{:S(2)}) collective-permute-start(bf16[2,64,256]{2,1,0:T(8,128)(2,1)S(1)} %get-tuple-element.102), channel_id=1, source_target_pairs={{0,12},{1,13},{2,14},{3,15},{4,8},{5,9},{6,10},{7,11},{8,4},{9,5},... | collective-permute-start | bytes 196616 | tf_op jit(solution)/shard_map/ppermute | solution.py:469
  23.6 4.0 %collective-permute-start.6 = (bf16[2,64,256]{2,1,0:T(8,128)(2,1)S(1)}, bf16[2,64,256]{2,1,0:T(8,128)(2,1)S(1)}, u32[]{:S(2)}, u32[]{:S(2)}) collective-permute-start(bf16[2,64,256]{2,1,0:T(8,128)(2,1)S(1)} %get-tuple-element.103), channel_id=1, source_target_pairs={{0,14},{1,15},{2,12},{3,13},{4,10},{5,11},{6,8},{7,9},{8,6},{9,7},... | collective-permute-start | bytes 196616 | tf_op jit(solution)/shard_map/ppermute | solution.py:469
  28.1 4.5 %forward.1 = (bf16[768,512]{1,0:T(8,128)(2,1)S(1)}, bf16[512,512]{1,0:T(8,128)(2,1)S(1)}, f32[8,512]{1,0:T(8,128)S(1)}, f32[256,512]{1,0:T(8,128)S(1)}, bf16[256...) custom-call(f32[256,512]{1,0:T(8,128)S(1)} %get-tuple-element.91.ref, ...), custom_call_target="tpu_custom_call" | custom-call | flops 7699999744 | bytes 12339200 | tf_op jit(solution)/shard_map/forward/pallas_call | solution.py:515
  32.7 2.1 %collective-permute-done.3.refs_4_ = bf16[2,64,256]{2,1,0:T(8,128)(2,1)S(1)} collective-permute-done((bf16[2,64,256]{2,1,0:T(8,128)(2,1)S(1)}, bf16[2,64,256]{2,1,0:T(8,128)(2,1)S(1)}, u32[]{:S(2)}, u32[]{:S(2)}) %collective-permute-start.3) | collective-permute-done | bytes 65568 | tf_op jit(solution)/shard_map/ppermute | solution.py:469
  34.8 2.3 %collective-permute-done.4.refs_5_ = bf16[2,64,256]{2,1,0:T(8,128)(2,1)S(1)} collective-permute-done((bf16[2,64,256]{2,1,0:T(8,128)(2,1)S(1)}, bf16[2,64,256]{2,1,0:T(8,128)(2,1)S(1)}, u32[]{:S(2)}, u32[]{:S(2)}) %collective-permute-start.4) | collective-permute-done | bytes 65568 | tf_op jit(solution)/shard_map/ppermute | solution.py:469
  37.3 1.5 %collective-permute-done.7.refs_6_ = bf16[8,64,256]{2,1,0:T(8,128)(2,1)S(1)} collective-permute-done((bf16[8,64,256]{2,1,0:T(8,128)(2,1)S(1)}, bf16[8,64,256]{2,1,0:T(8,128)(2,1)S(1)}, u32[]{:S(2)}, u32[]{:S(2)}) %collective-permute-start.7) | collective-permute-done | bytes 262176 | tf_op jit(solution)/shard_map/ppermute | solution.py:469
  38.8 2.6 %mlp_weights.1 = (bf16[1024,512]{1,0:T(8,128)(2,1)S(1)}, f32[256,512]{1,0:T(8,128)S(1)}, f32[2,4,128,256]{3,2,1,0:T(8,128)S(1)}, bf16[2,4,128,256]{3,2,1,0:T(8,128)(2,1)S(1)}) custom-call(s32[1,1024]{1,0:T(1,128)S(1)} %get-tuple-element.90.refs_0_, bf16[1024,512]{1,0:T(8,128)(2,1)S(1)} %get-tuple-element.92.refs_1_, ...), custom_call_target="tpu_custom_call" | custom-call | flops 2750000128 | bytes 7606272 | tf_op jit(solution)/shard_map/mlp_weights/pallas_call | solution.py:515
  44.0 4.6 %attention_backward.1 = (bf16[1024,256]{1,0:T(8,128)(2,1)}, f32[2,4,72,256]{3,2,1,0:T(8,128)S(1)}, bf16[2,4,72,256]{3,2,1,0:T(8,128)(2,1)S(1)}) custom-call(bf16[768,512]{1,0:T(8,128)(2,1)S(1)} %get-tuple-element.127.refs_0_, bf16[512,512]{1,0:T(8,128)(2,1)S(1)} %get-tuple-element.128.refs_1_, f32[8,512]{1,0:T(8,128)S(1)} %get-tuple-element.120.refs_3_.refs_2_, ...), custom_call_target="tpu_custom_call" | custom-call | flops 6600000000 | bytes 9815040 | tf_op jit(solution)/shard_map/attention_backward/pallas_call | solution.py:515
  48.6 3.3 %collective-permute-done.9 = bf16[1,4,128,256]{3,2,1,0:T(8,128)(2,1)S(1)} collective-permute-done((bf16[1,4,128,256]{3,2,1,0:T(8,128)(2,1)S(1)}, bf16[1,4,128,256]{3,2,1,0:T(8,128)(2,1)S(1)}, u32[]{:S(2)}, u32[]{:S(2)}) %collective-permute-start.9) | collective-permute-done | bytes 262176 | tf_op jit(solution)/shard_map/ppermute | solution.py:469
  51.9 4.9 %all-to-all-start.1 = ((bf16[16,64,256]{2,1,0:T(8,128)(2,1)}), bf16[16,64,256]{2,1,0:T(8,128)(2,1)S(1)}, u32[]{:S(2)}, u32[]{:S(2)}) async-start(bf16[16,64,256]{2,1,0:T(8,128)(2,1)} %bitcast.5), calls=%async_computation.1 | async-start | bytes 1048576 | tf_op jit(solution)/shard_map/all_to_all | solution.py:528
  58.5 1.9 %collective-permute-start.11 = (bf16[2,128,256]{2,1,0:T(8,128)(2,1)S(1)}, bf16[2,128,256]{2,1,0:T(8,128)(2,1)S(1)}, u32[]{:S(2)}, u32[]{:S(2)}) collective-permute-start(bf16[2,128,256]{2,1,0:T(8,128)(2,1)S(1)} %get-tuple-element.141), channel_id=1, source_target_pairs={{0,4},{4,0},{8,12},{12,8},{1,5},{5,1},{9,13},{13,9},{2,6},{6,2},{1... | collective-permute-start | bytes 393224 | tf_op jit(solution)/shard_map/ppermute | solution.py:469
  60.4 1.5 %collective-permute-start.12 = (bf16[2,72,256]{2,1,0:T(8,128)(2,1)S(1)}, bf16[2,72,256]{2,1,0:T(8,128)(2,1)S(1)}, u32[]{:S(2)}, u32[]{:S(2)}) collective-permute-start(bf16[2,72,256]{2,1,0:T(8,128)(2,1)S(1)} %get-tuple-element.145), channel_id=1, source_target_pairs={{0,2},{1,3},{2,0},{3,1},{4,6},{5,7},{6,4},{7,5},{8,10},{9,11},{10,... | collective-permute-start | bytes 221192 | tf_op jit(solution)/shard_map/ppermute | solution.py:469
  62.5 1.5 %collective-permute-start.14 = (bf16[2,72,256]{2,1,0:T(8,128)(2,1)S(1)}, bf16[2,72,256]{2,1,0:T(8,128)(2,1)S(1)}, u32[]{:S(2)}, u32[]{:S(2)}) collective-permute-start(bf16[2,72,256]{2,1,0:T(8,128)(2,1)S(1)} %get-tuple-element.147), channel_id=1, source_target_pairs={{0,6},{1,7},{2,4},{3,5},{4,2},{5,3},{6,0},{7,1},{8,14},{9,15},{10,... | collective-permute-start | bytes 221192 | tf_op jit(solution)/shard_map/ppermute | solution.py:469
  65.3 7.9 %collective-permute-done.13.refs_4_ = bf16[2,72,256]{2,1,0:T(8,128)(2,1)S(1)} collective-permute-done((bf16[2,72,256]{2,1,0:T(8,128)(2,1)S(1)}, bf16[2,72,256]{2,1,0:T(8,128)(2,1)S(1)}, u32[]{:S(2)}, u32[]{:S(2)}) %collective-permute-start.13) | collective-permute-done | bytes 73760 | tf_op jit(solution)/shard_map/ppermute | solution.py:469
  73.2 2.0 %collective-permute-done.14.refs_5_ = bf16[2,72,256]{2,1,0:T(8,128)(2,1)S(1)} collective-permute-done((bf16[2,72,256]{2,1,0:T(8,128)(2,1)S(1)}, bf16[2,72,256]{2,1,0:T(8,128)(2,1)S(1)}, u32[]{:S(2)}, u32[]{:S(2)}) %collective-permute-start.14) | collective-permute-done | bytes 73760 | tf_op jit(solution)/shard_map/ppermute | solution.py:469
  75.3 2.5 %collective-permute-start.15 = (bf16[200,256]{1,0:T(8,128)(2,1)S(1)}, bf16[200,256]{1,0:T(8,128)(2,1)S(1)}, u32[]{:S(2)}, u32[]{:S(2)}) collective-permute-start(bf16[200,256]{1,0:T(8,128)(2,1)S(1)} %get-tuple-element.149), channel_id=1, source_target_pairs={{0,8},{4,12},{8,0},{12,4},{1,9},{5,13},{9,1},{13,5},{2,10},{6,14},... | collective-permute-start | bytes 307208 | tf_op jit(solution)/shard_map/ppermute | solution.py:469
  77.9 5.0 %collective-permute-done.15.refs_1_ = bf16[200,256]{1,0:T(8,128)(2,1)S(1)} collective-permute-done((bf16[200,256]{1,0:T(8,128)(2,1)S(1)}, bf16[200,256]{1,0:T(8,128)(2,1)S(1)}, u32[]{:S(2)}, u32[]{:S(2)}) %collective-permute-start.15) | collective-permute-done | bytes 102432 | tf_op jit(solution)/shard_map/ppermute | solution.py:469
  83.6 4.0 %collective-permute-done.16 = bf16[1,192,256]{2,1,0:T(8,128)(2,1)S(1)} collective-permute-done((bf16[1,192,256]{2,1,0:T(8,128)(2,1)S(1)}, bf16[1,192,256]{2,1,0:T(8,128)(2,1)S(1)}, u32[]{:S(2)}, u32[]{:S(2)}) %collective-permute-start.16) | collective-permute-done | bytes 98336 | tf_op jit(solution)/shard_map/ppermute | solution.py:469
  (52 shorter events, 13.3 us)
Async XLA Ops:
  0.6 10.0 %copy-start.3 = (bf16[512,256]{1,0:T(8,128)(2,1)S(1)}, bf16[512,256]{1,0:T(8,128)(2,1)}, u32[]{:S(2)}) copy-start(bf16[512,256]{1,0:T(8,128)(2,1)} %refs_1_.4) | copy-start | bytes 786436
  3.2 24.3 %all-to-all-start = ((bf16[16,144,128]{2,1,0:T(8,128)(2,1)}), bf16[16,144,128]{2,1,0:T(8,128)(2,1)S(1)}, u32[]{:S(2)}, u32[]{:S(2)}) async-start(bf16[16,144,128]{2,1,0:T(8,128)(2,1)} %get-tuple-element.88), calls=%async_computation | async-start | bytes 1179648 | tf_op jit(solution)/shard_map/all_to_all | solution.py:528
  11.8 7.8 %collective-permute-start = (bf16[2,64,256]{2,1,0:T(8,128)(2,1)S(1)}, bf16[2,64,256]{2,1,0:T(8,128)(2,1)S(1)}, u32[]{:S(2)}, u32[]{:S(2)}) collective-permute-start(bf16[2,64,256]{2,1,0:T(8,128)(2,1)S(1)} %get-tuple-element.86), channel_id=1, source_target_pairs={{0,2},{1,3},{2,0},{3,1},{4,6},{5,7},{6,4},{7,5},{8,10},{9,11},{10,... | collective-permute-start | bytes 196616 | tf_op jit(solution)/shard_map/ppermute | solution.py:469
  13.8 9.8 %collective-permute-start.1 = (bf16[2,64,256]{2,1,0:T(8,128)(2,1)S(1)}, bf16[2,64,256]{2,1,0:T(8,128)(2,1)S(1)}, u32[]{:S(2)}, u32[]{:S(2)}) collective-permute-start(bf16[2,64,256]{2,1,0:T(8,128)(2,1)S(1)} %get-tuple-element.87), channel_id=1, source_target_pairs={{0,4},{1,5},{2,6},{3,7},{4,0},{5,1},{6,2},{7,3},{8,12},{9,13},{10,... | collective-permute-start | bytes 196616 | tf_op jit(solution)/shard_map/ppermute | solution.py:469
  15.2 17.5 %collective-permute-start.2 = (bf16[2,64,256]{2,1,0:T(8,128)(2,1)S(1)}, bf16[2,64,256]{2,1,0:T(8,128)(2,1)S(1)}, u32[]{:S(2)}, u32[]{:S(2)}) collective-permute-start(bf16[2,64,256]{2,1,0:T(8,128)(2,1)S(1)} %get-tuple-element.99), channel_id=1, source_target_pairs={{0,6},{1,7},{2,4},{3,5},{4,2},{5,3},{6,0},{7,1},{8,14},{9,15},{10,... | collective-permute-start | bytes 196616 | tf_op jit(solution)/shard_map/ppermute | solution.py:469
  15.3 19.5 %collective-permute-start.3 = (bf16[2,64,256]{2,1,0:T(8,128)(2,1)S(1)}, bf16[2,64,256]{2,1,0:T(8,128)(2,1)S(1)}, u32[]{:S(2)}, u32[]{:S(2)}) collective-permute-start(bf16[2,64,256]{2,1,0:T(8,128)(2,1)S(1)} %get-tuple-element.100), channel_id=1, source_target_pairs={{0,8},{1,9},{2,10},{3,11},{4,12},{5,13},{6,14},{7,15},{8,0},{9,1},... | collective-permute-start | bytes 196616 | tf_op jit(solution)/shard_map/ppermute | solution.py:469
  18.1 19.0 %collective-permute-start.4 = (bf16[2,64,256]{2,1,0:T(8,128)(2,1)S(1)}, bf16[2,64,256]{2,1,0:T(8,128)(2,1)S(1)}, u32[]{:S(2)}, u32[]{:S(2)}) collective-permute-start(bf16[2,64,256]{2,1,0:T(8,128)(2,1)S(1)} %get-tuple-element.101), channel_id=1, source_target_pairs={{0,10},{1,11},{2,8},{3,9},{4,14},{5,15},{6,12},{7,13},{8,2},{9,3},... | collective-permute-start | bytes 196616 | tf_op jit(solution)/shard_map/ppermute | solution.py:469
  19.6 17.5 %collective-permute-start.5 = (bf16[2,64,256]{2,1,0:T(8,128)(2,1)S(1)}, bf16[2,64,256]{2,1,0:T(8,128)(2,1)S(1)}, u32[]{:S(2)}, u32[]{:S(2)}) collective-permute-start(bf16[2,64,256]{2,1,0:T(8,128)(2,1)S(1)} %get-tuple-element.102), channel_id=1, source_target_pairs={{0,12},{1,13},{2,14},{3,15},{4,8},{5,9},{6,10},{7,11},{8,4},{9,5},... | collective-permute-start | bytes 196616 | tf_op jit(solution)/shard_map/ppermute | solution.py:469
  23.6 4.6 %copy-start.6 = (f32[256]{0:T(256)S(1)}, f32[256]{0:T(256)}, u32[]{:S(2)}) copy-start(f32[256]{0:T(256)} %param.17) | copy-start | bytes 3076
  23.6 13.6 %collective-permute-start.6 = (bf16[2,64,256]{2,1,0:T(8,128)(2,1)S(1)}, bf16[2,64,256]{2,1,0:T(8,128)(2,1)S(1)}, u32[]{:S(2)}, u32[]{:S(2)}) collective-permute-start(bf16[2,64,256]{2,1,0:T(8,128)(2,1)S(1)} %get-tuple-element.103), channel_id=1, source_target_pairs={{0,14},{1,15},{2,12},{3,13},{4,10},{5,11},{6,8},{7,9},{8,6},{9,7},... | collective-permute-start | bytes 196616 | tf_op jit(solution)/shard_map/ppermute | solution.py:469
  28.1 10.7 %copy-start = (bf16[1024,256]{1,0:T(8,128)(2,1)S(1)}, bf16[1024,256]{1,0:T(8,128)(2,1)}, u32[]{:S(2)}) copy-start(bf16[1024,256]{1,0:T(8,128)(2,1)} %refs_4_.1) | copy-start | bytes 1572868
  37.2 1.6 %collective-permute-start.7 = (bf16[8,64,256]{2,1,0:T(8,128)(2,1)S(1)}, bf16[8,64,256]{2,1,0:T(8,128)(2,1)S(1)}, u32[]{:S(2)}, u32[]{:S(2)}) collective-permute-start(bf16[8,64,256]{2,1,0:T(8,128)(2,1)S(1)} %get-tuple-element.113), channel_id=1, source_target_pairs={{0,1},{1,0},{2,3},{3,2},{4,5},{5,4},{6,7},{7,6},{8,9},{9,8},{10,11... | collective-permute-start | bytes 786440 | tf_op jit(solution)/shard_map/ppermute | solution.py:469
  41.4 2.0 %collective-permute-start.8 = (bf16[2,4,128,256]{3,2,1,0:T(8,128)(2,1)S(1)}, bf16[2,4,128,256]{3,2,1,0:T(8,128)(2,1)S(1)}, u32[]{:S(2)}, u32[]{:S(2)}) collective-permute-start(bf16[2,4,128,256]{3,2,1,0:T(8,128)(2,1)S(1)} %get-tuple-element.115), channel_id=1, source_target_pairs={{0,1},{1,0},{2,3},{3,2},{4,5},{5,4},{6,7},{7,6},{8,9},{9,8},{10,11... | collective-permute-start | bytes 1572872 | tf_op jit(solution)/shard_map/ppermute | solution.py:469
  43.5 8.5 %collective-permute-start.9 = (bf16[1,4,128,256]{3,2,1,0:T(8,128)(2,1)S(1)}, bf16[1,4,128,256]{3,2,1,0:T(8,128)(2,1)S(1)}, u32[]{:S(2)}, u32[]{:S(2)}) collective-permute-start(bf16[1,4,128,256]{3,2,1,0:T(8,128)(2,1)S(1)} %get-tuple-element.125), channel_id=1, source_target_pairs={{0,2},{1,3},{2,0},{3,1},{4,6},{5,7},{6,4},{7,5},{8,10},{9,11},{10,... | collective-permute-start | bytes 786440 | tf_op jit(solution)/shard_map/ppermute | solution.py:469
  51.9 35.7 %all-to-all-start.1 = ((bf16[16,64,256]{2,1,0:T(8,128)(2,1)}), bf16[16,64,256]{2,1,0:T(8,128)(2,1)S(1)}, u32[]{:S(2)}, u32[]{:S(2)}) async-start(bf16[16,64,256]{2,1,0:T(8,128)(2,1)} %bitcast.5), calls=%async_computation.1 | async-start | bytes 1048576 | tf_op jit(solution)/shard_map/all_to_all | solution.py:528
  56.8 1.6 %collective-permute-start.10 = (bf16[2,4,72,256]{3,2,1,0:T(8,128)(2,1)S(1)}, bf16[2,4,72,256]{3,2,1,0:T(8,128)(2,1)S(1)}, u32[]{:S(2)}, u32[]{:S(2)}) collective-permute-start(bf16[2,4,72,256]{3,2,1,0:T(8,128)(2,1)S(1)} %get-tuple-element.139), channel_id=1, source_target_pairs={{0,1},{1,0},{2,3},{3,2},{4,5},{5,4},{6,7},{7,6},{8,9},{9,8},{10,11... | collective-permute-start | bytes 884744 | tf_op jit(solution)/shard_map/ppermute | solution.py:469
  57.3 30.4 %copy-start.8 = (s32[1,512]{1,0:T(1,128)S(1)}, s32[1,512]{1,0:T(1,128)}, u32[]{:S(2)}) copy-start(s32[1,512]{1,0:T(1,128)} %get-tuple-element.85.refs_0_) | copy-start | bytes 6148
  58.5 16.8 %collective-permute-start.11 = (bf16[2,128,256]{2,1,0:T(8,128)(2,1)S(1)}, bf16[2,128,256]{2,1,0:T(8,128)(2,1)S(1)}, u32[]{:S(2)}, u32[]{:S(2)}) collective-permute-start(bf16[2,128,256]{2,1,0:T(8,128)(2,1)S(1)} %get-tuple-element.141), channel_id=1, source_target_pairs={{0,4},{4,0},{8,12},{12,8},{1,5},{5,1},{9,13},{13,9},{2,6},{6,2},{1... | collective-permute-start | bytes 393224 | tf_op jit(solution)/shard_map/ppermute | solution.py:469
  60.4 4.9 %collective-permute-start.12 = (bf16[2,72,256]{2,1,0:T(8,128)(2,1)S(1)}, bf16[2,72,256]{2,1,0:T(8,128)(2,1)S(1)}, u32[]{:S(2)}, u32[]{:S(2)}) collective-permute-start(bf16[2,72,256]{2,1,0:T(8,128)(2,1)S(1)} %get-tuple-element.145), channel_id=1, source_target_pairs={{0,2},{1,3},{2,0},{3,1},{4,6},{5,7},{6,4},{7,5},{8,10},{9,11},{10,... | collective-permute-start | bytes 221192 | tf_op jit(solution)/shard_map/ppermute | solution.py:469
  61.9 11.3 %collective-permute-start.13 = (bf16[2,72,256]{2,1,0:T(8,128)(2,1)S(1)}, bf16[2,72,256]{2,1,0:T(8,128)(2,1)S(1)}, u32[]{:S(2)}, u32[]{:S(2)}) collective-permute-start(bf16[2,72,256]{2,1,0:T(8,128)(2,1)S(1)} %get-tuple-element.146), channel_id=1, source_target_pairs={{0,4},{4,0},{8,12},{12,8},{1,5},{5,1},{9,13},{13,9},{2,6},{6,2},{1... | collective-permute-start | bytes 221192 | tf_op jit(solution)/shard_map/ppermute | solution.py:469
  62.5 12.8 %collective-permute-start.14 = (bf16[2,72,256]{2,1,0:T(8,128)(2,1)S(1)}, bf16[2,72,256]{2,1,0:T(8,128)(2,1)S(1)}, u32[]{:S(2)}, u32[]{:S(2)}) collective-permute-start(bf16[2,72,256]{2,1,0:T(8,128)(2,1)S(1)} %get-tuple-element.147), channel_id=1, source_target_pairs={{0,6},{1,7},{2,4},{3,5},{4,2},{5,3},{6,0},{7,1},{8,14},{9,15},{10,... | collective-permute-start | bytes 221192 | tf_op jit(solution)/shard_map/ppermute | solution.py:469
  75.3 7.6 %collective-permute-start.15 = (bf16[200,256]{1,0:T(8,128)(2,1)S(1)}, bf16[200,256]{1,0:T(8,128)(2,1)S(1)}, u32[]{:S(2)}, u32[]{:S(2)}) collective-permute-start(bf16[200,256]{1,0:T(8,128)(2,1)S(1)} %get-tuple-element.149), channel_id=1, source_target_pairs={{0,8},{4,12},{8,0},{12,4},{1,9},{5,13},{9,1},{13,5},{2,10},{6,14},... | collective-permute-start | bytes 307208 | tf_op jit(solution)/shard_map/ppermute | solution.py:469
  82.9 4.7 %collective-permute-start.16 = (bf16[1,192,256]{2,1,0:T(8,128)(2,1)S(1)}, bf16[1,192,256]{2,1,0:T(8,128)(2,1)S(1)}, u32[]{:S(2)}, u32[]{:S(2)}) collective-permute-start(bf16[1,192,256]{2,1,0:T(8,128)(2,1)S(1)} %get-tuple-element.150), channel_id=1, source_target_pairs={{0,2},{1,3},{2,0},{3,1},{4,6},{5,7},{6,4},{7,5},{8,10},{9,11},{10,... | collective-permute-start | bytes 294920 | tf_op jit(solution)/shard_map/ppermute | solution.py:469
  88.9 1.4 %collective-permute-start.17 = (bf16[2,192,256]{2,1,0:T(8,128)(2,1)S(1)}, bf16[2,192,256]{2,1,0:T(8,128)(2,1)S(1)}, u32[]{:S(2)}, u32[]{:S(2)}) collective-permute-start(bf16[2,192,256]{2,1,0:T(8,128)(2,1)S(1)} %pad_maximum_fusion.refs_0_), channel_id=1, source_target_pairs={{0,1},{1,0},{2,3},{3,2},{4,5},{5,4},{6,7},{7,6},{8,9},{9,8},{10,11... | collective-permute-start | bytes 589832 | tf_op jit(solution)/shard_map/ppermute | solution.py:469
  (5 other events, 18.8 us)

commit v6 on v4

--- a/solution.py
+++ b/solution.py
@@ -407,17 +407,21 @@
     mine = lax.rem(lax.div(lax.axis_index(axis), bit), 2)
     for high in range(keep_out_ref.shape[0]):
         for ref, at in ((keep_out_ref, 2 * high + mine), (send_out_ref, 2 * high + 1 - mine)):
-            ref[high] = (keep_ref[at] + got_ref[at].astype(F32)).astype(ref.dtype)
-
-
-def quarter_kernel(keep_ref, got_ref, keep_out_ref, *send_refs):
+            here = (at, slice(None), slice(0, ref.shape[2])) if len(ref.shape) == 4 else (at,)
+            ref[high] = (keep_ref[here] + got_ref[here].astype(F32)).astype(ref.dtype)
+
+
+def quarter_kernel(skip, keep_mlp_ref, got_mlp_ref, keep_qkv_ref, got_qkv_ref, keep_out_ref, *send_refs):
     mine = lax.rem(lax.div(lax.axis_index("sample"), 2), 2)
     low = lax.rem(lax.axis_index("leaf"), 2)
     places = ((mine, low), (1 - mine, low), (mine, 1 - low), (1 - mine, 1 - low))
+    count = keep_mlp_ref.shape[2] - skip
     for ref, (sample, leaf) in zip((keep_out_ref, *send_refs), places):
         for high in range(ref.shape[0]):
-            total = keep_ref[sample, 2 * high + leaf] + got_ref[sample, 2 * high + leaf].astype(F32)
-            ref[high] = total.astype(ref.dtype)
+            at = (sample, 2 * high + leaf)
+            rest = at + (slice(skip, None),)
+            ref[high, :count, :] = (keep_mlp_ref[rest] + got_mlp_ref[rest].astype(F32)).astype(ref.dtype)
+            ref[high, count:, :] = (keep_qkv_ref[at] + got_qkv_ref[at].astype(F32)).astype(ref.dtype)
 
 
 def join_kernel(counts, *refs):
@@ -469,8 +473,10 @@
     return lax.ppermute(value, axis, [(i, i ^ bit) for i in range(size)])
 
 
-def halve(keep, got, axis, bit, name, micros=0.5):
+def halve(keep, got, axis, bit, name, micros=0.5, rows=None):
     shape = (keep.shape[0] // 2,) + keep.shape[1:]
+    if rows is not None:
+        shape = shape[:2] + (rows,) + shape[3:]
     return call(functools.partial(halve_kernel, axis, bit), [(shape, F32), (shape, BF16)], name, micros, keep, got)
 
 
@@ -623,13 +629,11 @@
     )
     if arranged:
         keep_mlp, send_mlp = mlp_grads
-        got_mlp = permute(send_mlp, "sample", sample_size, 1)
-        bit = 2
-        while bit < sample_size:
-            keep_mlp, send_mlp = halve(keep_mlp, got_mlp, "sample", bit, "halve_mlp")
-            grad_att, send_mlp = lax.optimization_barrier((grad_att, send_mlp))
-            got_mlp = permute(send_mlp, "sample", sample_size, bit)
-            bit *= 2
+        arrived_mlp = permute(send_mlp, "sample", sample_size, 1)
+        up_rows = width // leaf_size
+        keep_up, send_up = halve(keep_mlp, arrived_mlp, "sample", 2, "halve_up", rows=up_rows)
+        grad_att, send_up = lax.optimization_barrier((grad_att, send_up))
+        got_up = permute(send_up, "sample", sample_size, 2)
     back, *qkv_grads = call(
         functools.partial(attention_backward_kernel, arranged),
         [((slots, width), BF16)] + qkv_mats, "attention_backward", 6,
@@ -648,11 +652,12 @@
         )
     keep_qkv, send_qkv = qkv_grads
     got_qkv = permute(send_qkv, "sample", sample_size, 1)
-    keep_mlp, leaving = halve(keep_mlp[0], got_mlp[0], "leaf", 1, "leaf_mlp", 1.0)
+    keep_up, leaving = halve(keep_up[0], got_up[0], "leaf", 1, "leaf_up", 2.0)
     got_qkv, leaving = lax.optimization_barrier((got_qkv, leaving))
-    quarter = (leaf_size // 2, qkv_rows, width)
+    quarter = (leaf_size // 2, mlp_rows - up_rows + qkv_rows, width)
     keep_qkv, send_sample, send_leaf, send_both = call(
-        quarter_kernel, [(quarter, F32)] + [(quarter, BF16)] * 3, "quarter_qkv", 0.5, keep_qkv, got_qkv
+        functools.partial(quarter_kernel, up_rows), [(quarter, F32)] + [(quarter, BF16)] * 3, "quarter", 0.5,
+        keep_mlp, arrived_mlp, keep_qkv, got_qkv,
     )
     back = lax.optimization_barrier((back, leaving, send_sample))[0]
     returned = exchange(back, axes, peers)
@@ -660,7 +665,7 @@
     joined = (mlp_rows + qkv_rows, width)
     keep, leaving = call(
         functools.partial(join_kernel, (2, 4)), [(joined, F32), (joined, BF16)], "leaf_last", 0.5,
-        keep_mlp, permute(leaving, "leaf", leaf_size, 1), keep_qkv,
+        keep_up, permute(leaving, "leaf", leaf_size, 1), keep_qkv,
         permute(send_sample, "sample", sample_size, 2),
         permute(send_leaf, "leaf", leaf_size, 1),
         permute(send_both, axes, peers, sample_size + 2),

time: 83.7 us -> 84.7 us (1.012)
  waiting for transfers between devices: 25.5 us -> 27.5 us
  starting transfers between devices: 37.1 us -> 36.1 us
    ppermute x18, waiting for transfers between devices: 22.2 us -> 24.2 us  [permute(): return lax.ppermute(value, axis, [(i, i ^ bit) for i in range(size)])]
  transfers between devices with their start and end apart: 20 -> 20, of which waited for: 13 -> 12; matrix products, arithmetic and copies ran while one was open for 1% -> 1% of each run, Pallas kernels for 14% -> 14%
where the time goes in v6:
time: 84.7 us; the launch traced here: 84.4 us
  starting transfers between devices  36.1 us (43%)
  waiting for transfers between devices  27.5 us (32%)
  Pallas kernels  18.6 us (22%)
  local copies, waits for them, and re-layouts  1.25 us (1%)
    ppermute x18, starting transfers between devices, permute(): return lax.ppermute(value, axis, [(i, i ^ bit) for i in range(size)])  24.7 us
    ppermute x18, waiting for transfers between devices, permute(): return lax.ppermute(value, axis, [(i, i ^ bit) for i in range(size)])  24.2 us
    pallas_call x15, Pallas kernels, call(): pl.pallas_call(body, out_shape=[jax.ShapeDtypeStruct(shape, dtype) for sh...  18.6 us
    all_to_all x2, starting transfers between devices, exchange(): lax.all_to_all(flat.reshape((peers, -1) + flat.shape[1:]), axes, split_ax...  11.4 us
    all_to_all x2, waiting for transfers between devices, exchange(): lax.all_to_all(flat.reshape((peers, -1) + flat.shape[1:]), axes, split_ax...  3.28 us
  transfers between devices with their start and end apart: 20, of which 12 were waited for; matrix products, arithmetic and copies ran while one was open for 1% of the time, Pallas kernels for 14%

profile of v6, /device:TPU:0, one launch (start us, length us, event | category | flops | bytes accessed | tf_op | source)
XLA Modules:
  0.0 84.4 jit_solution(3018838470512405228)
XLA Ops:
  0.6 2.6 %pack_points.1 = (s32[1,512]{1,0:T(1,128)}, bf16[16,144,128]{2,1,0:T(8,128)(2,1)}) custom-call(s32[1,512]{1,0:T(1,128)} %bitcast.16, bf16[512,256]{1,0:T(8,128)(2,1)} %refs_1_.3), custom_call_target="tpu_custom_call" | custom-call | flops 2200000000 | bytes 856064 | tf_op jit(solution)/shard_map/pack_points/pallas_call | solution.py:521
  3.2 7.4 %all-to-all-start = ((bf16[16,144,128]{2,1,0:T(8,128)(2,1)}), bf16[16,144,128]{2,1,0:T(8,128)(2,1)S(1)}, u32[]{:S(2)}, u32[]{:S(2)}) async-start(bf16[16,144,128]{2,1,0:T(8,128)(2,1)} %get-tuple-element.86), calls=%async_computation | async-start | bytes 1179648 | tf_op jit(solution)/shard_map/all_to_all | solution.py:534
  11.8 2.0 %collective-permute-start = (bf16[2,64,256]{2,1,0:T(8,128)(2,1)S(1)}, bf16[2,64,256]{2,1,0:T(8,128)(2,1)S(1)}, u32[]{:S(2)}, u32[]{:S(2)}) collective-permute-start(bf16[2,64,256]{2,1,0:T(8,128)(2,1)S(1)} %get-tuple-element.84), channel_id=1, source_target_pairs={{0,2},{1,3},{2,0},{3,1},{4,6},{5,7},{6,4},{7,5},{8,10},{9,11},{10,... | collective-permute-start | bytes 196616 | tf_op jit(solution)/shard_map/ppermute | solution.py:473
  13.8 1.5 %collective-permute-start.1 = (bf16[2,64,256]{2,1,0:T(8,128)(2,1)S(1)}, bf16[2,64,256]{2,1,0:T(8,128)(2,1)S(1)}, u32[]{:S(2)}, u32[]{:S(2)}) collective-permute-start(bf16[2,64,256]{2,1,0:T(8,128)(2,1)S(1)} %get-tuple-element.85), channel_id=1, source_target_pairs={{0,4},{1,5},{2,6},{3,7},{4,0},{5,1},{6,2},{7,3},{8,12},{9,13},{10,... | collective-permute-start | bytes 196616 | tf_op jit(solution)/shard_map/ppermute | solution.py:473
  15.3 2.8 %collective-permute-start.3 = (bf16[2,64,256]{2,1,0:T(8,128)(2,1)S(1)}, bf16[2,64,256]{2,1,0:T(8,128)(2,1)S(1)}, u32[]{:S(2)}, u32[]{:S(2)}) collective-permute-start(bf16[2,64,256]{2,1,0:T(8,128)(2,1)S(1)} %get-tuple-element.96), channel_id=1, source_target_pairs={{0,8},{1,9},{2,10},{3,11},{4,12},{5,13},{6,14},{7,15},{8,0},{9,1},... | collective-permute-start | bytes 196616 | tf_op jit(solution)/shard_map/ppermute | solution.py:473
  18.1 1.5 %collective-permute-start.4 = (bf16[2,64,256]{2,1,0:T(8,128)(2,1)S(1)}, bf16[2,64,256]{2,1,0:T(8,128)(2,1)S(1)}, u32[]{:S(2)}, u32[]{:S(2)}) collective-permute-start(bf16[2,64,256]{2,1,0:T(8,128)(2,1)S(1)} %get-tuple-element.97), channel_id=1, source_target_pairs={{0,10},{1,11},{2,8},{3,9},{4,14},{5,15},{6,12},{7,13},{8,2},{9,3},... | collective-permute-start | bytes 196616 | tf_op jit(solution)/shard_map/ppermute | solution.py:473
  19.6 3.3 %collective-permute-start.5 = (bf16[2,64,256]{2,1,0:T(8,128)(2,1)S(1)}, bf16[2,64,256]{2,1,0:T(8,128)(2,1)S(1)}, u32[]{:S(2)}, u32[]{:S(2)}) collective-permute-start(bf16[2,64,256]{2,1,0:T(8,128)(2,1)S(1)} %get-tuple-element.98), channel_id=1, source_target_pairs={{0,12},{1,13},{2,14},{3,15},{4,8},{5,9},{6,10},{7,11},{8,4},{9,5},... | collective-permute-start | bytes 196616 | tf_op jit(solution)/shard_map/ppermute | solution.py:473
  23.6 4.0 %collective-permute-start.6 = (bf16[2,64,256]{2,1,0:T(8,128)(2,1)S(1)}, bf16[2,64,256]{2,1,0:T(8,128)(2,1)S(1)}, u32[]{:S(2)}, u32[]{:S(2)}) collective-permute-start(bf16[2,64,256]{2,1,0:T(8,128)(2,1)S(1)} %get-tuple-element.99), channel_id=1, source_target_pairs={{0,14},{1,15},{2,12},{3,13},{4,10},{5,11},{6,8},{7,9},{8,6},{9,7},... | collective-permute-start | bytes 196616 | tf_op jit(solution)/shard_map/ppermute | solution.py:473
  28.1 4.5 %forward.1 = (bf16[768,512]{1,0:T(8,128)(2,1)S(1)}, bf16[512,512]{1,0:T(8,128)(2,1)S(1)}, f32[8,512]{1,0:T(8,128)S(1)}, f32[256,512]{1,0:T(8,128)S(1)}, bf16[256...) custom-call(f32[256,512]{1,0:T(8,128)S(1)} %get-tuple-element.88.ref, ...), custom_call_target="tpu_custom_call" | custom-call | flops 7699999744 | bytes 12339200 | tf_op jit(solution)/shard_map/forward/pallas_call | solution.py:521
  32.7 2.1 %collective-permute-done.3.refs_4_ = bf16[2,64,256]{2,1,0:T(8,128)(2,1)S(1)} collective-permute-done((bf16[2,64,256]{2,1,0:T(8,128)(2,1)S(1)}, bf16[2,64,256]{2,1,0:T(8,128)(2,1)S(1)}, u32[]{:S(2)}, u32[]{:S(2)}) %collective-permute-start.3) | collective-permute-done | bytes 65568 | tf_op jit(solution)/shard_map/ppermute | solution.py:473
  34.8 2.3 %collective-permute-done.4.refs_5_ = bf16[2,64,256]{2,1,0:T(8,128)(2,1)S(1)} collective-permute-done((bf16[2,64,256]{2,1,0:T(8,128)(2,1)S(1)}, bf16[2,64,256]{2,1,0:T(8,128)(2,1)S(1)}, u32[]{:S(2)}, u32[]{:S(2)}) %collective-permute-start.4) | collective-permute-done | bytes 65568 | tf_op jit(solution)/shard_map/ppermute | solution.py:473
  37.3 1.5 %collective-permute-done.7.refs_6_ = bf16[8,64,256]{2,1,0:T(8,128)(2,1)S(1)} collective-permute-done((bf16[8,64,256]{2,1,0:T(8,128)(2,1)S(1)}, bf16[8,64,256]{2,1,0:T(8,128)(2,1)S(1)}, u32[]{:S(2)}, u32[]{:S(2)}) %collective-permute-start.7) | collective-permute-done | bytes 262176 | tf_op jit(solution)/shard_map/ppermute | solution.py:473
  38.8 2.6 %mlp_weights.1 = (bf16[1024,512]{1,0:T(8,128)(2,1)S(1)}, f32[256,512]{1,0:T(8,128)S(1)}, f32[2,4,128,256]{3,2,1,0:T(8,128)S(1)}, bf16[2,4,128,256]{3,2,1,0:T(8,128)(2,1)S(1)}) custom-call(s32[1,1024]{1,0:T(1,128)S(1)} %get-tuple-element.101.refs_0_, bf16[1024,512]{1,0:T(8,128)(2,1)S(1)} %get-tuple-element.102.refs_1_, ...), custom_call_target="tpu_custom_call" | custom-call | flops 2750000128 | bytes 7606272 | tf_op jit(solution)/shard_map/mlp_weights/pallas_call | solution.py:521
  44.0 4.6 %attention_backward.1 = (bf16[1024,256]{1,0:T(8,128)(2,1)}, f32[2,4,72,256]{3,2,1,0:T(8,128)S(1)}, bf16[2,4,72,256]{3,2,1,0:T(8,128)(2,1)S(1)}) custom-call(bf16[768,512]{1,0:T(8,128)(2,1)S(1)} %get-tuple-element.89.refs_0_, bf16[512,512]{1,0:T(8,128)(2,1)S(1)} %get-tuple-element.90.refs_1_, f32[8,512]{1,0:T(8,128)S(1)} %get-tuple-element.100.refs_3_.refs_2_, ...), custom_call_target="tpu_custom_call" | custom-call | flops 6600000000 | bytes 9815040 | tf_op jit(solution)/shard_map/attention_backward/pallas_call | solution.py:521
  50.3 1.6 %collective-permute-start.12 = (bf16[2,136,256]{2,1,0:T(8,128)(2,1)S(1)}, bf16[2,136,256]{2,1,0:T(8,128)(2,1)S(1)}, u32[]{:S(2)}, u32[]{:S(2)}) collective-permute-start(bf16[2,136,256]{2,1,0:T(8,128)(2,1)S(1)} %get-tuple-element.142), channel_id=1, source_target_pairs={{0,2},{1,3},{2,0},{3,1},{4,6},{5,7},{6,4},{7,5},{8,10},{9,11},{10,... | collective-permute-start | bytes 417800 | tf_op jit(solution)/shard_map/ppermute | solution.py:473
  51.9 2.9 %collective-permute-start.13 = (bf16[2,136,256]{2,1,0:T(8,128)(2,1)S(1)}, bf16[2,136,256]{2,1,0:T(8,128)(2,1)S(1)}, u32[]{:S(2)}, u32[]{:S(2)}) collective-permute-start(bf16[2,136,256]{2,1,0:T(8,128)(2,1)S(1)} %get-tuple-element.146), channel_id=1, source_target_pairs={{0,4},{4,0},{8,12},{12,8},{1,5},{5,1},{9,13},{13,9},{2,6},{6,2},{1... | collective-permute-start | bytes 417800 | tf_op jit(solution)/shard_map/ppermute | solution.py:473
  54.8 2.0 %collective-permute-start.11 = (bf16[2,64,256]{2,1,0:T(8,128)(2,1)S(1)}, bf16[2,64,256]{2,1,0:T(8,128)(2,1)S(1)}, u32[]{:S(2)}, u32[]{:S(2)}) collective-permute-start(bf16[2,64,256]{2,1,0:T(8,128)(2,1)S(1)} %get-tuple-element.139), channel_id=1, source_target_pairs={{0,4},{4,0},{8,12},{12,8},{1,5},{5,1},{9,13},{13,9},{2,6},{6,2},{1... | collective-permute-start | bytes 196616 | tf_op jit(solution)/shard_map/ppermute | solution.py:473
  56.7 6.1 %collective-permute-done.11.refs_1_ = bf16[2,64,256]{2,1,0:T(8,128)(2,1)S(1)} collective-permute-done((bf16[2,64,256]{2,1,0:T(8,128)(2,1)S(1)}, bf16[2,64,256]{2,1,0:T(8,128)(2,1)S(1)}, u32[]{:S(2)}, u32[]{:S(2)}) %collective-permute-start.11) | collective-permute-done | bytes 65568 | tf_op jit(solution)/shard_map/ppermute | solution.py:473
  63.0 1.7 %collective-permute-start.15 = (bf16[200,256]{1,0:T(8,128)(2,1)S(1)}, bf16[200,256]{1,0:T(8,128)(2,1)S(1)}, u32[]{:S(2)}, u32[]{:S(2)}) collective-permute-start(bf16[200,256]{1,0:T(8,128)(2,1)S(1)} %get-tuple-element.149), channel_id=1, source_target_pairs={{0,8},{4,12},{8,0},{12,4},{1,9},{5,13},{9,1},{13,5},{2,10},{6,14},... | collective-permute-start | bytes 307208 | tf_op jit(solution)/shard_map/ppermute | solution.py:473
  64.7 4.0 %all-to-all-start.1 = ((bf16[16,64,256]{2,1,0:T(8,128)(2,1)}), bf16[16,64,256]{2,1,0:T(8,128)(2,1)S(1)}, u32[]{:S(2)}, u32[]{:S(2)}) async-start(bf16[16,64,256]{2,1,0:T(8,128)(2,1)} %bitcast.5), calls=%async_computation.1 | async-start | bytes 1048576 | tf_op jit(solution)/shard_map/all_to_all | solution.py:534
  68.7 1.5 %collective-permute-done.15.refs_1_ = bf16[200,256]{1,0:T(8,128)(2,1)S(1)} collective-permute-done((bf16[200,256]{1,0:T(8,128)(2,1)S(1)}, bf16[200,256]{1,0:T(8,128)(2,1)S(1)}, u32[]{:S(2)}, u32[]{:S(2)}) %collective-permute-start.15) | collective-permute-done | bytes 102432 | tf_op jit(solution)/shard_map/ppermute | solution.py:473
  70.8 6.6 %collective-permute-done.16 = bf16[1,192,256]{2,1,0:T(8,128)(2,1)S(1)} collective-permute-done((bf16[1,192,256]{2,1,0:T(8,128)(2,1)S(1)}, bf16[1,192,256]{2,1,0:T(8,128)(2,1)S(1)}, u32[]{:S(2)}, u32[]{:S(2)}) %collective-permute-start.16) | collective-permute-done | bytes 98336 | tf_op jit(solution)/shard_map/ppermute | solution.py:473
  79.9 3.3 %all-to-all-done.1 = bf16[16,64,256]{2,1,0:T(8,128)(2,1)S(1)} async-done(((bf16[16,64,256]{2,1,0:T(8,128)(2,1)}), bf16[16,64,256]{2,1,0:T(8,128)(2,1)S(1)}, u32[]{:S(2)}, u32[]{:S(2)}) %all-to-all-start.1) | async-done | bytes 524320 | tf_op jit(solution)/shard_map/all_to_all | solution.py:534
  83.2 1.2 %unpack.1 = bf16[512,256]{1,0:T(8,128)(2,1)} custom-call(s32[1,512]{1,0:T(1,128)S(1)} %copy-done.8, bf16[1024,256]{1,0:T(8,128)(2,1)S(1)} %bitcast.11), custom_call_target="tpu_custom_call" | custom-call | flops 1100000000 | bytes 788480 | tf_op jit(solution)/shard_map/unpack/pallas_call | solution.py:521
  (53 shorter events, 10.1 us)
Async XLA Ops:
  0.6 10.0 %copy-start.3 = (bf16[512,256]{1,0:T(8,128)(2,1)S(1)}, bf16[512,256]{1,0:T(8,128)(2,1)}, u32[]{:S(2)}) copy-start(bf16[512,256]{1,0:T(8,128)(2,1)} %refs_1_.4) | copy-start | bytes 786436
  3.2 24.3 %all-to-all-start = ((bf16[16,144,128]{2,1,0:T(8,128)(2,1)}), bf16[16,144,128]{2,1,0:T(8,128)(2,1)S(1)}, u32[]{:S(2)}, u32[]{:S(2)}) async-start(bf16[16,144,128]{2,1,0:T(8,128)(2,1)} %get-tuple-element.86), calls=%async_computation | async-start | bytes 1179648 | tf_op jit(solution)/shard_map/all_to_all | solution.py:534
  11.8 7.8 %collective-permute-start = (bf16[2,64,256]{2,1,0:T(8,128)(2,1)S(1)}, bf16[2,64,256]{2,1,0:T(8,128)(2,1)S(1)}, u32[]{:S(2)}, u32[]{:S(2)}) collective-permute-start(bf16[2,64,256]{2,1,0:T(8,128)(2,1)S(1)} %get-tuple-element.84), channel_id=1, source_target_pairs={{0,2},{1,3},{2,0},{3,1},{4,6},{5,7},{6,4},{7,5},{8,10},{9,11},{10,... | collective-permute-start | bytes 196616 | tf_op jit(solution)/shard_map/ppermute | solution.py:473
  13.8 9.8 %collective-permute-start.1 = (bf16[2,64,256]{2,1,0:T(8,128)(2,1)S(1)}, bf16[2,64,256]{2,1,0:T(8,128)(2,1)S(1)}, u32[]{:S(2)}, u32[]{:S(2)}) collective-permute-start(bf16[2,64,256]{2,1,0:T(8,128)(2,1)S(1)} %get-tuple-element.85), channel_id=1, source_target_pairs={{0,4},{1,5},{2,6},{3,7},{4,0},{5,1},{6,2},{7,3},{8,12},{9,13},{10,... | collective-permute-start | bytes 196616 | tf_op jit(solution)/shard_map/ppermute | solution.py:473
  15.2 17.5 %collective-permute-start.2 = (bf16[2,64,256]{2,1,0:T(8,128)(2,1)S(1)}, bf16[2,64,256]{2,1,0:T(8,128)(2,1)S(1)}, u32[]{:S(2)}, u32[]{:S(2)}) collective-permute-start(bf16[2,64,256]{2,1,0:T(8,128)(2,1)S(1)} %get-tuple-element.95), channel_id=1, source_target_pairs={{0,6},{1,7},{2,4},{3,5},{4,2},{5,3},{6,0},{7,1},{8,14},{9,15},{10,... | collective-permute-start | bytes 196616 | tf_op jit(solution)/shard_map/ppermute | solution.py:473
  15.3 19.5 %collective-permute-start.3 = (bf16[2,64,256]{2,1,0:T(8,128)(2,1)S(1)}, bf16[2,64,256]{2,1,0:T(8,128)(2,1)S(1)}, u32[]{:S(2)}, u32[]{:S(2)}) collective-permute-start(bf16[2,64,256]{2,1,0:T(8,128)(2,1)S(1)} %get-tuple-element.96), channel_id=1, source_target_pairs={{0,8},{1,9},{2,10},{3,11},{4,12},{5,13},{6,14},{7,15},{8,0},{9,1},... | collective-permute-start | bytes 196616 | tf_op jit(solution)/shard_map/ppermute | solution.py:473
  18.1 19.0 %collective-permute-start.4 = (bf16[2,64,256]{2,1,0:T(8,128)(2,1)S(1)}, bf16[2,64,256]{2,1,0:T(8,128)(2,1)S(1)}, u32[]{:S(2)}, u32[]{:S(2)}) collective-permute-start(bf16[2,64,256]{2,1,0:T(8,128)(2,1)S(1)} %get-tuple-element.97), channel_id=1, source_target_pairs={{0,10},{1,11},{2,8},{3,9},{4,14},{5,15},{6,12},{7,13},{8,2},{9,3},... | collective-permute-start | bytes 196616 | tf_op jit(solution)/shard_map/ppermute | solution.py:473
  19.6 17.5 %collective-permute-start.5 = (bf16[2,64,256]{2,1,0:T(8,128)(2,1)S(1)}, bf16[2,64,256]{2,1,0:T(8,128)(2,1)S(1)}, u32[]{:S(2)}, u32[]{:S(2)}) collective-permute-start(bf16[2,64,256]{2,1,0:T(8,128)(2,1)S(1)} %get-tuple-element.98), channel_id=1, source_target_pairs={{0,12},{1,13},{2,14},{3,15},{4,8},{5,9},{6,10},{7,11},{8,4},{9,5},... | collective-permute-start | bytes 196616 | tf_op jit(solution)/shard_map/ppermute | solution.py:473
  23.6 4.6 %copy-start.6 = (f32[256]{0:T(256)S(1)}, f32[256]{0:T(256)}, u32[]{:S(2)}) copy-start(f32[256]{0:T(256)} %param.17) | copy-start | bytes 3076
  23.6 13.6 %collective-permute-start.6 = (bf16[2,64,256]{2,1,0:T(8,128)(2,1)S(1)}, bf16[2,64,256]{2,1,0:T(8,128)(2,1)S(1)}, u32[]{:S(2)}, u32[]{:S(2)}) collective-permute-start(bf16[2,64,256]{2,1,0:T(8,128)(2,1)S(1)} %get-tuple-element.99), channel_id=1, source_target_pairs={{0,14},{1,15},{2,12},{3,13},{4,10},{5,11},{6,8},{7,9},{8,6},{9,7},... | collective-permute-start | bytes 196616 | tf_op jit(solution)/shard_map/ppermute | solution.py:473
  28.1 10.7 %copy-start = (bf16[1024,256]{1,0:T(8,128)(2,1)S(1)}, bf16[1024,256]{1,0:T(8,128)(2,1)}, u32[]{:S(2)}) copy-start(bf16[1024,256]{1,0:T(8,128)(2,1)} %refs_4_.1) | copy-start | bytes 1572868
  37.2 1.6 %collective-permute-start.7 = (bf16[8,64,256]{2,1,0:T(8,128)(2,1)S(1)}, bf16[8,64,256]{2,1,0:T(8,128)(2,1)S(1)}, u32[]{:S(2)}, u32[]{:S(2)}) collective-permute-start(bf16[8,64,256]{2,1,0:T(8,128)(2,1)S(1)} %get-tuple-element.114), channel_id=1, source_target_pairs={{0,1},{1,0},{2,3},{3,2},{4,5},{5,4},{6,7},{7,6},{8,9},{9,8},{10,11... | collective-permute-start | bytes 786440 | tf_op jit(solution)/shard_map/ppermute | solution.py:473
  41.4 2.0 %collective-permute-start.8 = (bf16[2,4,128,256]{3,2,1,0:T(8,128)(2,1)S(1)}, bf16[2,4,128,256]{3,2,1,0:T(8,128)(2,1)S(1)}, u32[]{:S(2)}, u32[]{:S(2)}) collective-permute-start(bf16[2,4,128,256]{3,2,1,0:T(8,128)(2,1)S(1)} %get-tuple-element.122), channel_id=1, source_target_pairs={{0,1},{1,0},{2,3},{3,2},{4,5},{5,4},{6,7},{7,6},{8,9},{9,8},{10,11... | collective-permute-start | bytes 1572872 | tf_op jit(solution)/shard_map/ppermute | solution.py:473
  43.4 5.6 %collective-permute-start.10 = (bf16[1,4,64,256]{3,2,1,0:T(8,128)(2,1)S(1)}, bf16[1,4,64,256]{3,2,1,0:T(8,128)(2,1)S(1)}, u32[]{:S(2)}, u32[]{:S(2)}) collective-permute-start(bf16[1,4,64,256]{3,2,1,0:T(8,128)(2,1)S(1)} %get-tuple-element.137), channel_id=1, source_target_pairs={{0,2},{1,3},{2,0},{3,1},{4,6},{5,7},{6,4},{7,5},{8,10},{9,11},{10,... | collective-permute-start | bytes 393224 | tf_op jit(solution)/shard_map/ppermute | solution.py:473
  48.6 1.6 %collective-permute-start.9 = (bf16[2,4,72,256]{3,2,1,0:T(8,128)(2,1)S(1)}, bf16[2,4,72,256]{3,2,1,0:T(8,128)(2,1)S(1)}, u32[]{:S(2)}, u32[]{:S(2)}) collective-permute-start(bf16[2,4,72,256]{3,2,1,0:T(8,128)(2,1)S(1)} %get-tuple-element.135), channel_id=1, source_target_pairs={{0,1},{1,0},{2,3},{3,2},{4,5},{5,4},{6,7},{7,6},{8,9},{9,8},{10,11... | collective-permute-start | bytes 884744 | tf_op jit(solution)/shard_map/ppermute | solution.py:473
  50.3 12.6 %collective-permute-start.12 = (bf16[2,136,256]{2,1,0:T(8,128)(2,1)S(1)}, bf16[2,136,256]{2,1,0:T(8,128)(2,1)S(1)}, u32[]{:S(2)}, u32[]{:S(2)}) collective-permute-start(bf16[2,136,256]{2,1,0:T(8,128)(2,1)S(1)} %get-tuple-element.142), channel_id=1, source_target_pairs={{0,2},{1,3},{2,0},{3,1},{4,6},{5,7},{6,4},{7,5},{8,10},{9,11},{10,... | collective-permute-start | bytes 417800 | tf_op jit(solution)/shard_map/ppermute | solution.py:473
  51.9 11.0 %collective-permute-start.13 = (bf16[2,136,256]{2,1,0:T(8,128)(2,1)S(1)}, bf16[2,136,256]{2,1,0:T(8,128)(2,1)S(1)}, u32[]{:S(2)}, u32[]{:S(2)}) collective-permute-start(bf16[2,136,256]{2,1,0:T(8,128)(2,1)S(1)} %get-tuple-element.146), channel_id=1, source_target_pairs={{0,4},{4,0},{8,12},{12,8},{1,5},{5,1},{9,13},{13,9},{2,6},{6,2},{1... | collective-permute-start | bytes 417800 | tf_op jit(solution)/shard_map/ppermute | solution.py:473
  54.8 8.1 %collective-permute-start.14 = (bf16[2,136,256]{2,1,0:T(8,128)(2,1)S(1)}, bf16[2,136,256]{2,1,0:T(8,128)(2,1)S(1)}, u32[]{:S(2)}, u32[]{:S(2)}) collective-permute-start(bf16[2,136,256]{2,1,0:T(8,128)(2,1)S(1)} %get-tuple-element.147), channel_id=1, source_target_pairs={{0,6},{1,7},{2,4},{3,5},{4,2},{5,3},{6,0},{7,1},{8,14},{9,15},{10,... | collective-permute-start | bytes 417800 | tf_op jit(solution)/shard_map/ppermute | solution.py:473
  54.8 8.1 %collective-permute-start.11 = (bf16[2,64,256]{2,1,0:T(8,128)(2,1)S(1)}, bf16[2,64,256]{2,1,0:T(8,128)(2,1)S(1)}, u32[]{:S(2)}, u32[]{:S(2)}) collective-permute-start(bf16[2,64,256]{2,1,0:T(8,128)(2,1)S(1)} %get-tuple-element.139), channel_id=1, source_target_pairs={{0,4},{4,0},{8,12},{12,8},{1,5},{5,1},{9,13},{13,9},{2,6},{6,2},{1... | collective-permute-start | bytes 196616 | tf_op jit(solution)/shard_map/ppermute | solution.py:473
  63.0 7.3 %collective-permute-start.15 = (bf16[200,256]{1,0:T(8,128)(2,1)S(1)}, bf16[200,256]{1,0:T(8,128)(2,1)S(1)}, u32[]{:S(2)}, u32[]{:S(2)}) collective-permute-start(bf16[200,256]{1,0:T(8,128)(2,1)S(1)} %get-tuple-element.149), channel_id=1, source_target_pairs={{0,8},{4,12},{8,0},{12,4},{1,9},{5,13},{9,1},{13,5},{2,10},{6,14},... | collective-permute-start | bytes 307208 | tf_op jit(solution)/shard_map/ppermute | solution.py:473
  64.7 18.5 %all-to-all-start.1 = ((bf16[16,64,256]{2,1,0:T(8,128)(2,1)}), bf16[16,64,256]{2,1,0:T(8,128)(2,1)S(1)}, u32[]{:S(2)}, u32[]{:S(2)}) async-start(bf16[16,64,256]{2,1,0:T(8,128)(2,1)} %bitcast.5), calls=%async_computation.1 | async-start | bytes 1048576 | tf_op jit(solution)/shard_map/all_to_all | solution.py:534
  70.2 7.2 %collective-permute-start.16 = (bf16[1,192,256]{2,1,0:T(8,128)(2,1)S(1)}, bf16[1,192,256]{2,1,0:T(8,128)(2,1)S(1)}, u32[]{:S(2)}, u32[]{:S(2)}) collective-permute-start(bf16[1,192,256]{2,1,0:T(8,128)(2,1)S(1)} %get-tuple-element.150), channel_id=1, source_target_pairs={{0,2},{1,3},{2,0},{3,1},{4,6},{5,7},{6,4},{7,5},{8,10},{9,11},{10,... | collective-permute-start | bytes 294920 | tf_op jit(solution)/shard_map/ppermute | solution.py:473
  70.8 12.3 %copy-start.8 = (s32[1,512]{1,0:T(1,128)S(1)}, s32[1,512]{1,0:T(1,128)}, u32[]{:S(2)}) copy-start(s32[1,512]{1,0:T(1,128)} %get-tuple-element.83.refs_0_) | copy-start | bytes 6148
  77.4 1.5 %collective-permute-start.17 = (bf16[2,192,256]{2,1,0:T(8,128)(2,1)S(1)}, bf16[2,192,256]{2,1,0:T(8,128)(2,1)S(1)}, u32[]{:S(2)}, u32[]{:S(2)}) collective-permute-start(bf16[2,192,256]{2,1,0:T(8,128)(2,1)S(1)} %constant_dynamic-update-slice_fusion.refs_0_), channel_id=1, source_target_pairs={{0,1},{1,0},{2,3},{3,2},{4,5},{5,4},{6,7},{7,6},{8,9},{9,8},{10,11... | collective-permute-start | bytes 589832 | tf_op jit(solution)/shard_map/ppermute | solution.py:473
  (5 other events, 18.8 us)

commit v7 on v4

--- a/solution.py
+++ b/solution.py
@@ -570,8 +570,7 @@
             pack_cot_kernel, [((2, cap, width), BF16)] * (peers // 2), "pack_cot", 1, slot, cotangent,
             scratch=[pltpu.VMEM((peers, cap, width), BF16)],
         )
-        pairs = [packed_cot[0]] + [permute(packed_cot[step], axes, peers, 2 * step) for step in range(1, peers // 2)]
-        *pairs[1:3], forward_args[0] = lax.optimization_barrier((*pairs[1:3], forward_args[0]))
+        far = [permute(packed_cot[step], axes, peers, 2 * step) for step in range(3, peers // 2)]
     else:
         (packed_cot,) = call(pack_cot_kernel, [((slots, width), BF16)], "pack_cot", 1, slot, cotangent)
         arrived_cot = [exchange(packed_cot, axes, peers)]
@@ -594,7 +593,10 @@
         "forward", 7, rotated, w_qkv, w_out, w_up, gain_attn.reshape(1, width), gain_mlp.reshape(1, width),
     )
     if by_permute:
-        scales, *pairs = lax.optimization_barrier((scales, *pairs))
+        near = lax.optimization_barrier((scales, *packed_cot[1:3]))[1:]
+        scales, *far = lax.optimization_barrier((scales, *far))
+        near = [permute(block, axes, peers, 2 * step) for step, block in enumerate(near, 1)]
+        pairs = [packed_cot[0], *near, *far]
         half = ((peers // 2, cap, width), BF16)
         mine, for_mate = call(regroup_kernel, [half] * 2, "regroup", 0.3, *pairs)
         arrived_cot = [mine, permute(for_mate, axes, peers, 1)]

time: 83.7 us -> 88.3 us (1.055)
  waiting for transfers between devices: 25.5 us -> 30 us
    all_to_all x2, waiting for transfers between devices: 3.28 us -> 7.47 us  [exchange(): lax.all_to_all(flat.reshape((peers, -1) + flat.shape[1:]), axes, split_ax...]
    ppermute x18, starting transfers between devices: 25.1 us -> 26.2 us  [permute(): return lax.ppermute(value, axis, [(i, i ^ bit) for i in range(size)])]
    all_to_all x2, starting transfers between devices: 11.9 us -> 10.9 us  [exchange(): lax.all_to_all(flat.reshape((peers, -1) + flat.shape[1:]), axes, split_ax...]
where the time goes in v7:
time: 88.3 us; the launch traced here: 87.9 us
  starting transfers between devices  37.1 us (42%)
  waiting for transfers between devices  30 us (34%)
  Pallas kernels  18.6 us (21%)
  local copies, waits for them, and re-layouts  1.25 us (1%)
    ppermute x18, starting transfers between devices, permute(): return lax.ppermute(value, axis, [(i, i ^ bit) for i in range(size)])  26.2 us
    ppermute x18, waiting for transfers between devices, permute(): return lax.ppermute(value, axis, [(i, i ^ bit) for i in range(size)])  22.5 us
    pallas_call x15, Pallas kernels, call(): pl.pallas_call(body, out_shape=[jax.ShapeDtypeStruct(shape, dtype) for sh...  18.6 us
    all_to_all x2, starting transfers between devices, exchange(): lax.all_to_all(flat.reshape((peers, -1) + flat.shape[1:]), axes, split_ax...  10.9 us
    all_to_all x2, waiting for transfers between devices, exchange(): lax.all_to_all(flat.reshape((peers, -1) + flat.shape[1:]), axes, split_ax...  7.47 us
  transfers between devices with their start and end apart: 20, of which 13 were waited for; matrix products, arithmetic and copies ran while one was open for 1% of the time, Pallas kernels for 14%

profile of v7, /device:TPU:0, one launch (start us, length us, event | category | flops | bytes accessed | tf_op | source)
XLA Modules:
  0.0 87.9 jit_solution(13970543437837143095)
XLA Ops:
  0.6 2.6 %pack_points.1 = (s32[1,512]{1,0:T(1,128)}, bf16[16,144,128]{2,1,0:T(8,128)(2,1)}) custom-call(s32[1,512]{1,0:T(1,128)} %bitcast.16, bf16[512,256]{1,0:T(8,128)(2,1)} %refs_1_.3), custom_call_target="tpu_custom_call" | custom-call | flops 2200000000 | bytes 856064 | tf_op jit(solution)/shard_map/pack_points/pallas_call | solution.py:515
  3.2 7.4 %all-to-all-start = ((bf16[16,144,128]{2,1,0:T(8,128)(2,1)}), bf16[16,144,128]{2,1,0:T(8,128)(2,1)S(1)}, u32[]{:S(2)}, u32[]{:S(2)}) async-start(bf16[16,144,128]{2,1,0:T(8,128)(2,1)} %get-tuple-element.80), calls=%async_computation | async-start | bytes 1179648 | tf_op jit(solution)/shard_map/all_to_all | solution.py:528
  11.8 2.9 %collective-permute-start = (bf16[2,64,256]{2,1,0:T(8,128)(2,1)S(1)}, bf16[2,64,256]{2,1,0:T(8,128)(2,1)S(1)}, u32[]{:S(2)}, u32[]{:S(2)}) collective-permute-start(bf16[2,64,256]{2,1,0:T(8,128)(2,1)S(1)} %get-tuple-element.85), channel_id=1, source_target_pairs={{0,6},{1,7},{2,4},{3,5},{4,2},{5,3},{6,0},{7,1},{8,14},{9,15},{10,... | collective-permute-start | bytes 196616 | tf_op jit(solution)/shard_map/ppermute | solution.py:469
  14.7 2.4 %collective-permute-start.1 = (bf16[2,64,256]{2,1,0:T(8,128)(2,1)S(1)}, bf16[2,64,256]{2,1,0:T(8,128)(2,1)S(1)}, u32[]{:S(2)}, u32[]{:S(2)}) collective-permute-start(bf16[2,64,256]{2,1,0:T(8,128)(2,1)S(1)} %get-tuple-element.86), channel_id=1, source_target_pairs={{0,8},{1,9},{2,10},{3,11},{4,12},{5,13},{6,14},{7,15},{8,0},{9,1},... | collective-permute-start | bytes 196616 | tf_op jit(solution)/shard_map/ppermute | solution.py:469
  17.6 2.4 %collective-permute-start.3 = (bf16[2,64,256]{2,1,0:T(8,128)(2,1)S(1)}, bf16[2,64,256]{2,1,0:T(8,128)(2,1)S(1)}, u32[]{:S(2)}, u32[]{:S(2)}) collective-permute-start(bf16[2,64,256]{2,1,0:T(8,128)(2,1)S(1)} %get-tuple-element.88), channel_id=1, source_target_pairs={{0,12},{1,13},{2,14},{3,15},{4,8},{5,9},{6,10},{7,11},{8,4},{9,5},... | collective-permute-start | bytes 196616 | tf_op jit(solution)/shard_map/ppermute | solution.py:469
  20.0 2.4 %collective-permute-start.4 = (bf16[2,64,256]{2,1,0:T(8,128)(2,1)S(1)}, bf16[2,64,256]{2,1,0:T(8,128)(2,1)S(1)}, u32[]{:S(2)}, u32[]{:S(2)}) collective-permute-start(bf16[2,64,256]{2,1,0:T(8,128)(2,1)S(1)} %get-tuple-element.89), channel_id=1, source_target_pairs={{0,14},{1,15},{2,12},{3,13},{4,10},{5,11},{6,8},{7,9},{8,6},{9,7},... | collective-permute-start | bytes 196616 | tf_op jit(solution)/shard_map/ppermute | solution.py:469
  22.4 4.1 %all-to-all-done.refs_0_ = bf16[16,144,128]{2,1,0:T(8,128)(2,1)S(1)} async-done(((bf16[16,144,128]{2,1,0:T(8,128)(2,1)}), bf16[16,144,128]{2,1,0:T(8,128)(2,1)S(1)}, u32[]{:S(2)}, u32[]{:S(2)}) %all-to-all-start) | async-done | bytes 589856 | tf_op jit(solution)/shard_map/all_to_all | solution.py:528
  27.1 4.6 %forward.1 = (bf16[768,512]{1,0:T(8,128)(2,1)S(1)}, bf16[512,512]{1,0:T(8,128)(2,1)S(1)}, f32[8,512]{1,0:T(8,128)S(1)}, f32[256,512]{1,0:T(8,128)S(1)}, bf16[256...) custom-call(f32[256,512]{1,0:T(8,128)S(1)} %get-tuple-element.81.ref, ...), custom_call_target="tpu_custom_call" | custom-call | flops 7699999744 | bytes 12339200 | tf_op jit(solution)/shard_map/forward/pallas_call | solution.py:515
  31.9 2.9 %collective-permute-done.1.refs_4_ = bf16[2,64,256]{2,1,0:T(8,128)(2,1)S(1)} collective-permute-done((bf16[2,64,256]{2,1,0:T(8,128)(2,1)S(1)}, bf16[2,64,256]{2,1,0:T(8,128)(2,1)S(1)}, u32[]{:S(2)}, u32[]{:S(2)}) %collective-permute-start.1) | collective-permute-done | bytes 65568 | tf_op jit(solution)/shard_map/ppermute | solution.py:469
  34.8 4.9 %collective-permute-start.6 = (bf16[2,64,256]{2,1,0:T(8,128)(2,1)S(1)}, bf16[2,64,256]{2,1,0:T(8,128)(2,1)S(1)}, u32[]{:S(2)}, u32[]{:S(2)}) collective-permute-start(bf16[2,64,256]{2,1,0:T(8,128)(2,1)S(1)} %get-tuple-element.99), channel_id=1, source_target_pairs={{0,4},{1,5},{2,6},{3,7},{4,0},{5,1},{6,2},{7,3},{8,12},{9,13},{10,... | collective-permute-start | bytes 196616 | tf_op jit(solution)/shard_map/ppermute | solution.py:469
  39.7 2.7 %collective-permute-done.6.refs_2_ = bf16[2,64,256]{2,1,0:T(8,128)(2,1)S(1)} collective-permute-done((bf16[2,64,256]{2,1,0:T(8,128)(2,1)S(1)}, bf16[2,64,256]{2,1,0:T(8,128)(2,1)S(1)}, u32[]{:S(2)}, u32[]{:S(2)}) %collective-permute-start.6) | collective-permute-done | bytes 65568 | tf_op jit(solution)/shard_map/ppermute | solution.py:469
  42.6 1.5 %collective-permute-done.7.refs_6_ = bf16[8,64,256]{2,1,0:T(8,128)(2,1)S(1)} collective-permute-done((bf16[8,64,256]{2,1,0:T(8,128)(2,1)S(1)}, bf16[8,64,256]{2,1,0:T(8,128)(2,1)S(1)}, u32[]{:S(2)}, u32[]{:S(2)}) %collective-permute-start.7) | collective-permute-done | bytes 262176 | tf_op jit(solution)/shard_map/ppermute | solution.py:469
  44.1 2.6 %mlp_weights.1 = (bf16[1024,512]{1,0:T(8,128)(2,1)S(1)}, f32[256,512]{1,0:T(8,128)S(1)}, f32[2,4,128,256]{3,2,1,0:T(8,128)S(1)}, bf16[2,4,128,256]{3,2,1,0:T(8,128)(2,1)S(1)}) custom-call(s32[1,1024]{1,0:T(1,128)S(1)} %get-tuple-element.91.refs_0_, bf16[1024,512]{1,0:T(8,128)(2,1)S(1)} %get-tuple-element.92.refs_1_, ...), custom_call_target="tpu_custom_call" | custom-call | flops 2750000128 | bytes 7606272 | tf_op jit(solution)/shard_map/mlp_weights/pallas_call | solution.py:515
  48.8 4.6 %attention_backward.1 = (bf16[1024,256]{1,0:T(8,128)(2,1)}, f32[2,4,72,256]{3,2,1,0:T(8,128)S(1)}, bf16[2,4,72,256]{3,2,1,0:T(8,128)(2,1)S(1)}) custom-call(bf16[768,512]{1,0:T(8,128)(2,1)S(1)} %get-tuple-element.82.refs_0_, bf16[512,512]{1,0:T(8,128)(2,1)S(1)} %get-tuple-element.83.refs_1_, f32[8,512]{1,0:T(8,128)S(1)} %get-tuple-element.90.refs_3_.refs_2_, ...), custom_call_target="tpu_custom_call" | custom-call | flops 6600000000 | bytes 9815040 | tf_op jit(solution)/shard_map/attention_backward/pallas_call | solution.py:515
  53.6 3.6 %collective-permute-done.10 = bf16[1,4,128,256]{3,2,1,0:T(8,128)(2,1)S(1)} collective-permute-done((bf16[1,4,128,256]{3,2,1,0:T(8,128)(2,1)S(1)}, bf16[1,4,128,256]{3,2,1,0:T(8,128)(2,1)S(1)}, u32[]{:S(2)}, u32[]{:S(2)}) %collective-permute-start.10) | collective-permute-done | bytes 262176 | tf_op jit(solution)/shard_map/ppermute | solution.py:469
  57.3 1.8 %collective-permute-start.11 = (bf16[2,128,256]{2,1,0:T(8,128)(2,1)S(1)}, bf16[2,128,256]{2,1,0:T(8,128)(2,1)S(1)}, u32[]{:S(2)}, u32[]{:S(2)}) collective-permute-start(bf16[2,128,256]{2,1,0:T(8,128)(2,1)S(1)} %get-tuple-element.131), channel_id=1, source_target_pairs={{0,4},{4,0},{8,12},{12,8},{1,5},{5,1},{9,13},{13,9},{2,6},{6,2},{1... | collective-permute-start | bytes 393224 | tf_op jit(solution)/shard_map/ppermute | solution.py:469
  59.8 2.9 %collective-permute-start.14 = (bf16[2,72,256]{2,1,0:T(8,128)(2,1)S(1)}, bf16[2,72,256]{2,1,0:T(8,128)(2,1)S(1)}, u32[]{:S(2)}, u32[]{:S(2)}) collective-permute-start(bf16[2,72,256]{2,1,0:T(8,128)(2,1)S(1)} %get-tuple-element.139), channel_id=1, source_target_pairs={{0,6},{1,7},{2,4},{3,5},{4,2},{5,3},{6,0},{7,1},{8,14},{9,15},{10,... | collective-permute-start | bytes 221192 | tf_op jit(solution)/shard_map/ppermute | solution.py:469
  62.7 1.7 %collective-permute-done.12.refs_3_ = bf16[2,72,256]{2,1,0:T(8,128)(2,1)S(1)} collective-permute-done((bf16[2,72,256]{2,1,0:T(8,128)(2,1)S(1)}, bf16[2,72,256]{2,1,0:T(8,128)(2,1)S(1)}, u32[]{:S(2)}, u32[]{:S(2)}) %collective-permute-start.12) | collective-permute-done | bytes 73760 | tf_op jit(solution)/shard_map/ppermute | solution.py:469
  65.9 2.8 %collective-permute-start.15 = (bf16[200,256]{1,0:T(8,128)(2,1)S(1)}, bf16[200,256]{1,0:T(8,128)(2,1)S(1)}, u32[]{:S(2)}, u32[]{:S(2)}) collective-permute-start(bf16[200,256]{1,0:T(8,128)(2,1)S(1)} %get-tuple-element.141), channel_id=1, source_target_pairs={{0,8},{4,12},{8,0},{12,4},{1,9},{5,13},{9,1},{13,5},{2,10},{6,14},... | collective-permute-start | bytes 307208 | tf_op jit(solution)/shard_map/ppermute | solution.py:469
  68.7 3.6 %all-to-all-start.1 = ((bf16[16,64,256]{2,1,0:T(8,128)(2,1)}), bf16[16,64,256]{2,1,0:T(8,128)(2,1)S(1)}, u32[]{:S(2)}, u32[]{:S(2)}) async-start(bf16[16,64,256]{2,1,0:T(8,128)(2,1)} %bitcast.5), calls=%async_computation.1 | async-start | bytes 1048576 | tf_op jit(solution)/shard_map/all_to_all | solution.py:528
  72.6 1.6 %collective-permute-start.16 = (bf16[1,192,256]{2,1,0:T(8,128)(2,1)S(1)}, bf16[1,192,256]{2,1,0:T(8,128)(2,1)S(1)}, u32[]{:S(2)}, u32[]{:S(2)}) collective-permute-start(bf16[1,192,256]{2,1,0:T(8,128)(2,1)S(1)} %get-tuple-element.142), channel_id=1, source_target_pairs={{0,2},{1,3},{2,0},{3,1},{4,6},{5,7},{6,4},{7,5},{8,10},{9,11},{10,... | collective-permute-start | bytes 294920 | tf_op jit(solution)/shard_map/ppermute | solution.py:469
  74.3 6.6 %collective-permute-done.16 = bf16[1,192,256]{2,1,0:T(8,128)(2,1)S(1)} collective-permute-done((bf16[1,192,256]{2,1,0:T(8,128)(2,1)S(1)}, bf16[1,192,256]{2,1,0:T(8,128)(2,1)S(1)}, u32[]{:S(2)}, u32[]{:S(2)}) %collective-permute-start.16) | collective-permute-done | bytes 98336 | tf_op jit(solution)/shard_map/ppermute | solution.py:469
  83.4 3.3 %all-to-all-done.1 = bf16[16,64,256]{2,1,0:T(8,128)(2,1)S(1)} async-done(((bf16[16,64,256]{2,1,0:T(8,128)(2,1)}), bf16[16,64,256]{2,1,0:T(8,128)(2,1)S(1)}, u32[]{:S(2)}, u32[]{:S(2)}) %all-to-all-start.1) | async-done | bytes 524320 | tf_op jit(solution)/shard_map/all_to_all | solution.py:528
  86.7 1.2 %unpack.1 = bf16[512,256]{1,0:T(8,128)(2,1)} custom-call(s32[1,512]{1,0:T(1,128)S(1)} %copy-done.8, bf16[1024,256]{1,0:T(8,128)(2,1)S(1)} %bitcast.11), custom_call_target="tpu_custom_call" | custom-call | flops 1100000000 | bytes 788480 | tf_op jit(solution)/shard_map/unpack/pallas_call | solution.py:515
  (53 shorter events, 10.1 us)
Async XLA Ops:
  0.6 10.0 %copy-start.3 = (bf16[512,256]{1,0:T(8,128)(2,1)S(1)}, bf16[512,256]{1,0:T(8,128)(2,1)}, u32[]{:S(2)}) copy-start(bf16[512,256]{1,0:T(8,128)(2,1)} %refs_1_.5) | copy-start | bytes 786436
  3.2 23.3 %all-to-all-start = ((bf16[16,144,128]{2,1,0:T(8,128)(2,1)}), bf16[16,144,128]{2,1,0:T(8,128)(2,1)S(1)}, u32[]{:S(2)}, u32[]{:S(2)}) async-start(bf16[16,144,128]{2,1,0:T(8,128)(2,1)} %get-tuple-element.80), calls=%async_computation | async-start | bytes 1179648 | tf_op jit(solution)/shard_map/all_to_all | solution.py:528
  11.8 19.9 %collective-permute-start = (bf16[2,64,256]{2,1,0:T(8,128)(2,1)S(1)}, bf16[2,64,256]{2,1,0:T(8,128)(2,1)S(1)}, u32[]{:S(2)}, u32[]{:S(2)}) collective-permute-start(bf16[2,64,256]{2,1,0:T(8,128)(2,1)S(1)} %get-tuple-element.85), channel_id=1, source_target_pairs={{0,6},{1,7},{2,4},{3,5},{4,2},{5,3},{6,0},{7,1},{8,14},{9,15},{10,... | collective-permute-start | bytes 196616 | tf_op jit(solution)/shard_map/ppermute | solution.py:469
  14.7 20.2 %collective-permute-start.1 = (bf16[2,64,256]{2,1,0:T(8,128)(2,1)S(1)}, bf16[2,64,256]{2,1,0:T(8,128)(2,1)S(1)}, u32[]{:S(2)}, u32[]{:S(2)}) collective-permute-start(bf16[2,64,256]{2,1,0:T(8,128)(2,1)S(1)} %get-tuple-element.86), channel_id=1, source_target_pairs={{0,8},{1,9},{2,10},{3,11},{4,12},{5,13},{6,14},{7,15},{8,0},{9,1},... | collective-permute-start | bytes 196616 | tf_op jit(solution)/shard_map/ppermute | solution.py:469
  17.0 22.7 %collective-permute-start.2 = (bf16[2,64,256]{2,1,0:T(8,128)(2,1)S(1)}, bf16[2,64,256]{2,1,0:T(8,128)(2,1)S(1)}, u32[]{:S(2)}, u32[]{:S(2)}) collective-permute-start(bf16[2,64,256]{2,1,0:T(8,128)(2,1)S(1)} %get-tuple-element.87), channel_id=1, source_target_pairs={{0,10},{1,11},{2,8},{3,9},{4,14},{5,15},{6,12},{7,13},{8,2},{9,3},... | collective-permute-start | bytes 196616 | tf_op jit(solution)/shard_map/ppermute | solution.py:469
  17.6 22.1 %collective-permute-start.3 = (bf16[2,64,256]{2,1,0:T(8,128)(2,1)S(1)}, bf16[2,64,256]{2,1,0:T(8,128)(2,1)S(1)}, u32[]{:S(2)}, u32[]{:S(2)}) collective-permute-start(bf16[2,64,256]{2,1,0:T(8,128)(2,1)S(1)} %get-tuple-element.88), channel_id=1, source_target_pairs={{0,12},{1,13},{2,14},{3,15},{4,8},{5,9},{6,10},{7,11},{8,4},{9,5},... | collective-permute-start | bytes 196616 | tf_op jit(solution)/shard_map/ppermute | solution.py:469
  20.0 7.1 %copy-start.6 = (f32[256]{0:T(256)S(1)}, f32[256]{0:T(256)}, u32[]{:S(2)}) copy-start(f32[256]{0:T(256)} %param.17) | copy-start | bytes 3076
  20.0 19.8 %collective-permute-start.4 = (bf16[2,64,256]{2,1,0:T(8,128)(2,1)S(1)}, bf16[2,64,256]{2,1,0:T(8,128)(2,1)S(1)}, u32[]{:S(2)}, u32[]{:S(2)}) collective-permute-start(bf16[2,64,256]{2,1,0:T(8,128)(2,1)S(1)} %get-tuple-element.89), channel_id=1, source_target_pairs={{0,14},{1,15},{2,12},{3,13},{4,10},{5,11},{6,8},{7,9},{8,6},{9,7},... | collective-permute-start | bytes 196616 | tf_op jit(solution)/shard_map/ppermute | solution.py:469
  27.1 17.0 %copy-start = (bf16[1024,256]{1,0:T(8,128)(2,1)S(1)}, bf16[1024,256]{1,0:T(8,128)(2,1)}, u32[]{:S(2)}) copy-start(bf16[1024,256]{1,0:T(8,128)(2,1)} %refs_4_.1) | copy-start | bytes 1572868
  31.7 8.0 %collective-permute-start.5 = (bf16[2,64,256]{2,1,0:T(8,128)(2,1)S(1)}, bf16[2,64,256]{2,1,0:T(8,128)(2,1)S(1)}, u32[]{:S(2)}, u32[]{:S(2)}) collective-permute-start(bf16[2,64,256]{2,1,0:T(8,128)(2,1)S(1)} %get-tuple-element.98), channel_id=1, source_target_pairs={{0,2},{1,3},{2,0},{3,1},{4,6},{5,7},{6,4},{7,5},{8,10},{9,11},{10,... | collective-permute-start | bytes 196616 | tf_op jit(solution)/shard_map/ppermute | solution.py:469
  34.8 7.6 %collective-permute-start.6 = (bf16[2,64,256]{2,1,0:T(8,128)(2,1)S(1)}, bf16[2,64,256]{2,1,0:T(8,128)(2,1)S(1)}, u32[]{:S(2)}, u32[]{:S(2)}) collective-permute-start(bf16[2,64,256]{2,1,0:T(8,128)(2,1)S(1)} %get-tuple-element.99), channel_id=1, source_target_pairs={{0,4},{1,5},{2,6},{3,7},{4,0},{5,1},{6,2},{7,3},{8,12},{9,13},{10,... | collective-permute-start | bytes 196616 | tf_op jit(solution)/shard_map/ppermute | solution.py:469
  42.5 1.6 %collective-permute-start.7 = (bf16[8,64,256]{2,1,0:T(8,128)(2,1)S(1)}, bf16[8,64,256]{2,1,0:T(8,128)(2,1)S(1)}, u32[]{:S(2)}, u32[]{:S(2)}) collective-permute-start(bf16[8,64,256]{2,1,0:T(8,128)(2,1)S(1)} %get-tuple-element.106), channel_id=1, source_target_pairs={{0,1},{1,0},{2,3},{3,2},{4,5},{5,4},{6,7},{7,6},{8,9},{9,8},{10,11... | collective-permute-start | bytes 786440 | tf_op jit(solution)/shard_map/ppermute | solution.py:469
  46.7 2.0 %collective-permute-start.8 = (bf16[2,4,128,256]{3,2,1,0:T(8,128)(2,1)S(1)}, bf16[2,4,128,256]{3,2,1,0:T(8,128)(2,1)S(1)}, u32[]{:S(2)}, u32[]{:S(2)}) collective-permute-start(bf16[2,4,128,256]{3,2,1,0:T(8,128)(2,1)S(1)} %get-tuple-element.114), channel_id=1, source_target_pairs={{0,1},{1,0},{2,3},{3,2},{4,5},{5,4},{6,7},{7,6},{8,9},{9,8},{10,11... | collective-permute-start | bytes 1572872 | tf_op jit(solution)/shard_map/ppermute | solution.py:469
  48.7 8.4 %collective-permute-start.10 = (bf16[1,4,128,256]{3,2,1,0:T(8,128)(2,1)S(1)}, bf16[1,4,128,256]{3,2,1,0:T(8,128)(2,1)S(1)}, u32[]{:S(2)}, u32[]{:S(2)}) collective-permute-start(bf16[1,4,128,256]{3,2,1,0:T(8,128)(2,1)S(1)} %get-tuple-element.129), channel_id=1, source_target_pairs={{0,2},{1,3},{2,0},{3,1},{4,6},{5,7},{6,4},{7,5},{8,10},{9,11},{10,... | collective-permute-start | bytes 786440 | tf_op jit(solution)/shard_map/ppermute | solution.py:469
  53.4 3.8 %collective-permute-start.9 = (bf16[2,4,72,256]{3,2,1,0:T(8,128)(2,1)S(1)}, bf16[2,4,72,256]{3,2,1,0:T(8,128)(2,1)S(1)}, u32[]{:S(2)}, u32[]{:S(2)}) collective-permute-start(bf16[2,4,72,256]{3,2,1,0:T(8,128)(2,1)S(1)} %get-tuple-element.127), channel_id=1, source_target_pairs={{0,1},{1,0},{2,3},{3,2},{4,5},{5,4},{6,7},{7,6},{8,9},{9,8},{10,11... | collective-permute-start | bytes 884744 | tf_op jit(solution)/shard_map/ppermute | solution.py:469
  57.3 8.6 %collective-permute-start.11 = (bf16[2,128,256]{2,1,0:T(8,128)(2,1)S(1)}, bf16[2,128,256]{2,1,0:T(8,128)(2,1)S(1)}, u32[]{:S(2)}, u32[]{:S(2)}) collective-permute-start(bf16[2,128,256]{2,1,0:T(8,128)(2,1)S(1)} %get-tuple-element.131), channel_id=1, source_target_pairs={{0,4},{4,0},{8,12},{12,8},{1,5},{5,1},{9,13},{13,9},{2,6},{6,2},{1... | collective-permute-start | bytes 393224 | tf_op jit(solution)/shard_map/ppermute | solution.py:469
  59.1 5.2 %collective-permute-start.12 = (bf16[2,72,256]{2,1,0:T(8,128)(2,1)S(1)}, bf16[2,72,256]{2,1,0:T(8,128)(2,1)S(1)}, u32[]{:S(2)}, u32[]{:S(2)}) collective-permute-start(bf16[2,72,256]{2,1,0:T(8,128)(2,1)S(1)} %get-tuple-element.134), channel_id=1, source_target_pairs={{0,2},{1,3},{2,0},{3,1},{4,6},{5,7},{6,4},{7,5},{8,10},{9,11},{10,... | collective-permute-start | bytes 221192 | tf_op jit(solution)/shard_map/ppermute | solution.py:469
  59.7 5.0 %collective-permute-start.13 = (bf16[2,72,256]{2,1,0:T(8,128)(2,1)S(1)}, bf16[2,72,256]{2,1,0:T(8,128)(2,1)S(1)}, u32[]{:S(2)}, u32[]{:S(2)}) collective-permute-start(bf16[2,72,256]{2,1,0:T(8,128)(2,1)S(1)} %get-tuple-element.138), channel_id=1, source_target_pairs={{0,4},{4,0},{8,12},{12,8},{1,5},{5,1},{9,13},{13,9},{2,6},{6,2},{1... | collective-permute-start | bytes 221192 | tf_op jit(solution)/shard_map/ppermute | solution.py:469
  59.8 6.0 %collective-permute-start.14 = (bf16[2,72,256]{2,1,0:T(8,128)(2,1)S(1)}, bf16[2,72,256]{2,1,0:T(8,128)(2,1)S(1)}, u32[]{:S(2)}, u32[]{:S(2)}) collective-permute-start(bf16[2,72,256]{2,1,0:T(8,128)(2,1)S(1)} %get-tuple-element.139), channel_id=1, source_target_pairs={{0,6},{1,7},{2,4},{3,5},{4,2},{5,3},{6,0},{7,1},{8,14},{9,15},{10,... | collective-permute-start | bytes 221192 | tf_op jit(solution)/shard_map/ppermute | solution.py:469
  65.9 6.7 %collective-permute-start.15 = (bf16[200,256]{1,0:T(8,128)(2,1)S(1)}, bf16[200,256]{1,0:T(8,128)(2,1)S(1)}, u32[]{:S(2)}, u32[]{:S(2)}) collective-permute-start(bf16[200,256]{1,0:T(8,128)(2,1)S(1)} %get-tuple-element.141), channel_id=1, source_target_pairs={{0,8},{4,12},{8,0},{12,4},{1,9},{5,13},{9,1},{13,5},{2,10},{6,14},... | collective-permute-start | bytes 307208 | tf_op jit(solution)/shard_map/ppermute | solution.py:469
  68.7 18.0 %all-to-all-start.1 = ((bf16[16,64,256]{2,1,0:T(8,128)(2,1)}), bf16[16,64,256]{2,1,0:T(8,128)(2,1)S(1)}, u32[]{:S(2)}, u32[]{:S(2)}) async-start(bf16[16,64,256]{2,1,0:T(8,128)(2,1)} %bitcast.5), calls=%async_computation.1 | async-start | bytes 1048576 | tf_op jit(solution)/shard_map/all_to_all | solution.py:528
  72.6 8.3 %collective-permute-start.16 = (bf16[1,192,256]{2,1,0:T(8,128)(2,1)S(1)}, bf16[1,192,256]{2,1,0:T(8,128)(2,1)S(1)}, u32[]{:S(2)}, u32[]{:S(2)}) collective-permute-start(bf16[1,192,256]{2,1,0:T(8,128)(2,1)S(1)} %get-tuple-element.142), channel_id=1, source_target_pairs={{0,2},{1,3},{2,0},{3,1},{4,6},{5,7},{6,4},{7,5},{8,10},{9,11},{10,... | collective-permute-start | bytes 294920 | tf_op jit(solution)/shard_map/ppermute | solution.py:469
  74.3 12.4 %copy-start.8 = (s32[1,512]{1,0:T(1,128)S(1)}, s32[1,512]{1,0:T(1,128)}, u32[]{:S(2)}) copy-start(s32[1,512]{1,0:T(1,128)} %get-tuple-element.79.refs_0_) | copy-start | bytes 6148
  80.9 1.5 %collective-permute-start.17 = (bf16[2,192,256]{2,1,0:T(8,128)(2,1)S(1)}, bf16[2,192,256]{2,1,0:T(8,128)(2,1)S(1)}, u32[]{:S(2)}, u32[]{:S(2)}) collective-permute-start(bf16[2,192,256]{2,1,0:T(8,128)(2,1)S(1)} %constant_dynamic-update-slice_fusion.refs_0_), channel_id=1, source_target_pairs={{0,1},{1,0},{2,3},{3,2},{4,5},{5,4},{6,7},{7,6},{8,9},{9,8},{10,11... | collective-permute-start | bytes 589832 | tf_op jit(solution)/shard_map/ppermute | solution.py:469
  (5 other events, 29.2 us)

commit v8 on v4

--- a/solution.py
+++ b/solution.py
@@ -100,7 +100,6 @@
     rank = (jnp.sum(counts * owned, axis=0, keepdims=True) - 1.0).astype(jnp.int32)
     slot = owner * cap + rank
     slot_ref[...] = slot
-    packed = mm(one_hot(slot, (slots, rows), 0), points_ref[...]).astype(BF16)
     within = one_hot(rank, (cap, rows), 0)
     within = jnp.concatenate([within] * (128 // cap), axis=0)
     high = (lax.shift_right_logical(target, 4) + 1).astype(F32)
@@ -109,15 +108,19 @@
     low_rows = mm_nt((owned * low).astype(BF16), within)
     if direct:
         (msg_ref,) = out_refs
-        msg_ref[:, :cap, :] = packed[:, :128].reshape(peers, cap, 128)
-        msg_ref[:, cap : 2 * cap, :] = packed[:, 128:].reshape(peers, cap, 128)
         first = iota((META, 128), 0) == 0
-        for peer in range(peers):
-            block = jnp.where(first, high_rows[peer : peer + 1], low_rows[peer : peer + 1])
-            msg_ref[peer, 2 * cap :, :] = block.astype(BF16)
+        half = peers // 2
+        for start in (0, half):
+            packed = mm(one_hot(slot - start * cap, (half * cap, rows), 0), points_ref[...]).astype(BF16)
+            msg_ref[start : start + half, :cap, :] = packed[:, :128].reshape(half, cap, 128)
+            msg_ref[start : start + half, cap : 2 * cap, :] = packed[:, 128:].reshape(half, cap, 128)
+            for peer in range(start, start + half):
+                block = jnp.where(first, high_rows[peer : peer + 1], low_rows[peer : peer + 1])
+                msg_ref[peer, 2 * cap :, :] = block.astype(BF16)
+            send(msg_ref, start + half)
     else:
         packed_ref, high_ref, low_ref = out_refs
-        packed_ref[...] = packed
+        packed_ref[...] = mm(one_hot(slot, (slots, rows), 0), points_ref[...]).astype(BF16)
         high_ref[...] = high_rows
         low_ref[...] = low_rows
 
@@ -178,7 +181,7 @@
         tails = [msg_ref[peer, 2 * cap :, :].astype(F32) for peer in range(peers)]
         high_rows = jnp.concatenate([tail[0:1] for tail in tails], axis=0)
         low_rows = jnp.concatenate([tail[1:2] for tail in tails], axis=0)
-    target_ref, target_col_ref, rotated_ref = refs[-3:]
+    gather_ref, place_ref, rotated_ref = refs[-3:]
     rows = rotated_ref.shape[1]
     slots = peers * cap
     targets = (high_rows - 1.0) * 16.0 + low_rows
@@ -189,9 +192,10 @@
         block = targets[group * per_row : (group + 1) * per_row]
         pieces.append(jnp.sum(jnp.where(own_lane, block, 0.0), axis=0, keepdims=True))
     target = jnp.concatenate(pieces, axis=1)
-    target_ref[...] = target.astype(jnp.int32)
-    target_col_ref[...] = column_of(target).astype(jnp.int32)
-    rotated_ref[...] = mm(one_hot(target.astype(jnp.int32), (rows, slots), 0), recv).T
+    gather = one_hot(target.astype(jnp.int32), (rows, slots), 0)
+    gather_ref[...] = gather
+    rotated_ref[...] = mm(gather, recv).T
+    place_ref[...] = one_hot(lane_tile(column_of(target).astype(jnp.int32), rows), (slots, rows), 1)
 
 
 def forward_kernel(
@@ -277,7 +281,7 @@
 
 
 def mlp_weights_kernel(
-    arranged, direct, target_ref, hidden_ref, slope_ref, normed_two_ref, w_down_ref, *refs
+    arranged, direct, gather_ref, hidden_ref, slope_ref, normed_two_ref, w_down_ref, *refs
 ):
     width, rows = normed_two_ref.shape
     if direct:
@@ -290,7 +294,7 @@
         recv_ref, *refs = refs
     grad_pre_ref, cot_t_ref, *mat_refs = refs
     recv = recv_ref[...].reshape(-1, width)
-    cot_f = mm(one_hot(target_ref[...], (rows, recv.shape[0]), 0), recv)
+    cot_f = mm(gather_ref[...], recv)
     cot = cot_f.astype(BF16)
     cot_t = cot_f.T
     cot_t_ref[...] = cot_t
@@ -361,7 +365,7 @@
 def attention_backward_kernel(
     arranged,
     qkv_t_ref, kv_ref, scales_ref, grad_att_ref, grad_middle_ref, norm_one_ref, normed_one_ref,
-    w_qkv_ref, gain_attn_ref, target_col_ref, gain_two_ref, grad_out_ref, *refs,
+    w_qkv_ref, gain_attn_ref, place_ref, gain_two_ref, grad_out_ref, *refs,
 ):
     width, rows = norm_one_ref.shape
     probs_refs, refs = refs[: rows // BALL], refs[rows // BALL :]
@@ -374,8 +378,7 @@
     gain_one = gain_row(grad_normed * norm_one)
     gain = lane_tile(gain_attn_ref[...], rows)
     grad_rot = grad_middle_ref[...] + norm_backward(grad_normed, norm_one, scales_ref[0:1, :], gain)
-    place = one_hot(lane_tile(target_col_ref[...], rows), (back_ref.shape[0], rows), 1)
-    back_ref[...] = mm_nt(place, grad_rot.astype(BF16)).astype(BF16)
+    back_ref[...] = mm_nt(place_ref[...], grad_rot.astype(BF16)).astype(BF16)
     normed_one = normed_one_ref[...]
     if not arranged:
         mat_refs[0][...] = mm_nt(normed_one, grad_rows).astype(BF16)
@@ -575,9 +578,9 @@
     else:
         (packed_cot,) = call(pack_cot_kernel, [((slots, width), BF16)], "pack_cot", 1, slot, cotangent)
         arrived_cot = [exchange(packed_cot, axes, peers)]
-    target, target_col, rotated = call(
+    gather, place, rotated = call(
         functools.partial(unpack_points_kernel, cap, peers, direct),
-        [((1, slots), jnp.int32), ((slots, 128), jnp.int32), ((width, rows), F32)],
+        [((rows, slots), BF16), ((slots, rows), BF16), ((width, rows), F32)],
         "unpack_points", 2, *forward_args,
     )
     (
@@ -613,7 +616,7 @@
     grad_pre, cot_t, *mlp_grads = call(
         functools.partial(mlp_weights_kernel, arranged, by_permute),
         [((hidden_width, rows), BF16), ((width, rows), F32)] + mlp_mats,
-        "mlp_weights", 2.5, target, hidden, slope, normed_two, w_down, *arrived_cot,
+        "mlp_weights", 2.5, gather, hidden, slope, normed_two, w_down, *arrived_cot,
         scratch=mlp_scratch + ([pltpu.VMEM((peers, cap, width), BF16)] if by_permute else []),
     )
     gain_two, grad_middle, grad_att, grad_out = call(
@@ -634,7 +637,7 @@
         functools.partial(attention_backward_kernel, arranged),
         [((slots, width), BF16)] + qkv_mats, "attention_backward", 6,
         qkv_t, kv, scales, grad_att, grad_middle, norm_one, normed_one,
-        w_qkv, gain_attn_col, target_col, gain_two, grad_out, *probs,
+        w_qkv, gain_attn_col, place, gain_two, grad_out, *probs,
         scratch=qkv_scratch + [pltpu.VMEM((3 * width, rows), BF16)],
     )
     if not arranged:

time: 83.7 us -> 83.7 us (level)
  transfers between devices with their start and end apart: 20 -> 20, of which waited for: 13 -> 13; matrix products, arithmetic and copies ran while one was open for 1% -> 1% of each run, Pallas kernels for 14% -> 15%
where the time goes in v8:
time: 83.7 us; the launch traced here: 83.3 us
  starting transfers between devices  37.1 us (44%)
  waiting for transfers between devices  25.2 us (30%)
  Pallas kernels  18.8 us (22%)
  local copies, waits for them, and re-layouts  1.25 us (1%)
  between operations  0.85 us (1%)
    ppermute x18, starting transfers between devices, permute(): return lax.ppermute(value, axis, [(i, i ^ bit) for i in range(size)])  25.2 us
    ppermute x18, waiting for transfers between devices, permute(): return lax.ppermute(value, axis, [(i, i ^ bit) for i in range(size)])  21.9 us
    pallas_call x15, Pallas kernels, call(): pl.pallas_call(body, out_shape=[jax.ShapeDtypeStruct(shape, dtype) for sh...  18.8 us
    all_to_all x2, starting transfers between devices, exchange(): lax.all_to_all(flat.reshape((peers, -1) + flat.shape[1:]), axes, split_ax...  11.9 us
    all_to_all x2, waiting for transfers between devices, exchange(): lax.all_to_all(flat.reshape((peers, -1) + flat.shape[1:]), axes, split_ax...  3.28 us
  transfers between devices with their start and end apart: 20, of which 13 were waited for; matrix products, arithmetic and copies ran while one was open for 1% of the time, Pallas kernels for 15%

profile of v8, /device:TPU:0, one launch (start us, length us, event | category | flops | bytes accessed | tf_op | source)
XLA Modules:
  0.0 83.3 jit_solution(17879570910161476536)
XLA Ops:
  0.6 2.5 %pack_points.1 = (s32[1,512]{1,0:T(1,128)}, bf16[16,144,128]{2,1,0:T(8,128)(2,1)}) custom-call(s32[1,512]{1,0:T(1,128)} %bitcast.16, bf16[512,256]{1,0:T(8,128)(2,1)} %refs_1_.3), custom_call_target="tpu_custom_call" | custom-call | flops 2200000000 | bytes 856064 | tf_op jit(solution)/shard_map/pack_points/pallas_call | solution.py:518
  3.1 7.4 %all-to-all-start = ((bf16[16,144,128]{2,1,0:T(8,128)(2,1)}), bf16[16,144,128]{2,1,0:T(8,128)(2,1)S(1)}, u32[]{:S(2)}, u32[]{:S(2)}) async-start(bf16[16,144,128]{2,1,0:T(8,128)(2,1)} %get-tuple-element.86), calls=%async_computation | async-start | bytes 1179648 | tf_op jit(solution)/shard_map/all_to_all | solution.py:531
  11.7 2.0 %collective-permute-start = (bf16[2,64,256]{2,1,0:T(8,128)(2,1)S(1)}, bf16[2,64,256]{2,1,0:T(8,128)(2,1)S(1)}, u32[]{:S(2)}, u32[]{:S(2)}) collective-permute-start(bf16[2,64,256]{2,1,0:T(8,128)(2,1)S(1)} %get-tuple-element.84), channel_id=1, source_target_pairs={{0,2},{1,3},{2,0},{3,1},{4,6},{5,7},{6,4},{7,5},{8,10},{9,11},{10,... | collective-permute-start | bytes 196616 | tf_op jit(solution)/shard_map/ppermute | solution.py:472
  13.7 1.5 %collective-permute-start.1 = (bf16[2,64,256]{2,1,0:T(8,128)(2,1)S(1)}, bf16[2,64,256]{2,1,0:T(8,128)(2,1)S(1)}, u32[]{:S(2)}, u32[]{:S(2)}) collective-permute-start(bf16[2,64,256]{2,1,0:T(8,128)(2,1)S(1)} %get-tuple-element.85), channel_id=1, source_target_pairs={{0,4},{1,5},{2,6},{3,7},{4,0},{5,1},{6,2},{7,3},{8,12},{9,13},{10,... | collective-permute-start | bytes 196616 | tf_op jit(solution)/shard_map/ppermute | solution.py:472
  15.2 2.8 %collective-permute-start.3 = (bf16[2,64,256]{2,1,0:T(8,128)(2,1)S(1)}, bf16[2,64,256]{2,1,0:T(8,128)(2,1)S(1)}, u32[]{:S(2)}, u32[]{:S(2)}) collective-permute-start(bf16[2,64,256]{2,1,0:T(8,128)(2,1)S(1)} %get-tuple-element.96), channel_id=1, source_target_pairs={{0,8},{1,9},{2,10},{3,11},{4,12},{5,13},{6,14},{7,15},{8,0},{9,1},... | collective-permute-start | bytes 196616 | tf_op jit(solution)/shard_map/ppermute | solution.py:472
  18.1 1.5 %collective-permute-start.4 = (bf16[2,64,256]{2,1,0:T(8,128)(2,1)S(1)}, bf16[2,64,256]{2,1,0:T(8,128)(2,1)S(1)}, u32[]{:S(2)}, u32[]{:S(2)}) collective-permute-start(bf16[2,64,256]{2,1,0:T(8,128)(2,1)S(1)} %get-tuple-element.97), channel_id=1, source_target_pairs={{0,10},{1,11},{2,8},{3,9},{4,14},{5,15},{6,12},{7,13},{8,2},{9,3},... | collective-permute-start | bytes 196616 | tf_op jit(solution)/shard_map/ppermute | solution.py:472
  19.5 3.3 %collective-permute-start.5 = (bf16[2,64,256]{2,1,0:T(8,128)(2,1)S(1)}, bf16[2,64,256]{2,1,0:T(8,128)(2,1)S(1)}, u32[]{:S(2)}, u32[]{:S(2)}) collective-permute-start(bf16[2,64,256]{2,1,0:T(8,128)(2,1)S(1)} %get-tuple-element.98), channel_id=1, source_target_pairs={{0,12},{1,13},{2,14},{3,15},{4,8},{5,9},{6,10},{7,11},{8,4},{9,5},... | collective-permute-start | bytes 196616 | tf_op jit(solution)/shard_map/ppermute | solution.py:472
  23.5 4.0 %collective-permute-start.6 = (bf16[2,64,256]{2,1,0:T(8,128)(2,1)S(1)}, bf16[2,64,256]{2,1,0:T(8,128)(2,1)S(1)}, u32[]{:S(2)}, u32[]{:S(2)}) collective-permute-start(bf16[2,64,256]{2,1,0:T(8,128)(2,1)S(1)} %get-tuple-element.99), channel_id=1, source_target_pairs={{0,14},{1,15},{2,12},{3,13},{4,10},{5,11},{6,8},{7,9},{8,6},{9,7},... | collective-permute-start | bytes 196616 | tf_op jit(solution)/shard_map/ppermute | solution.py:472
  28.4 4.5 %forward.1 = (bf16[768,512]{1,0:T(8,128)(2,1)S(1)}, bf16[512,512]{1,0:T(8,128)(2,1)S(1)}, f32[8,512]{1,0:T(8,128)S(1)}, f32[256,512]{1,0:T(8,128)S(1)}, bf16[256...) custom-call(f32[256,512]{1,0:T(8,128)S(1)} %get-tuple-element.88.ref, ...), custom_call_target="tpu_custom_call" | custom-call | flops 7699999744 | bytes 12339200 | tf_op jit(solution)/shard_map/forward/pallas_call | solution.py:518
  32.9 1.8 %collective-permute-done.3.refs_4_ = bf16[2,64,256]{2,1,0:T(8,128)(2,1)S(1)} collective-permute-done((bf16[2,64,256]{2,1,0:T(8,128)(2,1)S(1)}, bf16[2,64,256]{2,1,0:T(8,128)(2,1)S(1)}, u32[]{:S(2)}, u32[]{:S(2)}) %collective-permute-start.3) | collective-permute-done | bytes 65568 | tf_op jit(solution)/shard_map/ppermute | solution.py:472
  34.7 2.3 %collective-permute-done.4.refs_5_ = bf16[2,64,256]{2,1,0:T(8,128)(2,1)S(1)} collective-permute-done((bf16[2,64,256]{2,1,0:T(8,128)(2,1)S(1)}, bf16[2,64,256]{2,1,0:T(8,128)(2,1)S(1)}, u32[]{:S(2)}, u32[]{:S(2)}) %collective-permute-start.4) | collective-permute-done | bytes 65568 | tf_op jit(solution)/shard_map/ppermute | solution.py:472
  37.2 1.5 %collective-permute-done.7.refs_6_ = bf16[8,64,256]{2,1,0:T(8,128)(2,1)S(1)} collective-permute-done((bf16[8,64,256]{2,1,0:T(8,128)(2,1)S(1)}, bf16[8,64,256]{2,1,0:T(8,128)(2,1)S(1)}, u32[]{:S(2)}, u32[]{:S(2)}) %collective-permute-start.7) | collective-permute-done | bytes 262176 | tf_op jit(solution)/shard_map/ppermute | solution.py:472
  38.7 2.6 %mlp_weights.1 = (bf16[1024,512]{1,0:T(8,128)(2,1)S(1)}, f32[256,512]{1,0:T(8,128)S(1)}, f32[2,4,128,256]{3,2,1,0:T(8,128)S(1)}, bf16[2,4,128,256]{3,2,1,0:T(8,128)(2,1)S(1)}) custom-call(bf16[512,1024]{1,0:T(8,128)(2,1)S(1)} %get-tuple-element.101.refs_0_, bf16[1024,512]{1,0:T(8,128)(2,1)S(1)} %get-tuple-element.102.refs_1_, ...), custom_call_target="tpu_custom_call" | custom-call | flops 2750000128 | bytes 8650752 | tf_op jit(solution)/shard_map/mlp_weights/pallas_call | solution.py:518
  44.0 4.6 %attention_backward.1 = (bf16[1024,256]{1,0:T(8,128)(2,1)}, f32[2,4,72,256]{3,2,1,0:T(8,128)S(1)}, bf16[2,4,72,256]{3,2,1,0:T(8,128)(2,1)S(1)}) custom-call(bf16[768,512]{1,0:T(8,128)(2,1)S(1)} %get-tuple-element.89.refs_0_, bf16[512,512]{1,0:T(8,128)(2,1)S(1)} %get-tuple-element.90.refs_1_, f32[8,512]{1,0:T(8,128)S(1)} %get-tuple-element.100.refs_3_.refs_2_, ...), custom_call_target="tpu_custom_call" | custom-call | flops 6600000000 | bytes 10339328 | tf_op jit(solution)/shard_map/attention_backward/pallas_call | solution.py:518
  48.5 3.3 %collective-permute-done.10 = bf16[1,4,128,256]{3,2,1,0:T(8,128)(2,1)S(1)} collective-permute-done((bf16[1,4,128,256]{3,2,1,0:T(8,128)(2,1)S(1)}, bf16[1,4,128,256]{3,2,1,0:T(8,128)(2,1)S(1)}, u32[]{:S(2)}, u32[]{:S(2)}) %collective-permute-start.10) | collective-permute-done | bytes 262176 | tf_op jit(solution)/shard_map/ppermute | solution.py:472
  51.9 3.0 %collective-permute-start.11 = (bf16[2,128,256]{2,1,0:T(8,128)(2,1)S(1)}, bf16[2,128,256]{2,1,0:T(8,128)(2,1)S(1)}, u32[]{:S(2)}, u32[]{:S(2)}) collective-permute-start(bf16[2,128,256]{2,1,0:T(8,128)(2,1)S(1)} %get-tuple-element.139), channel_id=1, source_target_pairs={{0,4},{4,0},{8,12},{12,8},{1,5},{5,1},{9,13},{13,9},{2,6},{6,2},{1... | collective-permute-start | bytes 393224 | tf_op jit(solution)/shard_map/ppermute | solution.py:472
  55.5 2.9 %collective-permute-start.14 = (bf16[2,72,256]{2,1,0:T(8,128)(2,1)S(1)}, bf16[2,72,256]{2,1,0:T(8,128)(2,1)S(1)}, u32[]{:S(2)}, u32[]{:S(2)}) collective-permute-start(bf16[2,72,256]{2,1,0:T(8,128)(2,1)S(1)} %get-tuple-element.147), channel_id=1, source_target_pairs={{0,6},{1,7},{2,4},{3,5},{4,2},{5,3},{6,0},{7,1},{8,14},{9,15},{10,... | collective-permute-start | bytes 221192 | tf_op jit(solution)/shard_map/ppermute | solution.py:472
  58.5 1.7 %collective-permute-done.12.refs_3_ = bf16[2,72,256]{2,1,0:T(8,128)(2,1)S(1)} collective-permute-done((bf16[2,72,256]{2,1,0:T(8,128)(2,1)S(1)}, bf16[2,72,256]{2,1,0:T(8,128)(2,1)S(1)}, u32[]{:S(2)}, u32[]{:S(2)}) %collective-permute-start.12) | collective-permute-done | bytes 73760 | tf_op jit(solution)/shard_map/ppermute | solution.py:472
  60.2 1.4 %collective-permute-done.14.refs_5_ = bf16[2,72,256]{2,1,0:T(8,128)(2,1)S(1)} collective-permute-done((bf16[2,72,256]{2,1,0:T(8,128)(2,1)S(1)}, bf16[2,72,256]{2,1,0:T(8,128)(2,1)S(1)}, u32[]{:S(2)}, u32[]{:S(2)}) %collective-permute-start.14) | collective-permute-done | bytes 73760 | tf_op jit(solution)/shard_map/ppermute | solution.py:472
  61.7 1.4 %collective-permute-start.15 = (bf16[200,256]{1,0:T(8,128)(2,1)S(1)}, bf16[200,256]{1,0:T(8,128)(2,1)S(1)}, u32[]{:S(2)}, u32[]{:S(2)}) collective-permute-start(bf16[200,256]{1,0:T(8,128)(2,1)S(1)} %get-tuple-element.149), channel_id=1, source_target_pairs={{0,8},{4,12},{8,0},{12,4},{1,9},{5,13},{9,1},{13,5},{2,10},{6,14},... | collective-permute-start | bytes 307208 | tf_op jit(solution)/shard_map/ppermute | solution.py:472
  63.1 4.5 %all-to-all-start.1 = ((bf16[16,64,256]{2,1,0:T(8,128)(2,1)}), bf16[16,64,256]{2,1,0:T(8,128)(2,1)S(1)}, u32[]{:S(2)}, u32[]{:S(2)}) async-start(bf16[16,64,256]{2,1,0:T(8,128)(2,1)} %bitcast.5), calls=%async_computation.1 | async-start | bytes 1048576 | tf_op jit(solution)/shard_map/all_to_all | solution.py:531
  68.4 1.2 %collective-permute-start.16 = (bf16[1,192,256]{2,1,0:T(8,128)(2,1)S(1)}, bf16[1,192,256]{2,1,0:T(8,128)(2,1)S(1)}, u32[]{:S(2)}, u32[]{:S(2)}) collective-permute-start(bf16[1,192,256]{2,1,0:T(8,128)(2,1)S(1)} %get-tuple-element.150), channel_id=1, source_target_pairs={{0,2},{1,3},{2,0},{3,1},{4,6},{5,7},{6,4},{7,5},{8,10},{9,11},{10,... | collective-permute-start | bytes 294920 | tf_op jit(solution)/shard_map/ppermute | solution.py:472
  69.7 6.6 %collective-permute-done.16 = bf16[1,192,256]{2,1,0:T(8,128)(2,1)S(1)} collective-permute-done((bf16[1,192,256]{2,1,0:T(8,128)(2,1)S(1)}, bf16[1,192,256]{2,1,0:T(8,128)(2,1)S(1)}, u32[]{:S(2)}, u32[]{:S(2)}) %collective-permute-start.16) | collective-permute-done | bytes 98336 | tf_op jit(solution)/shard_map/ppermute | solution.py:472
  78.8 3.3 %all-to-all-done.1 = bf16[16,64,256]{2,1,0:T(8,128)(2,1)S(1)} async-done(((bf16[16,64,256]{2,1,0:T(8,128)(2,1)}), bf16[16,64,256]{2,1,0:T(8,128)(2,1)S(1)}, u32[]{:S(2)}, u32[]{:S(2)}) %all-to-all-start.1) | async-done | bytes 524320 | tf_op jit(solution)/shard_map/all_to_all | solution.py:531
  (53 shorter events, 11.0 us)
Async XLA Ops:
  0.6 9.9 %copy-start.3 = (bf16[512,256]{1,0:T(8,128)(2,1)S(1)}, bf16[512,256]{1,0:T(8,128)(2,1)}, u32[]{:S(2)}) copy-start(bf16[512,256]{1,0:T(8,128)(2,1)} %refs_1_.4) | copy-start | bytes 786436
  3.1 24.3 %all-to-all-start = ((bf16[16,144,128]{2,1,0:T(8,128)(2,1)}), bf16[16,144,128]{2,1,0:T(8,128)(2,1)S(1)}, u32[]{:S(2)}, u32[]{:S(2)}) async-start(bf16[16,144,128]{2,1,0:T(8,128)(2,1)} %get-tuple-element.86), calls=%async_computation | async-start | bytes 1179648 | tf_op jit(solution)/shard_map/all_to_all | solution.py:531
  11.7 7.8 %collective-permute-start = (bf16[2,64,256]{2,1,0:T(8,128)(2,1)S(1)}, bf16[2,64,256]{2,1,0:T(8,128)(2,1)S(1)}, u32[]{:S(2)}, u32[]{:S(2)}) collective-permute-start(bf16[2,64,256]{2,1,0:T(8,128)(2,1)S(1)} %get-tuple-element.84), channel_id=1, source_target_pairs={{0,2},{1,3},{2,0},{3,1},{4,6},{5,7},{6,4},{7,5},{8,10},{9,11},{10,... | collective-permute-start | bytes 196616 | tf_op jit(solution)/shard_map/ppermute | solution.py:472
  13.7 9.8 %collective-permute-start.1 = (bf16[2,64,256]{2,1,0:T(8,128)(2,1)S(1)}, bf16[2,64,256]{2,1,0:T(8,128)(2,1)S(1)}, u32[]{:S(2)}, u32[]{:S(2)}) collective-permute-start(bf16[2,64,256]{2,1,0:T(8,128)(2,1)S(1)} %get-tuple-element.85), channel_id=1, source_target_pairs={{0,4},{1,5},{2,6},{3,7},{4,0},{5,1},{6,2},{7,3},{8,12},{9,13},{10,... | collective-permute-start | bytes 196616 | tf_op jit(solution)/shard_map/ppermute | solution.py:472
  15.1 17.8 %collective-permute-start.2 = (bf16[2,64,256]{2,1,0:T(8,128)(2,1)S(1)}, bf16[2,64,256]{2,1,0:T(8,128)(2,1)S(1)}, u32[]{:S(2)}, u32[]{:S(2)}) collective-permute-start(bf16[2,64,256]{2,1,0:T(8,128)(2,1)S(1)} %get-tuple-element.95), channel_id=1, source_target_pairs={{0,6},{1,7},{2,4},{3,5},{4,2},{5,3},{6,0},{7,1},{8,14},{9,15},{10,... | collective-permute-start | bytes 196616 | tf_op jit(solution)/shard_map/ppermute | solution.py:472
  15.2 19.5 %collective-permute-start.3 = (bf16[2,64,256]{2,1,0:T(8,128)(2,1)S(1)}, bf16[2,64,256]{2,1,0:T(8,128)(2,1)S(1)}, u32[]{:S(2)}, u32[]{:S(2)}) collective-permute-start(bf16[2,64,256]{2,1,0:T(8,128)(2,1)S(1)} %get-tuple-element.96), channel_id=1, source_target_pairs={{0,8},{1,9},{2,10},{3,11},{4,12},{5,13},{6,14},{7,15},{8,0},{9,1},... | collective-permute-start | bytes 196616 | tf_op jit(solution)/shard_map/ppermute | solution.py:472
  18.1 19.0 %collective-permute-start.4 = (bf16[2,64,256]{2,1,0:T(8,128)(2,1)S(1)}, bf16[2,64,256]{2,1,0:T(8,128)(2,1)S(1)}, u32[]{:S(2)}, u32[]{:S(2)}) collective-permute-start(bf16[2,64,256]{2,1,0:T(8,128)(2,1)S(1)} %get-tuple-element.97), channel_id=1, source_target_pairs={{0,10},{1,11},{2,8},{3,9},{4,14},{5,15},{6,12},{7,13},{8,2},{9,3},... | collective-permute-start | bytes 196616 | tf_op jit(solution)/shard_map/ppermute | solution.py:472
  19.5 17.5 %collective-permute-start.5 = (bf16[2,64,256]{2,1,0:T(8,128)(2,1)S(1)}, bf16[2,64,256]{2,1,0:T(8,128)(2,1)S(1)}, u32[]{:S(2)}, u32[]{:S(2)}) collective-permute-start(bf16[2,64,256]{2,1,0:T(8,128)(2,1)S(1)} %get-tuple-element.98), channel_id=1, source_target_pairs={{0,12},{1,13},{2,14},{3,15},{4,8},{5,9},{6,10},{7,11},{8,4},{9,5},... | collective-permute-start | bytes 196616 | tf_op jit(solution)/shard_map/ppermute | solution.py:472
  23.5 4.9 %copy-start.6 = (f32[256]{0:T(256)S(1)}, f32[256]{0:T(256)}, u32[]{:S(2)}) copy-start(f32[256]{0:T(256)} %param.17) | copy-start | bytes 3076
  23.5 13.6 %collective-permute-start.6 = (bf16[2,64,256]{2,1,0:T(8,128)(2,1)S(1)}, bf16[2,64,256]{2,1,0:T(8,128)(2,1)S(1)}, u32[]{:S(2)}, u32[]{:S(2)}) collective-permute-start(bf16[2,64,256]{2,1,0:T(8,128)(2,1)S(1)} %get-tuple-element.99), channel_id=1, source_target_pairs={{0,14},{1,15},{2,12},{3,13},{4,10},{5,11},{6,8},{7,9},{8,6},{9,7},... | collective-permute-start | bytes 196616 | tf_op jit(solution)/shard_map/ppermute | solution.py:472
  28.4 10.3 %copy-start = (bf16[1024,256]{1,0:T(8,128)(2,1)S(1)}, bf16[1024,256]{1,0:T(8,128)(2,1)}, u32[]{:S(2)}) copy-start(bf16[1024,256]{1,0:T(8,128)(2,1)} %refs_4_.1) | copy-start | bytes 1572868
  37.1 1.6 %collective-permute-start.7 = (bf16[8,64,256]{2,1,0:T(8,128)(2,1)S(1)}, bf16[8,64,256]{2,1,0:T(8,128)(2,1)S(1)}, u32[]{:S(2)}, u32[]{:S(2)}) collective-permute-start(bf16[8,64,256]{2,1,0:T(8,128)(2,1)S(1)} %get-tuple-element.114), channel_id=1, source_target_pairs={{0,1},{1,0},{2,3},{3,2},{4,5},{5,4},{6,7},{7,6},{8,9},{9,8},{10,11... | collective-permute-start | bytes 786440 | tf_op jit(solution)/shard_map/ppermute | solution.py:472
  41.3 2.0 %collective-permute-start.8 = (bf16[2,4,128,256]{3,2,1,0:T(8,128)(2,1)S(1)}, bf16[2,4,128,256]{3,2,1,0:T(8,128)(2,1)S(1)}, u32[]{:S(2)}, u32[]{:S(2)}) collective-permute-start(bf16[2,4,128,256]{3,2,1,0:T(8,128)(2,1)S(1)} %get-tuple-element.122), channel_id=1, source_target_pairs={{0,1},{1,0},{2,3},{3,2},{4,5},{5,4},{6,7},{7,6},{8,9},{9,8},{10,11... | collective-permute-start | bytes 1572872 | tf_op jit(solution)/shard_map/ppermute | solution.py:472
  43.4 8.5 %collective-permute-start.10 = (bf16[1,4,128,256]{3,2,1,0:T(8,128)(2,1)S(1)}, bf16[1,4,128,256]{3,2,1,0:T(8,128)(2,1)S(1)}, u32[]{:S(2)}, u32[]{:S(2)}) collective-permute-start(bf16[1,4,128,256]{3,2,1,0:T(8,128)(2,1)S(1)} %get-tuple-element.137), channel_id=1, source_target_pairs={{0,2},{1,3},{2,0},{3,1},{4,6},{5,7},{6,4},{7,5},{8,10},{9,11},{10,... | collective-permute-start | bytes 786440 | tf_op jit(solution)/shard_map/ppermute | solution.py:472
  48.5 3.4 %collective-permute-start.9 = (bf16[2,4,72,256]{3,2,1,0:T(8,128)(2,1)S(1)}, bf16[2,4,72,256]{3,2,1,0:T(8,128)(2,1)S(1)}, u32[]{:S(2)}, u32[]{:S(2)}) collective-permute-start(bf16[2,4,72,256]{3,2,1,0:T(8,128)(2,1)S(1)} %get-tuple-element.135), channel_id=1, source_target_pairs={{0,1},{1,0},{2,3},{3,2},{4,5},{5,4},{6,7},{7,6},{8,9},{9,8},{10,11... | collective-permute-start | bytes 884744 | tf_op jit(solution)/shard_map/ppermute | solution.py:472
  51.9 9.7 %collective-permute-start.11 = (bf16[2,128,256]{2,1,0:T(8,128)(2,1)S(1)}, bf16[2,128,256]{2,1,0:T(8,128)(2,1)S(1)}, u32[]{:S(2)}, u32[]{:S(2)}) collective-permute-start(bf16[2,128,256]{2,1,0:T(8,128)(2,1)S(1)} %get-tuple-element.139), channel_id=1, source_target_pairs={{0,4},{4,0},{8,12},{12,8},{1,5},{5,1},{9,13},{13,9},{2,6},{6,2},{1... | collective-permute-start | bytes 393224 | tf_op jit(solution)/shard_map/ppermute | solution.py:472
  54.9 5.2 %collective-permute-start.12 = (bf16[2,72,256]{2,1,0:T(8,128)(2,1)S(1)}, bf16[2,72,256]{2,1,0:T(8,128)(2,1)S(1)}, u32[]{:S(2)}, u32[]{:S(2)}) collective-permute-start(bf16[2,72,256]{2,1,0:T(8,128)(2,1)S(1)} %get-tuple-element.142), channel_id=1, source_target_pairs={{0,2},{1,3},{2,0},{3,1},{4,6},{5,7},{6,4},{7,5},{8,10},{9,11},{10,... | collective-permute-start | bytes 221192 | tf_op jit(solution)/shard_map/ppermute | solution.py:472
  55.5 4.7 %collective-permute-start.13 = (bf16[2,72,256]{2,1,0:T(8,128)(2,1)S(1)}, bf16[2,72,256]{2,1,0:T(8,128)(2,1)S(1)}, u32[]{:S(2)}, u32[]{:S(2)}) collective-permute-start(bf16[2,72,256]{2,1,0:T(8,128)(2,1)S(1)} %get-tuple-element.146), channel_id=1, source_target_pairs={{0,4},{4,0},{8,12},{12,8},{1,5},{5,1},{9,13},{13,9},{2,6},{6,2},{1... | collective-permute-start | bytes 221192 | tf_op jit(solution)/shard_map/ppermute | solution.py:472
  55.5 6.0 %collective-permute-start.14 = (bf16[2,72,256]{2,1,0:T(8,128)(2,1)S(1)}, bf16[2,72,256]{2,1,0:T(8,128)(2,1)S(1)}, u32[]{:S(2)}, u32[]{:S(2)}) collective-permute-start(bf16[2,72,256]{2,1,0:T(8,128)(2,1)S(1)} %get-tuple-element.147), channel_id=1, source_target_pairs={{0,6},{1,7},{2,4},{3,5},{4,2},{5,3},{6,0},{7,1},{8,14},{9,15},{10,... | collective-permute-start | bytes 221192 | tf_op jit(solution)/shard_map/ppermute | solution.py:472
  61.7 6.7 %collective-permute-start.15 = (bf16[200,256]{1,0:T(8,128)(2,1)S(1)}, bf16[200,256]{1,0:T(8,128)(2,1)S(1)}, u32[]{:S(2)}, u32[]{:S(2)}) collective-permute-start(bf16[200,256]{1,0:T(8,128)(2,1)S(1)} %get-tuple-element.149), channel_id=1, source_target_pairs={{0,8},{4,12},{8,0},{12,4},{1,9},{5,13},{9,1},{13,5},{2,10},{6,14},... | collective-permute-start | bytes 307208 | tf_op jit(solution)/shard_map/ppermute | solution.py:472
  63.1 19.0 %all-to-all-start.1 = ((bf16[16,64,256]{2,1,0:T(8,128)(2,1)}), bf16[16,64,256]{2,1,0:T(8,128)(2,1)S(1)}, u32[]{:S(2)}, u32[]{:S(2)}) async-start(bf16[16,64,256]{2,1,0:T(8,128)(2,1)} %bitcast.5), calls=%async_computation.1 | async-start | bytes 1048576 | tf_op jit(solution)/shard_map/all_to_all | solution.py:531
  68.4 7.9 %collective-permute-start.16 = (bf16[1,192,256]{2,1,0:T(8,128)(2,1)S(1)}, bf16[1,192,256]{2,1,0:T(8,128)(2,1)S(1)}, u32[]{:S(2)}, u32[]{:S(2)}) collective-permute-start(bf16[1,192,256]{2,1,0:T(8,128)(2,1)S(1)} %get-tuple-element.150), channel_id=1, source_target_pairs={{0,2},{1,3},{2,0},{3,1},{4,6},{5,7},{6,4},{7,5},{8,10},{9,11},{10,... | collective-permute-start | bytes 294920 | tf_op jit(solution)/shard_map/ppermute | solution.py:472
  69.7 12.4 %copy-start.8 = (s32[1,512]{1,0:T(1,128)S(1)}, s32[1,512]{1,0:T(1,128)}, u32[]{:S(2)}) copy-start(s32[1,512]{1,0:T(1,128)} %get-tuple-element.83.refs_0_) | copy-start | bytes 6148
  76.4 1.5 %collective-permute-start.17 = (bf16[2,192,256]{2,1,0:T(8,128)(2,1)S(1)}, bf16[2,192,256]{2,1,0:T(8,128)(2,1)S(1)}, u32[]{:S(2)}, u32[]{:S(2)}) collective-permute-start(bf16[2,192,256]{2,1,0:T(8,128)(2,1)S(1)} %constant_dynamic-update-slice_fusion.refs_0_), channel_id=1, source_target_pairs={{0,1},{1,0},{2,3},{3,2},{4,5},{5,4},{6,7},{7,6},{8,9},{9,8},{10,11... | collective-permute-start | bytes 589832 | tf_op jit(solution)/shard_map/ppermute | solution.py:472
  (5 other events, 20.1 us)
